TPU v7x, 32 devices: a whole 2x2x4 slice. The times are simulated.
32 devices in a mesh: row: 4 (over y, x), col: 8 (over z, core).
Axes of the slice: x: 2, y: 2, z: 4, core: 2. Of those that a mesh axis runs over, the one named last changes fastest.
Arguments:
- features: float32 [2, 64, 512, 128], P(None, 'row', 'col'), may hold values from -6 to 6
- cotangent: float32 [2, 64, 512, 128], P(None, 'row', 'col'), may hold values from -6 to 6
- conv_kernel: float32 [7, 7, 128], P(None, None, ('row', 'col')), may hold values from -0.875 to 0.875
- conv_bias: float32 [128], P(('row', 'col')), may hold values from -3 to 3
- norm_gain: float32 [128], P(('row', 'col')), may hold values from 0.1 to 1.9
- norm_shift: float32 [128], P(('row', 'col')), may hold values from -2 to 2
- w_in: float32 [128, 512], P(None, ('row', 'col')), may hold values from -0.5 to 0.5
- in_bias: float32 [512], P(('row', 'col')), may hold values from -3 to 3
- w_out: float32 [512, 128], P(('row', 'col')), may hold values from -0.25 to 0.25
- out_bias: float32 [128], P(('row', 'col')), may hold values from -3 to 3
- layer_scale: float32 [128], P(('row', 'col')), may hold values from 0.5 to 1.5
Outputs:
- features_grad: float32 [2, 64, 512, 128], P(None, 'row', 'col')
- kernel_grad: float32 [7, 7, 128], P(None, None, ('row', 'col'))
- conv_bias_grad: float32 [128], P(('row', 'col'))
- gain_grad: float32 [128], P(('row', 'col'))
- shift_grad: float32 [128], P(('row', 'col'))
- w_in_grad: float32 [128, 512], P(None, ('row', 'col'))
- in_bias_grad: float32 [512], P(('row', 'col'))
- w_out_grad: float32 [512, 128], P(('row', 'col'))
- out_bias_grad: float32 [128], P(('row', 'col'))
- scale_grad: float32 [128], P(('row', 'col'))
All inputs are finite; a program needn't handle non-finite values.
Results may differ from a plain program's by a relative error of at most 0.0003.
Values sent between devices are 32-bit elements; how exact they have to be, the bound alone decides.
No kernel may reach another device: no remote copies, remote signals or barrier semaphores. Data moves between devices by JAX's collectives and lax.ppermute only.
A program may use at most 64 MiB of HBM per device.

v0:
```python
import math

import jax
import jax.numpy as jnp
from jax import lax
from jax.sharding import PartitionSpec as P

norm_eps = 1e-06
inverse_root_two = 0.7071067811865476
inverse_root_twopi = 0.3989422804014327


def extended(block, sides, width):
    for axis, dim in sides:
        count = lax.axis_size(axis)
        forward = [(i, i + 1) for i in range(count - 1)]
        backward = [(target, source) for source, target in forward]
        low = lax.ppermute(
            lax.slice_in_dim(block, block.shape[dim] - width, None, axis=dim), axis, forward
        )
        high = lax.ppermute(lax.slice_in_dim(block, 0, width, axis=dim), axis, backward)
        block = jnp.concatenate([low, block, high], axis=dim)
    return block


def depthwise(field, kernel):
    return lax.conv_general_dilated(
        field,
        kernel[:, :, None, :],
        (1, 1),
        "VALID",
        dimension_numbers=("NHWC", "HWIO", "NHWC"),
        feature_group_count=field.shape[-1],
        precision=lax.Precision.HIGHEST,
    )


def cell_total(block):
    return jnp.sum(block, axis=(0, 1, 2))


def mixing_back(
    conv_out,
    cot_field,
    gain_all,
    shift_all,
    input_all,
    inbias_all,
    output_all,
    outbias_all,
    scale_all,
):
    highest = lax.Precision.HIGHEST
    mean = jnp.mean(conv_out, -1, keepdims=True)
    centred = conv_out - mean
    variance = jnp.mean(centred * centred, -1, keepdims=True)
    inverse = lax.rsqrt(variance + norm_eps)
    normed = centred * inverse
    lin = normed * gain_all + shift_all
    act = jnp.einsum("bhwc,ck->bhwk", lin, input_all, precision=highest) + inbias_all
    hidden = 0.5 * act * (1.0 + lax.erf(act * inverse_root_two))
    branch = jnp.einsum("bhwk,kc->bhwc", hidden, output_all, precision=highest) + outbias_all
    d_branch = cot_field * scale_all
    d_hidden = jnp.einsum("bhwc,kc->bhwk", d_branch, output_all, precision=highest)
    slope = (
        0.5 * (1.0 + lax.erf(act * inverse_root_two))
        + act * jnp.exp(-0.5 * act * act) * inverse_root_twopi
    )
    d_act = d_hidden * slope
    d_lin = jnp.einsum("bhwk,ck->bhwc", d_act, input_all, precision=highest)
    d_norm = d_lin * gain_all
    d_conv = inverse * (
        d_norm
        - jnp.mean(d_norm, -1, keepdims=True)
        - normed * jnp.mean(d_norm * normed, -1, keepdims=True)
    )
    gain_grad = cell_total(d_lin * normed)
    shift_grad = cell_total(d_lin)
    win_grad = jnp.einsum("bhwc,bhwk->ck", lin, d_act, precision=highest)
    inb_grad = cell_total(d_act)
    wout_grad = jnp.einsum("bhwk,bhwc->kc", hidden, d_branch, precision=highest)
    outb_grad = cell_total(d_branch)
    scale_grad = cell_total(cot_field * branch)
    return (d_conv, (gain_grad, shift_grad, win_grad, inb_grad, wout_grad, outb_grad, scale_grad))


def per_device(
    features,
    cotangent,
    conv_kernel,
    conv_bias,
    norm_gain,
    norm_shift,
    w_in,
    in_bias,
    w_out,
    out_bias,
    layer_scale,
):
    gathered = (
        lax.all_gather(conv_kernel, ("row", "col"), axis=2, tiled=True),
        lax.all_gather(conv_bias, ("row", "col"), axis=0, tiled=True),
        lax.all_gather(norm_gain, ("row", "col"), axis=0, tiled=True),
        lax.all_gather(norm_shift, ("row", "col"), axis=0, tiled=True),
        lax.all_gather(w_in, ("row", "col"), axis=1, tiled=True),
        lax.all_gather(in_bias, ("row", "col"), axis=0, tiled=True),
        lax.all_gather(w_out, ("row", "col"), axis=0, tiled=True),
        lax.all_gather(out_bias, ("row", "col"), axis=0, tiled=True),
        lax.all_gather(layer_scale, ("row", "col"), axis=0, tiled=True),
    )
    (
        kernel_all,
        conv_all,
        gain_all,
        shift_all,
        input_all,
        inbias_all,
        output_all,
        outbias_all,
        scale_all,
    ) = gathered
    margin = kernel_all.shape[0] // 2
    source = extended(features, (("row", 1), ("col", 2)), margin)
    conv_out = depthwise(source, kernel_all) + conv_all
    dconv_inner, partials = mixing_back(
        conv_out,
        cotangent,
        gain_all,
        shift_all,
        input_all,
        inbias_all,
        output_all,
        outbias_all,
        scale_all,
    )
    dconv_wide = extended(dconv_inner, (("row", 1), ("col", 2)), margin)
    features_grad = cotangent + depthwise(dconv_wide, kernel_all[::-1, ::-1])
    kernel_part = jax.vjp(lambda weights: depthwise(source, weights), kernel_all)[1](dconv_inner)[0]
    bias_part = jnp.sum(dconv_inner, axis=(0, 1, 2))
    cells = (
        features.shape[0]
        * features.shape[1]
        * features.shape[2]
        * lax.axis_size("row")
        * lax.axis_size("col")
    )
    factor = 1.0 / math.sqrt(cells)
    gain_p, shift_p, win_p, inb_p, wout_p, outb_p, scale_p = partials
    reduced = (
        lax.psum_scatter(kernel_part * factor, ("row", "col"), scatter_dimension=2, tiled=True),
        lax.psum_scatter(bias_part * factor, ("row", "col"), scatter_dimension=0, tiled=True),
        lax.psum_scatter(gain_p * factor, ("row", "col"), scatter_dimension=0, tiled=True),
        lax.psum_scatter(shift_p * factor, ("row", "col"), scatter_dimension=0, tiled=True),
        lax.psum_scatter(win_p * factor, ("row", "col"), scatter_dimension=1, tiled=True),
        lax.psum_scatter(inb_p * factor, ("row", "col"), scatter_dimension=0, tiled=True),
        lax.psum_scatter(wout_p * factor, ("row", "col"), scatter_dimension=0, tiled=True),
        lax.psum_scatter(outb_p * factor, ("row", "col"), scatter_dimension=0, tiled=True),
        lax.psum_scatter(scale_p * factor, ("row", "col"), scatter_dimension=0, tiled=True),
    )
    (
        kernel_grad,
        bias_grad,
        gain_grad,
        shift_grad,
        win_grad,
        inb_grad,
        wout_grad,
        outb_grad,
        scale_grad,
    ) = reduced
    return (
        features_grad,
        kernel_grad,
        bias_grad,
        gain_grad,
        shift_grad,
        win_grad,
        inb_grad,
        wout_grad,
        outb_grad,
        scale_grad,
    )


def solution(mesh):
    in_specs = (
        P(None, "row", "col", None),
        P(None, "row", "col", None),
        P(None, None, ("row", "col")),
        P(("row", "col")),
        P(("row", "col")),
        P(("row", "col")),
        P(None, ("row", "col")),
        P(("row", "col")),
        P(("row", "col"), None),
        P(("row", "col")),
        P(("row", "col")),
    )
    out_specs = (
        P(None, "row", "col", None),
        P(None, None, ("row", "col")),
        P(("row", "col")),
        P(("row", "col")),
        P(("row", "col")),
        P(None, ("row", "col")),
        P(("row", "col")),
        P(("row", "col"), None),
        P(("row", "col")),
        P(("row", "col")),
    )
    return jax.shard_map(
        per_device, mesh=mesh, in_specs=in_specs, out_specs=out_specs, check_vma=False
    )
```

profile of v0, /device:TPU:0, one launch (start us, length us, event | category | flops | bytes accessed | tf_op | source)
XLA Modules:
  0.0 668.5 jit_solution(6840931754884915989)
XLA Ops:
  9.3 5.5 collective-permute-start
  17.6 44.2 %all_gather.33 = f32[128,512]{0,1:T(8,128)S(1)} all-gather(f32[128,16]{0,1:T(8,128)} %param.17), channel_id=1, replica_groups=mesh['row'=4,'col'=8] {'row','col'}, dimensions={1}, use_global_device_ids=true | all-gather | bytes 270336 | tf_op jit(solution)/shard_map/all_gather | solution.py:105
  61.8 38.9 %all_gather.27 = f32[7,7,128]{1,0,2:T(8,128)S(1)} all-gather(f32[7,7,4]{1,0,2:T(8,128)S(1)} %copy.73), channel_id=1, replica_groups=mesh['row'=4,'col'=8] {'row','col'}, dimensions={2}, use_global_device_ids=true | all-gather | bytes 25872 | tf_op jit(solution)/shard_map/all_gather | solution.py:101
  102.9 39.3 %all-reduce.13 = (f32[128]{0:T(128)S(1)}, f32[128]{0:T(128)S(1)}, f32[128]{0:T(128)S(1)}, f32[512]{0:T(512)S(1)}, f32[128]{0:T(128)S(1)}, /*index=5*/f32[128]{0:T(128)S(1)}) all-reduce(f32[128]{0:T(128)S(1)} %dynamic-update-slice.3, f32[128]{0:T(128)S(1)} %dynamic-update-slice.2, ...), channel_id=1, replica_groups=mesh['row'=4,'col'=8] {'row','col'}, use_global_device_ids=true, to_apply=%add.3 | all-reduce | flops 1152 | bytes 9216
  148.0 44.2 %all_gather.30 = f32[512,128]{1,0:T(8,128)S(1)} all-gather(f32[16,128]{1,0:T(8,128)S(1)} %copy-done.7), channel_id=1, replica_groups=mesh['row'=4,'col'=8] {'row','col'}, dimensions={0}, use_global_device_ids=true | all-gather | bytes 270336 | tf_op jit(solution)/shard_map/all_gather | solution.py:107
  194.2 5.9 fusion.61
  201.7 3.6 fusion.34
  205.3 1.9 copy-done.2
  207.2 8.0 %fusion.30 = f32[512,128]{1,0:T(8,128)} fusion(f32[2,16,64,512]{3,2,1,0:T(8,128)S(1)} %fusion.34, f32[512]{0:T(512)S(1)} %get-tuple-element.63, f32[2,16,64,128]{3,2,1,0:T(8,128)S(1)} %copy-done.1, f32[128]{0:T(128)S(1)} %get-tuple-element.64), kind=kOutput, calls=%fused_computation.33 | convolution fusion | flops 1616183296 | bytes 5507584 | tf_op jit(solution)/shard_map/bhwk,bhwc->kc/dot_general | solution.py:81
  215.3 6.8 %fusion.62 = (f32[512]{0:T(512)S(1)}, f32[2,16,64,512]{3,2,1,0:T(8,128)S(1)}) fusion(f32[2,16,64,512]{3,2,1,0:T(8,128)} %copy-done.2, f32[512]{0:T(512)S(1)} %get-tuple-element.63, f32[512,128]{1,0:T(8,128)S(1)} %all_gather.30, f32[2,16,64,128]{3,2,1,0:T(8,128)S(1)} %copy-done.1, f32[128]{0:T(128)S(1)} %get-tuple-element.64), kind=kOutput, calls=%fused_computation.90 | convolution fusion | flops 1622408704 | bytes 9703936 | tf_op jit(solution)/shard_map/bhwc,kc->bhwk/dot_general | solution.py:64
  222.1 2.0 copy-done
  224.1 8.0 %fusion.28 = f32[128,512]{0,1:T(8,128)} fusion(f32[2,16,64,512]{3,2,1,0:T(8,128)S(1)} %get-tuple-element.80, f32[128]{0:T(128)S(1)} %get-tuple-element.60, f32[128]{0:T(128)S(1)} %get-tuple-element.61, f32[16,2,64,128]{3,0,2,1:T(8,128)S(1)} %slice.42, f32[2,16,64]{2,1,0:T(8,128)S(1)} %add_rsqrt_fusion, f32[2,16,64]{2,1,0:T(8,128)S(1)} %copy.79), kind=kOutput, calls=%fused_computation.31 | convolution fusion | flops 1611726848 | bytes 5522432 | tf_op jit(solution)/shard_map/bhwc,bhwk->ck/dot_general | solution.py:79
  232.1 5.7 multiply_reduce_fusion
  237.8 4.1 fusion.27
  241.9 1.7 fusion.57
  243.7 20.2 %convolution_multiply_fusion = f32[7,7,1,128]{3,2,1,0:T(1,128)S(1)} fusion(f32[2,16,64,128]{3,2,1,0:T(8,128)S(1)} %get-tuple-element.67, f32[2,22,3,128]{3,0,2,1:T(2,128)S(1)} %collective-permute-done.3, f32[2,22,64,128]{3,0,2,1:T(2,128)S(1)} %copy-done.5, f32[2,22,3,128]{3,0,2,1:T(2,128)S(1)} %collective-permute-done.2), kind=kOutput, calls=%fused_computation.34 | convolution fusion | flops 154935424 | bytes 2650624 | tf_op jit(solution)/shard_map/transpose(jvp())/conv_general_dilated | solution.py:27
  267.7 3.6 collective-permute-done.4
  271.2 7.9 %collective-permute-done.5 = f32[2,3,64,128]{3,2,1,0:T(8,128)S(1)} collective-permute-done((f32[2,3,64,128]{3,2,1,0:T(8,128)S(1)}, f32[2,3,64,128]{3,2,1,0:T(8,128)S(1)}, u32[]{:S(2)}, u32[]{:S(2)}) %collective-permute-start.5) | collective-permute-done | bytes 196640 | tf_op jit(solution)/shard_map/ppermute | solution.py:21
  279.2 1.5 collective-permute-start.6
  282.0 40.4 %all-reduce.12 = (f32[128]{0:T(128)S(1)}, f32[128]{0:T(128)S(1)}, f32[128]{0:T(128)S(1)}, f32[512]{0:T(512)S(1)}, f32[128]{0:T(128)S(1)}, /*index=5*/f32[128]{0:T(128)S(1)}) all-reduce(f32[128]{0:T(128)S(1)} %broadcast_multiply_fusion.7, f32[128]{0:T(128)S(1)} %get-tuple-element.84, ...), channel_id=3, replica_groups=mesh['row'=4,'col'=8] {'row','col'}, use_global_device_ids=true, to_apply=%region_6.0.clone | all-reduce | flops 1152 | bytes 9216
  325.9 70.6 %reduce-scatter.4.cloned.1.call-done = f32[7,7,4]{1,0,2:T(8,128)} async-done(((f32[7,7,128]{1,0,2:T(8,128)}), f32[7,7,4]{1,0,2:T(8,128)}) %reduce-scatter.4.cloned.1.call-update) | async-done | bytes 800 | tf_op jit(solution)/shard_map/reduce_scatter | solution.py:150
  400.8 5.2 fusion.18
  408.3 120.9 %reduce-scatter.8.cloned.1.call-done = f32[16,128]{1,0:T(8,128)} async-done(((f32[512,128]{1,0:T(8,128)}), f32[16,128]{1,0:T(8,128)}) %reduce-scatter.8.cloned.1.call-update) | async-done | bytes 8208 | tf_op jit(solution)/shard_map/reduce_scatter | solution.py:156
  529.2 132.6 %reduce-scatter.6.cloned.1.call-done = f32[128,16]{0,1:T(8,128)} async-done(((f32[128,512]{0,1:T(8,128)}), f32[128,16]{0,1:T(8,128)}) %reduce-scatter.6.cloned.1.call-update) | async-done | bytes 8208 | tf_op jit(solution)/shard_map/reduce_scatter | solution.py:154
  (107 shorter events, 31.4 us)
Async XLA Ops:
  7.2 94.4 %copy-start.8 = (f32[4]{0:T(128)S(1)}, f32[4]{0:T(128)}, u32[]{:S(2)}) copy-start(f32[4]{0:T(128)} %param.21) | copy-start | bytes 52
  7.2 94.6 %copy-start.9 = (f32[4]{0:T(128)S(1)}, f32[4]{0:T(128)}, u32[]{:S(2)}) copy-start(f32[4]{0:T(128)} %param.14) | copy-start | bytes 52
  7.2 94.8 %copy-start.10 = (f32[4]{0:T(128)S(1)}, f32[4]{0:T(128)}, u32[]{:S(2)}) copy-start(f32[4]{0:T(128)} %param.15) | copy-start | bytes 52
  7.2 95.0 %copy-start.11 = (f32[4]{0:T(128)S(1)}, f32[4]{0:T(128)}, u32[]{:S(2)}) copy-start(f32[4]{0:T(128)} %param.16) | copy-start | bytes 52
  7.2 95.3 %copy-start.12 = (f32[4]{0:T(128)S(1)}, f32[4]{0:T(128)}, u32[]{:S(2)}) copy-start(f32[4]{0:T(128)} %param.20) | copy-start | bytes 52
  7.2 95.5 %copy-start.13 = (f32[16]{0:T(128)S(1)}, f32[16]{0:T(128)}, u32[]{:S(2)}) copy-start(f32[16]{0:T(128)} %param.18) | copy-start | bytes 196
  7.2 135.0 %copy-start.1 = (f32[2,16,64,128]{3,2,1,0:T(8,128)S(1)}, f32[2,16,64,128]{3,2,1,0:T(8,128)}, u32[]{:S(2)}) copy-start(f32[2,16,64,128]{3,2,1,0:T(8,128)} %param.12) | copy-start | bytes 3145732
  7.2 389.2 %reduce-scatter.4.cloned.1.call-start = ((), (), s32[]{:S(2)}) async-start(), calls=%async_computation.3 | async-start | bytes 540672 | tf_op jit(solution)/shard_map/reduce_scatter | solution.py:150
  8.4 135.1 %copy-start.6 = (f32[2,16,64,128]{3,2,1,0:T(8,128)S(1)}, f32[2,16,64,128]{3,2,1,0:T(8,128)}, u32[]{:S(2)}) copy-start(f32[2,16,64,128]{3,2,1,0:T(8,128)} %param.11) | copy-start | bytes 3145732
  9.3 133.3 %collective-permute-start = (f32[2,3,64,128]{3,0,2,1:T(2,128)}, f32[2,3,64,128]{3,0,2,1:T(2,128)}, u32[]{:S(2)}, u32[]{:S(2)}) collective-permute-start(f32[2,3,64,128]{3,0,2,1:T(2,128)} %copy.127), channel_id=1, source_target_pairs={{0,8},{8,16},{16,24},{1,9},{9,17},{17,25},{2,10},{10,18},{18,26},{... | collective-permute-start | bytes 589832 | tf_op jit(solution)/shard_map/ppermute | solution.py:18
  15.6 128.8 %collective-permute-start.1 = (f32[2,3,64,128]{3,0,2,1:T(2,128)}, f32[2,3,64,128]{3,0,2,1:T(2,128)}, u32[]{:S(2)}, u32[]{:S(2)}) collective-permute-start(f32[2,3,64,128]{3,0,2,1:T(2,128)} %copy.128), channel_id=1, source_target_pairs={{8,0},{16,8},{24,16},{9,1},{17,9},{25,17},{10,2},{18,10},{26,18},{... | collective-permute-start | bytes 589832 | tf_op jit(solution)/shard_map/ppermute | solution.py:21
  101.1 46.9 %copy-start.7 = (f32[16,128]{1,0:T(8,128)S(1)}, f32[16,128]{1,0:T(8,128)}, u32[]{:S(2)}) copy-start(f32[16,128]{1,0:T(8,128)} %param.19) | copy-start | bytes 24580
  145.4 48.2 %copy-start.4 = (f32[2,22,64,128]{3,0,2,1:T(2,128)}, f32[2,22,64,128]{3,0,2,1:T(2,128)S(1)}, u32[]{:S(2)}) copy-start(f32[2,22,64,128]{3,0,2,1:T(2,128)S(1)} %constant_dynamic-update-slice_fusion) | copy-start | bytes 4325380
  145.4 46.8 %collective-permute-start.2 = (f32[2,22,3,128]{3,0,2,1:T(2,128)S(1)}, f32[2,22,3,128]{3,0,2,1:T(2,128)S(1)}, u32[]{:S(2)}, u32[]{:S(2)}) collective-permute-start(f32[2,22,3,128]{3,0,2,1:T(2,128)S(1)} %get-tuple-element.70), channel_id=1, source_target_pairs={{0,1},{1,2},{2,3},{3,4},{4,5},{5,6},{6,7},{8,9},{9,10},{10,11},{11... | collective-permute-start | bytes 202760 | tf_op jit(solution)/shard_map/ppermute | solution.py:18
  146.7 45.5 %collective-permute-start.3 = (f32[2,22,3,128]{3,0,2,1:T(2,128)S(1)}, f32[2,22,3,128]{3,0,2,1:T(2,128)S(1)}, u32[]{:S(2)}, u32[]{:S(2)}) collective-permute-start(f32[2,22,3,128]{3,0,2,1:T(2,128)S(1)} %get-tuple-element.71), channel_id=1, source_target_pairs={{1,0},{2,1},{3,2},{4,3},{5,4},{6,5},{7,6},{9,8},{10,9},{11,10},{12... | collective-permute-start | bytes 202760 | tf_op jit(solution)/shard_map/ppermute | solution.py:21
  205.3 1.9 copy-start.2
  222.1 2.0 copy-start
  232.1 5.7 copy-start.3
  264.9 264.2 %reduce-scatter.8.cloned.1.call-start = ((), (), s32[]{:S(2)}) async-start(), calls=%async_computation.5 | async-start | bytes 270336 | tf_op jit(solution)/shard_map/reduce_scatter | solution.py:156
  265.0 6.3 collective-permute-start.4
  266.3 12.9 %collective-permute-start.5 = (f32[2,3,64,128]{3,2,1,0:T(8,128)S(1)}, f32[2,3,64,128]{3,2,1,0:T(8,128)S(1)}, u32[]{:S(2)}, u32[]{:S(2)}) collective-permute-start(f32[2,3,64,128]{3,2,1,0:T(8,128)S(1)} %get-tuple-element.73), channel_id=1, source_target_pairs={{8,0},{16,8},{24,16},{9,1},{17,9},{25,17},{10,2},{18,10},{26,18},{... | collective-permute-start | bytes 589832 | tf_op jit(solution)/shard_map/ppermute | solution.py:21
  267.6 394.1 %reduce-scatter.6.cloned.1.call-start = ((), (), s32[]{:S(2)}) async-start(), calls=%async_computation.4 | async-start | bytes 270336 | tf_op jit(solution)/shard_map/reduce_scatter | solution.py:154
  279.2 118.6 %collective-permute-start.6 = (f32[2,22,3,128]{3,2,1,0:T(4,128)S(1)}, f32[2,22,3,128]{3,2,1,0:T(4,128)S(1)}, u32[]{:S(2)}, u32[]{:S(2)}) collective-permute-start(f32[2,22,3,128]{3,2,1,0:T(4,128)S(1)} %get-tuple-element.68), channel_id=1, source_target_pairs={{0,1},{1,2},{2,3},{3,4},{4,5},{5,6},{6,7},{8,9},{9,10},{10,11},{11... | collective-permute-start | bytes 202760 | tf_op jit(solution)/shard_map/ppermute | solution.py:18
  280.7 117.1 %collective-permute-start.7 = (f32[2,22,3,128]{3,2,1,0:T(4,128)S(1)}, f32[2,22,3,128]{3,2,1,0:T(4,128)S(1)}, u32[]{:S(2)}, u32[]{:S(2)}) collective-permute-start(f32[2,22,3,128]{3,2,1,0:T(4,128)S(1)} %get-tuple-element.69), channel_id=1, source_target_pairs={{1,0},{2,1},{3,2},{4,3},{5,4},{6,5},{7,6},{9,8},{10,9},{11,10},{12... | collective-permute-start | bytes 202760 | tf_op jit(solution)/shard_map/ppermute | solution.py:21
  (2 other events, 2.5 us)
Sparse Core Ops, SparseCore 0:
  265.0 131.3 reduce-scatter.3
  399.3 129.7 reduce-scatter.7
  532.0 129.7 reduce-scatter.5
where the time goes:
time: 674 us; the launch traced here: 668 us
  waiting for transfers between devices  336 us (50%)
  blocking collectives  207 us (31%)
  matrix products  67.6 us (10%)
  local copies, waits for them, and re-layouts  23.6 us (4%)
  starting transfers between devices  14.8 us (2%)
  between operations  14.5 us (2%)
    reduce_scatter x1, waiting for transfers between devices, per_device(): lax.psum_scatter(win_p * factor, ('row', 'col'), scatter_dimension=1, til...  133 us
    reduce_scatter x1, waiting for transfers between devices, per_device(): lax.psum_scatter(wout_p * factor, ('row', 'col'), scatter_dimension=0, ti...  121 us
    unnamed x2, blocking collectives  79.7 us
    reduce_scatter x1, waiting for transfers between devices, per_device(): lax.psum_scatter(kernel_part * factor, ('row', 'col'), scatter_dimension=...  70.6 us
    all_gather x1, blocking collectives, per_device(): lax.all_gather(w_out, ('row', 'col'), axis=0, tiled=True)  44.2 us
    all_gather x1, blocking collectives, per_device(): lax.all_gather(w_in, ('row', 'col'), axis=1, tiled=True)  44.2 us
    all_gather x1, blocking collectives, per_device(): lax.all_gather(conv_kernel, ('row', 'col'), axis=2, tiled=True)  38.9 us
    conv_general_dilated x3, matrix products, depthwise(): lax.conv_general_dilated(field, kernel[:, :, None, :], (1, 1), 'VALID', d...  31.3 us
  transfers between devices with their start and end apart: 11, of which 5 were waited for; matrix products, arithmetic and copies ran while one was open for 3% of the time, Pallas kernels for 0%

commit v1 on v0

v1 whole, which is shorter than its diff:
```python
import functools
import math

import jax
import jax.numpy as jnp
from jax import lax
from jax.experimental import pallas as pl
from jax.experimental.pallas import tpu as pltpu
from jax.sharding import PartitionSpec as P

norm_eps = 1e-06
inverse_root_twopi = 0.3989422804014327
half_log2e = 0.7213475204444817
tail_p = 0.275
tail_c = (
    0.1178092510180382,
    0.04211149421929024,
    0.3339322641039753,
    -0.33099338058058636,
    0.45199870802757525,
    -0.11485833206946416,
)
AXES = ("row", "col")
LANES = 128
LEFT = 8
NN = (((1,), (0,)), ((), ()))
NT = (((1,), (1,)), ((), ()))
f32, bf16 = jnp.float32, jnp.bfloat16
VMEM_LIMIT = 48 * 1024 * 1024


def ceil8(n):
    return (n + 7) // 8 * 8


def call(body, outs, scratch=(), flops=0, size=0):
    return pl.pallas_call(
        body,
        out_shape=outs,
        scratch_shapes=list(scratch),
        compiler_params=pltpu.CompilerParams(vmem_limit_bytes=VMEM_LIMIT),
        cost_estimate=pl.CostEstimate(flops=flops, bytes_accessed=size, transcendentals=0),
    )


def shape(*dims):
    return jax.ShapeDtypeStruct(dims, f32)


def device_index(mesh_shape):
    return lax.axis_index("row") * mesh_shape["col"] + lax.axis_index("col")


def split(x):
    high = x.astype(bf16)
    return high, (x - high.astype(f32)).astype(bf16)


def dot(a, b, dims):
    return lax.dot_general(a, b, dims, preferred_element_type=f32)


def exchange_order(x, unit, count, me):
    rows = x.shape[0]
    index = lax.broadcasted_iota(jnp.int32, x.shape, 0)
    step = unit
    bit = 1
    while bit < count:
        up = pltpu.roll(x, step, 0)
        down = pltpu.roll(x, rows - step, 0)
        swapped = jnp.where((index & step) != 0, up, down)
        x = jnp.where((me & bit) != 0, swapped, x)
        step *= 2
        bit *= 2
    return x


def pack_body(ms, kernel_ref, cb, ng, ns, ob, ls, win_ref, ib, wout_ref, out_ref):
    taps_i, cs, taps_j = kernel_ref.shape
    hs = win_ref.shape[0]
    taps = taps_i * taps_j
    out_ref[...] = jnp.zeros_like(out_ref)
    out_ref[0:hs, :] = win_ref[...]
    out_ref[hs : 2 * hs, :] = wout_ref[...]
    base = 2 * hs
    for i in range(taps_i):
        out_ref[base : base + cs, i * taps_j : (i + 1) * taps_j] = kernel_ref[i]
    for n, ref in enumerate((cb, ng, ns, ob, ls)):
        column = jnp.broadcast_to(ref[...], (8, cs)).T
        out_ref[base : base + cs, taps + n : taps + n + 1] = column[:, 0:1]
    out_ref[base + cs : base + cs + 1, 0:hs] = ib[...]


def depthwise_block(read, weight, rows, taps_i, taps_j, start):
    acc = start
    for j in range(taps_j):
        w = [weight(i, j) for i in range(taps_i)]
        for r in range(rows + taps_i - 1):
            s = read(r, j)
            for i in range(taps_i):
                p = r - i
                if 0 <= p < rows:
                    term = w[i] * s
                    acc[p] = term if acc[p] is None else acc[p] + term
    return acc


def fill(dst, inner, top, bottom, left, right):
    batch, rows, cols, _ = inner.shape
    m = top.shape[1]
    for b in range(batch):
        dst[b, m : m + rows, LEFT : LEFT + cols, :] = inner[b]
        dst[b, 0:m, LEFT : LEFT + cols, :] = top[b]
        dst[b, m + rows : m + rows + m, LEFT : LEFT + cols, :] = bottom[b]
        dst[b, :, LEFT - m : LEFT, :] = left[b]
        dst[b, :, LEFT + cols : LEFT + cols + m, :] = right[b]


def small_columns(slots_ref, hs, cs, count, me, order, scratch):
    base = 2 * hs
    for s in range(count):
        scratch[order[s] * cs : (order[s] + 1) * cs, :] = slots_ref[s, base : base + cs, :]
    return exchange_order(scratch[...], cs, count, me)


def mix_body(
    ms, order, factor, taps_i, taps_j, tile,
    feat, top, bottom, left, right, slots_ref, cot_ref,
    src_ref, dconv_ref, edge_top, edge_bottom, grads_ref, chan_ref, small_ref,
    conv_scr, cols_scr, kb_scr, win_scr, wout_scr, w1_scr, w2_scr, w4_scr, bias_scr,
    gw1_scr, gw2_scr, gb_scr, gg_scr, gs_scr, gc_scr, cot_sum,
):
    batch, rows, cols, C = feat.shape
    count = slots_ref.shape[0]
    cs = C // count
    taps = taps_i * taps_j
    m = taps_i // 2
    hid = win_scr.shape[0]
    hs = hid // count
    me = device_index(ms)

    fill(src_ref, feat, top, bottom, left, right)
    columns = small_columns(slots_ref, hs, cs, count, me, order, cols_scr)
    cols_scr[...] = columns
    rows_form = columns.T
    small_ref[...] = rows_form
    for t in range(taps):
        kb_scr[t] = jnp.broadcast_to(rows_form[t : t + 1, :], (8, C))
    conv_bias = jnp.broadcast_to(rows_form[taps : taps + 1, :], (8, C))

    for s in range(count):
        win_scr[s * hs : (s + 1) * hs, :] = slots_ref[s, 0:hs, :]
        wout_scr[s * hs : (s + 1) * hs, :] = slots_ref[s, hs : 2 * hs, :]
    for s in range(count):
        cols_bias = jnp.broadcast_to(slots_ref[s, 2 * hs + cs : 2 * hs + cs + 1, :], (LANES, LANES)).T
        bias_scr[s * hs : (s + 1) * hs, :] = cols_bias[0:hs, :]

    scale_row = rows_form[taps + 4 : taps + 5, :]
    wh, wl = split(win_scr[...])
    w1_scr[:, 0:C] = wh
    w1_scr[:, C : 2 * C] = wl
    w1_scr[:, 2 * C : 3 * C] = wh
    oh, ol = split(wout_scr[...] * scale_row)
    w2_scr[:, 0:C] = oh
    w2_scr[:, C : 2 * C] = ol
    w2_scr[:, 2 * C : 3 * C] = oh
    th, tl = split(win_scr[...].T)
    w4_scr[0:C, :] = th
    w4_scr[C : 2 * C, :] = tl

    def conv_step(b, _):
        for q in range(0, cols, 8):
            acc = depthwise_block(
                lambda r, j: src_ref[b, r, LEFT - m + q + j : LEFT - m + q + j + 8, :],
                lambda i, j: kb_scr[i * taps_j + j],
                rows, taps_i, taps_j, [conv_bias] * rows,
            )
            for p in range(rows):
                conv_scr[b, p, q : q + 8, :] = acc[p]
        return 0

    lax.fori_loop(0, batch, conv_step, 0)

    for ref in (gw1_scr, gw2_scr, gb_scr, gg_scr, gs_scr, gc_scr, cot_sum):
        ref[...] = jnp.zeros_like(ref)
    tile_rows = tile // cols
    per_image = rows // tile_rows
    gain = cols_scr[:, taps + 1 : taps + 2]
    shift = cols_scr[:, taps + 2 : taps + 3]

    def lanes_sum(x):
        total = x[:, 0:LANES]
        for k in range(LANES, x.shape[1], LANES):
            total = total + x[:, k : k + LANES]
        return total

    def step(t, _):
        b = t // per_image
        p0 = (t % per_image) * tile_rows
        x = conv_scr[b, pl.ds(p0, tile_rows)].reshape(tile, C).T
        mean = jnp.mean(x, axis=0, keepdims=True)
        centred = x - mean
        variance = jnp.mean(centred * centred, axis=0, keepdims=True)
        inverse = lax.rsqrt(variance + norm_eps)
        normed = centred * inverse
        lin = normed * gain + shift
        lh, ll = split(lin)
        cot = cot_ref[b, pl.ds(p0, tile_rows)].reshape(tile, C)
        ch, cl = split(cot)
        act = dot(w1_scr[...], jnp.concatenate([lh, lh, ll], axis=0), NN)
        d_hid = dot(w2_scr[...], jnp.concatenate([ch, ch, cl], axis=1), NT)
        bias = bias_scr[...]
        act = act + jnp.concatenate([bias] * (tile // LANES), axis=1)
        e = jnp.exp2((act * act) * (-half_log2e))
        d = 1.0 + tail_p * jnp.abs(act)
        r = pltpu.reciprocal(d, approx=True)
        r = r * (2.0 - d * r)
        q = tail_c[5] * r + tail_c[4]
        for k in (3, 2, 1, 0):
            q = q * r + tail_c[k]
        q = q * r * e
        phi = jnp.where(act > 0, 1.0 - q, q)
        hidden = act * phi
        d_act = d_hid * (phi + act * e * inverse_root_twopi)
        hh, hl = split(hidden)
        dh, dl = split(d_act)
        gb_scr[...] += lanes_sum(d_act)
        both = dot(w4_scr[...], dh, NN)
        d_lin = both[0:C] + both[C : 2 * C] + dot(w4_scr[0:C, :], dl, NN)
        gw1_scr[...] += dot(dh, jnp.concatenate([lh, ll], axis=0), NT)
        gw1_scr[:, 0:C] += dot(dl, lh, NT)
        gw2_scr[...] += dot(hh, jnp.concatenate([ch, cl], axis=1), NN)
        gw2_scr[:, 0:C] += dot(hl, ch, NN)
        gg_scr[...] += lanes_sum(d_lin * normed)
        gs_scr[...] += lanes_sum(d_lin)
        d_norm = d_lin * gain
        d_conv = inverse * (
            d_norm
            - jnp.mean(d_norm, axis=0, keepdims=True)
            - normed * jnp.mean(d_norm * normed, axis=0, keepdims=True)
        )
        gc_scr[...] += lanes_sum(d_conv)
        dconv_ref[b, pl.ds(p0, tile_rows)] = d_conv.T.reshape(tile_rows, cols, C)
        cot_sum[...] += jnp.sum(cot.reshape(tile // 8, 8, C), axis=0)
        return 0

    lax.fori_loop(0, batch * per_image, step, 0)

    edge_top[...] = dconv_ref[:, 0:m]
    edge_bottom[...] = dconv_ref[:, rows - m : rows]

    h = gw2_scr[:, 0:C] + gw2_scr[:, C : 2 * C]
    gw1 = (gw1_scr[:, 0:C] + gw1_scr[:, C : 2 * C]) * factor
    gw2 = h * (scale_row * factor)
    gb = (jnp.sum(gb_scr[...].T, axis=0, keepdims=True)) * factor
    for s in range(count):
        grads_ref[s, 0:hs, :] = gw1[s * hs : (s + 1) * hs, :]
        grads_ref[s, hs : 2 * hs, :] = gw2[s * hs : (s + 1) * hs, :]
    total = jnp.sum(cot_sum[...], axis=0, keepdims=True)
    outb = rows_form[taps + 3 : taps + 4, :]
    scale_grad = jnp.sum(h * wout_scr[...], axis=0, keepdims=True) + outb * total
    chan_ref[...] = jnp.zeros_like(chan_ref)
    chan_ref[0:1, 0:C] = jnp.sum(gc_scr[...].T, axis=0, keepdims=True) * factor
    chan_ref[1:2, 0:C] = jnp.sum(gg_scr[...].T, axis=0, keepdims=True) * factor
    chan_ref[2:3, 0:C] = jnp.sum(gs_scr[...].T, axis=0, keepdims=True) * factor
    chan_ref[3:4, 0:C] = total * scale_row * factor
    chan_ref[4:5, 0:C] = scale_grad * factor
    chan_ref[5:6, :] = gb


def kernel_grad_body(ms, order, factor, taps_i, taps_j, count, src_ref, dconv_ref, chan_ref, out_ref, acc_scr, rows_scr):
    batch, rows, cols, C = dconv_ref.shape
    m = taps_i // 2
    taps = taps_i * taps_j
    cs = C // count
    me = device_index(ms)
    acc_scr[...] = jnp.zeros_like(acc_scr)

    def step(b, _):
        for j in range(taps_j):
            acc = [acc_scr[i * taps_j + j] for i in range(taps_i)]
            for q in range(0, cols, 8):
                d = [dconv_ref[b, p, q : q + 8, :] for p in range(rows)]
                for r in range(rows + taps_i - 1):
                    s = src_ref[b, r, LEFT - m + q + j : LEFT - m + q + j + 8, :]
                    for i in range(taps_i):
                        p = r - i
                        if 0 <= p < rows:
                            acc[i] = acc[i] + d[p] * s
            for i in range(taps_i):
                acc_scr[i * taps_j + j] = acc[i]
        return 0

    lax.fori_loop(0, batch, step, 0)
    rows_scr[...] = jnp.zeros_like(rows_scr)
    for t in range(taps):
        rows_scr[t : t + 1, :] = jnp.sum(acc_scr[t], axis=0, keepdims=True) * factor
    rows_scr[taps : taps + 5, :] = chan_ref[0:5, 0:C]
    columns = exchange_order(rows_scr[...].T, cs, count, me)
    out_ref[...] = jnp.zeros_like(out_ref)
    hs = chan_ref.shape[1] // count
    for s in range(count):
        out_ref[s, 0:cs, :] = columns[order[s] * cs : (order[s] + 1) * cs, :]
        out_ref[s, cs : cs + 1, 0:hs] = chan_ref[5:6, s * hs : (s + 1) * hs]


def features_grad_body(taps_i, taps_j, inner, top, bottom, left, right, small_ref, cot_ref, out_ref, ext_scr, kb_scr):
    batch, rows, cols, C = inner.shape
    m = taps_i // 2
    taps = taps_i * taps_j
    fill(ext_scr, inner, top, bottom, left, right)
    for t in range(taps):
        kb_scr[t] = jnp.broadcast_to(small_ref[t : t + 1, :], (8, C))

    def step(b, _):
        for q in range(0, cols, 8):
            acc = depthwise_block(
                lambda r, j: ext_scr[b, r, LEFT - m + q + j : LEFT - m + q + j + 8, :],
                lambda i, j: kb_scr[taps - 1 - (i * taps_j + j)],
                rows, taps_i, taps_j, [cot_ref[b, p, q : q + 8, :] for p in range(rows)],
            )
            for p in range(rows):
                out_ref[b, p, q : q + 8, :] = acc[p]
        return 0

    lax.fori_loop(0, batch, step, 0)


def finish_body(taps_i, taps_j, cs, hs, *refs):
    parts, outs = refs[:-9], refs[-9:]
    total = parts[0][...]
    for part in parts[1:]:
        total = total + part[...]
    kernel_out, cb, ng, ns, win_out, ib, wout_out, ob, ls = outs
    taps = taps_i * taps_j
    win_out[...] = total[0:hs, :]
    wout_out[...] = total[hs : 2 * hs, :]
    small = total[2 * hs : 2 * hs + 8, :]
    for i in range(taps_i):
        kernel_out[i] = small[0:cs, i * taps_j : (i + 1) * taps_j]
    flipped = small.T
    for n, ref in enumerate((cb, ng, ns, ob, ls)):
        ref[...] = flipped[taps + n : taps + n + 1, 0:cs]
    ib[...] = small[cs : cs + 1, 0:hs]


def shifted(x, axis, step):
    count = lax.axis_size(axis)
    pairs = [(i, i + step) for i in range(count) if 0 <= i + step < count]
    return lax.ppermute(x, axis, pairs)


def flip(x, mask, count):
    return lax.ppermute(x, AXES, [(i, i ^ mask) for i in range(count)])


def groups_of(ms):
    bits_col = ms["col"].bit_length() - 1
    bits_row = ms["row"].bit_length() - 1
    col = [1 << k for k in range(bits_col)]
    row = [1 << (k + bits_col) for k in range(bits_row)]
    rest = col[1:]
    out = [rest[k : k + 2] for k in range(0, len(rest), 2)]
    out += [row[k : k + 2] for k in range(0, len(row), 2)]
    return out + [col[:1]]


def masks(group):
    out = [0]
    for bit in group:
        out += [bit ^ x for x in out]
    return out


def per_device(ms, features, cotangent, conv_kernel, conv_bias, norm_gain, norm_shift, w_in, in_bias, w_out, out_bias, layer_scale):
    batch, rows, cols, C = features.shape
    taps_i, taps_j, cs = conv_kernel.shape
    hs = w_out.shape[0]
    count = ms["row"] * ms["col"]
    hid = hs * count
    m = taps_i // 2
    taps = taps_i * taps_j
    cells = batch * rows * cols * count
    factor = 1.0 / math.sqrt(cells)
    slot = 2 * hs + 8
    wide = ceil8(LEFT + cols + m)

    block = call(functools.partial(pack_body, ms), shape(slot, LANES), size=100000)(
        conv_kernel.transpose(0, 2, 1),
        *(v.reshape(1, cs) for v in (conv_bias, norm_gain, norm_shift, out_bias, layer_scale)),
        w_in.T, in_bias.reshape(1, hs), w_out,
    )
    top = shifted(features[:, rows - m :], "row", 1)
    bottom = shifted(features[:, :m], "row", -1)
    slots = block[None]
    groups = groups_of(ms)
    order = [0]
    for group in groups:
        order = [mask ^ x for mask in masks(group) for x in order]
        slots = jnp.concatenate([slots] + [flip(slots, mask, count) for mask in masks(group)[1:]])

    def sides(top, inner, bottom):
        low = jnp.concatenate([x[:, :, cols - m :] for x in (top, inner, bottom)], axis=1)
        high = jnp.concatenate([x[:, :, :m] for x in (top, inner, bottom)], axis=1)
        return shifted(low, "col", 1), shifted(high, "col", -1)

    left, right = sides(top, features, bottom)
    tile = 4 * cols
    vm = pltpu.VMEM
    src, dconv, edge_top, edge_bottom, grads, chan, small = call(
        functools.partial(mix_body, ms, order, factor, taps_i, taps_j, tile),
        (
            shape(batch, rows + 2 * m, wide, C),
            shape(batch, rows, cols, C),
            shape(batch, m, cols, C),
            shape(batch, m, cols, C),
            shape(count, 2 * hs, C),
            shape(8, hid),
            shape(LANES, C),
        ),
        scratch=(
            vm((batch, rows, cols, C), f32),
            vm((C, LANES), f32),
            vm((taps, 8, C), f32),
            vm((hid, C), f32),
            vm((hid, C), f32),
            vm((hid, 3 * C), bf16),
            vm((hid, 3 * C), bf16),
            vm((2 * C, hid), bf16),
            vm((hid, LANES), f32),
            vm((hid, 2 * C), f32),
            vm((hid, 2 * C), f32),
            vm((hid, LANES), f32),
            vm((C, LANES), f32),
            vm((C, LANES), f32),
            vm((C, LANES), f32),
            vm((8, C), f32),
        ),
        flops=12 * 10**9,
        size=8 * 10**6,
    )(features, top, bottom, left, right, slots, cotangent)

    d_top = shifted(edge_bottom, "row", 1)
    d_bottom = shifted(edge_top, "row", -1)
    smalls = call(
        functools.partial(kernel_grad_body, ms, order, factor, taps_i, taps_j, count),
        shape(count, 8, LANES),
        scratch=(vm((taps, 8, C), f32), vm((LANES, C), f32)),
        flops=4 * 10**9,
        size=4 * 10**6,
    )(src, dconv, chan)

    d_left, d_right = sides(d_top, dconv, d_bottom)

    parts = [jnp.concatenate([grads, smalls], axis=1)]
    for group in groups[::-1]:
        whole = parts[0]
        for part in parts[1:]:
            whole = whole + part
        order = masks(group)
        step = whole.shape[0] // len(order)
        parts = [whole[:step]]
        parts += [flip(whole[k * step : (k + 1) * step], mask, count) for k, mask in enumerate(order) if k]

    features_grad = call(
        functools.partial(features_grad_body, taps_i, taps_j),
        shape(batch, rows, cols, C),
        scratch=(vm((batch, rows + 2 * m, wide, C), f32), vm((taps, 8, C), f32)),
        flops=4 * 10**9,
        size=4 * 10**6,
    )(dconv, d_top, d_bottom, d_left, d_right, small, cotangent)

    outs = call(
        functools.partial(finish_body, taps_i, taps_j, cs, hs),
        (
            shape(taps_i, cs, taps_j),
            *(shape(1, cs) for _ in range(3)),
            shape(hs, C),
            shape(1, hs),
            shape(hs, C),
            *(shape(1, cs) for _ in range(2)),
        ),
        size=100000,
    )(*(p.reshape(slot, LANES) for p in parts))
    kernel_grad, cb, ng, ns, win, ib, wout, ob, ls = outs
    return (
        features_grad,
        kernel_grad.transpose(0, 2, 1),
        cb.reshape(cs),
        ng.reshape(cs),
        ns.reshape(cs),
        win.T,
        ib.reshape(hs),
        wout,
        ob.reshape(cs),
        ls.reshape(cs),
    )


def solution(mesh):
    both = P(AXES)
    tiles = P(None, "row", "col", None)
    in_specs = (
        tiles, tiles, P(None, None, AXES), both, both, both, P(None, AXES), both, P(AXES, None), both, both,
    )
    out_specs = (
        tiles, P(None, None, AXES), both, both, both, P(None, AXES), both, P(AXES, None), both, both,
    )
    return jax.shard_map(
        functools.partial(per_device, dict(mesh.shape)),
        mesh=mesh, in_specs=in_specs, out_specs=out_specs, check_vma=False,
    )
```

time: 674 us -> 93.2 us (0.14)
  waiting for transfers between devices: 336 us -> 12.4 us
  blocking collectives: 207 us -> 0 us
  matrix products: 67.6 us -> 0 us
  Pallas kernels: 0 us -> 29.8 us
  starting transfers between devices: 14.8 us -> 39.4 us
  local copies, waits for them, and re-layouts: 23.6 us -> 9.81 us
  between operations: 14.5 us -> 1.02 us
    reduce_scatter x3 -> x0, waiting for transfers between devices: 324 us -> none  [the longest x1 133 us: per_device(): lax.psum_scatter(win_p * factor, ('row', 'col'), scatter_dimension=1, til...]
    all_gather x3 -> x0, blocking collectives: 127 us -> none  [the longest x1 44.2 us: per_device(): lax.all_gather(w_out, ('row', 'col'), axis=0, tiled=True)]
    unnamed x2 -> x0, blocking collectives: 79.7 us -> none
    dot_general x6 -> x0, matrix products: 36.3 us -> none  [the longest x1 8.04 us: mixing_back(): wout_grad = jnp.einsum('bhwk,bhwc->kc', hidden, d_branch, precision=highest)]
    conv_general_dilated x3 -> x0, matrix products: 31.3 us -> none  [depthwise(): lax.conv_general_dilated(field, kernel[:, :, None, :], (1, 1), 'VALID', d...]
    pallas_call x0 -> x5, Pallas kernels: none -> 29.8 us  [the longest x1 18.9 us: per_device(): call(functools.partial(mix_body, ms, order, factor, taps_i, taps_j, tile)...]
    ppermute x8 -> x22, starting transfers between devices: 14.7 us -> 39.4 us  [the longest x14 22 us: flip(): return lax.ppermute(x, AXES, [(i, i ^ mask) for i in range(count)])]
    unnamed x56 -> x30, local copies, waits for them, and re-layouts: 16.8 us -> 7.65 us
  transfers between devices with their start and end apart: 11 -> 22, of which waited for: 5 -> 4; matrix products, arithmetic and copies ran while one was open for 3% -> 3% of each run, Pallas kernels for 0% -> 11%
where the time goes in v1:
time: 93.2 us; the launch traced here: 92.7 us
  starting transfers between devices  39.4 us (42%)
  Pallas kernels  29.8 us (32%)
  waiting for transfers between devices  12.4 us (13%)
  local copies, waits for them, and re-layouts  9.81 us (11%)
  between operations  1.02 us (1%)
    ppermute x14, starting transfers between devices, flip(): return lax.ppermute(x, AXES, [(i, i ^ mask) for i in range(count)])  22 us
    pallas_call x1, Pallas kernels, per_device(): call(functools.partial(mix_body, ms, order, factor, taps_i, taps_j, tile)...  18.9 us
    ppermute x8, starting transfers between devices, shifted(): return lax.ppermute(x, axis, pairs)  17.4 us
    ppermute x14, waiting for transfers between devices, flip(): return lax.ppermute(x, AXES, [(i, i ^ mask) for i in range(count)])  10 us
    unnamed x30, local copies, waits for them, and re-layouts  7.65 us
    pallas_call x1, Pallas kernels, per_device(): call(functools.partial(kernel_grad_body, ms, order, factor, taps_i, taps_...  5.52 us
    pallas_call x1, Pallas kernels, per_device(): call(functools.partial(features_grad_body, taps_i, taps_j), shape(batch,...  4.54 us
    ppermute x8, waiting for transfers between devices, shifted(): return lax.ppermute(x, axis, pairs)  2.38 us
  transfers between devices with their start and end apart: 22, of which 4 were waited for; matrix products, arithmetic and copies ran while one was open for 3% of the time, Pallas kernels for 11%

profile of v1, /device:TPU:0, one launch (start us, length us, event | category | flops | bytes accessed | tf_op | source)
XLA Modules:
  0.0 92.7 jit_solution(4683858718483535128)
XLA Ops:
  6.9 5.1 %collective-permute-start.6 = (f32[1,40,128]{2,1,0:T(8,128)S(1)}, f32[1,40,128]{2,1,0:T(8,128)S(1)}, u32[]{:S(2)}, u32[]{:S(2)}) collective-permute-start(f32[1,40,128]{2,1,0:T(8,128)S(1)} %bitcast.24), channel_id=1, source_target_pairs={{0,6},{1,7},{2,4},{3,5},{4,2},{5,3},{6,0},{7,1},{8,14},{9,15},{10,... | collective-permute-start | bytes 61448 | tf_op jit(solution)/shard_map/ppermute | solution.py:354
  12.7 1.0 %fusion.6 = (f32[2,3,64,128]{3,2,1,0:T(8,128)S(1)}, f32[2,3,64,128]{3,2,1,0:T(8,128)S(1)}) fusion(f32[2,16,64,128]{3,2,1,0:T(8,128)} %feat.1), kind=kLoop, calls=%fused_computation.31 | loop fusion | bytes 786432 | tf_op jit(solution)/shard_map/slice | solution.py:394
  13.7 1.3 %collective-permute-start.1 = (f32[2,3,64,128]{3,2,1,0:T(8,128)S(1)}, f32[2,3,64,128]{3,2,1,0:T(8,128)S(1)}, u32[]{:S(2)}, u32[]{:S(2)}) collective-permute-start(f32[2,3,64,128]{3,2,1,0:T(8,128)S(1)} %get-tuple-element.46), channel_id=1, source_target_pairs={{8,0},{16,8},{24,16},{9,1},{17,9},{25,17},{10,2},{18,10},{26,18},{... | collective-permute-start | bytes 589832 | tf_op jit(solution)/shard_map/ppermute | solution.py:350
  15.0 4.6 %collective-permute-start = (f32[2,3,64,128]{3,2,1,0:T(8,128)S(1)}, f32[2,3,64,128]{3,2,1,0:T(8,128)S(1)}, u32[]{:S(2)}, u32[]{:S(2)}) collective-permute-start(f32[2,3,64,128]{3,2,1,0:T(8,128)S(1)} %get-tuple-element.47), channel_id=1, source_target_pairs={{0,8},{8,16},{16,24},{1,9},{9,17},{17,25},{2,10},{10,18},{18,26},{... | collective-permute-start | bytes 589832 | tf_op jit(solution)/shard_map/ppermute | solution.py:350
  21.2 3.5 %collective-permute-start.8 = (f32[4,40,128]{2,1,0:T(8,128)S(1)}, f32[4,40,128]{2,1,0:T(8,128)S(1)}, u32[]{:S(2)}, u32[]{:S(2)}) collective-permute-start(f32[4,40,128]{2,1,0:T(8,128)S(1)} %pad_maximum_fusion.5), channel_id=1, source_target_pairs={{0,16},{1,17},{2,18},{3,19},{4,20},{5,21},{6,22},{7,23},{8,24},{9,... | collective-permute-start | bytes 245768 | tf_op jit(solution)/shard_map/ppermute | solution.py:354
  24.7 4.7 %collective-permute-done.7 = f32[4,40,128]{2,1,0:T(8,128)S(1)} collective-permute-done((f32[4,40,128]{2,1,0:T(8,128)S(1)}, f32[4,40,128]{2,1,0:T(8,128)S(1)}, u32[]{:S(2)}, u32[]{:S(2)}) %collective-permute-start.7) | collective-permute-done | bytes 81952 | tf_op jit(solution)/shard_map/ppermute | solution.py:354
  29.6 2.4 %collective-permute-start.2 = (f32[2,22,3,128]{3,2,1,0:T(4,128)S(1)}, f32[2,22,3,128]{3,2,1,0:T(4,128)S(1)}, u32[]{:S(2)}, u32[]{:S(2)}) collective-permute-start(f32[2,22,3,128]{3,2,1,0:T(4,128)S(1)} %pad_maximum_fusion.1), channel_id=1, source_target_pairs={{0,1},{1,2},{2,3},{3,4},{4,5},{5,6},{6,7},{8,9},{9,10},{10,11},{11... | collective-permute-start | bytes 202760 | tf_op jit(solution)/shard_map/ppermute | solution.py:350
  32.1 1.3 %collective-permute-start.3 = (f32[2,22,3,128]{3,2,1,0:T(4,128)S(1)}, f32[2,22,3,128]{3,2,1,0:T(4,128)S(1)}, u32[]{:S(2)}, u32[]{:S(2)}) collective-permute-start(f32[2,22,3,128]{3,2,1,0:T(4,128)S(1)} %pad_maximum_fusion.2), channel_id=1, source_target_pairs={{1,0},{2,1},{3,2},{4,3},{5,4},{6,5},{7,6},{9,8},{10,9},{11,10},{12... | collective-permute-start | bytes 202760 | tf_op jit(solution)/shard_map/ppermute | solution.py:350
  33.4 2.4 %collective-permute-done.3.right = f32[2,22,3,128]{3,2,1,0:T(4,128)S(1)} collective-permute-done((f32[2,22,3,128]{3,2,1,0:T(4,128)S(1)}, f32[2,22,3,128]{3,2,1,0:T(4,128)S(1)}, u32[]{:S(2)}, u32[]{:S(2)}) %collective-permute-start.3) | collective-permute-done | bytes 67616 | tf_op jit(solution)/shard_map/ppermute | solution.py:350
  35.8 18.9 %shard_map.187 = (f32[2,22,80,128]{3,2,1,0:T(8,128)}, f32[2,16,64,128]{3,2,1,0:T(8,128)S(1)}, f32[2,3,64,128]{3,2,1,0:T(8,128)S(1)}, f32[2,3,64,128]{3,2,1,0:T(8...) custom-call(f32[2,16,64,128]{3,2,1,0:T(8,128)S(1)} %copy-done, ...), custom_call_target="tpu_custom_call" | custom-call | flops 12000000000 | bytes 8000000 | tf_op jit(solution)/shard_map/pallas_call | solution.py:410
  54.7 3.3 %collective-permute-start.11 = (f32[2,3,64,128]{3,2,1,0:T(8,128)S(1)}, f32[2,3,64,128]{3,2,1,0:T(8,128)S(1)}, u32[]{:S(2)}, u32[]{:S(2)}) collective-permute-start(f32[2,3,64,128]{3,2,1,0:T(8,128)S(1)} %get-tuple-element.27), channel_id=1, source_target_pairs={{0,8},{8,16},{16,24},{1,9},{9,17},{17,25},{2,10},{10,18},{18,26},{... | collective-permute-start | bytes 589832 | tf_op jit(solution)/shard_map/ppermute | solution.py:350
  58.0 1.3 %collective-permute-start.12 = (f32[2,3,64,128]{3,2,1,0:T(8,128)S(1)}, f32[2,3,64,128]{3,2,1,0:T(8,128)S(1)}, u32[]{:S(2)}, u32[]{:S(2)}) collective-permute-start(f32[2,3,64,128]{3,2,1,0:T(8,128)S(1)} %get-tuple-element.28), channel_id=1, source_target_pairs={{8,0},{16,8},{24,16},{9,1},{17,9},{25,17},{10,2},{18,10},{26,18},{... | collective-permute-start | bytes 589832 | tf_op jit(solution)/shard_map/ppermute | solution.py:350
  59.3 1.5 %copy-done.11 = f32[2,22,80,128]{3,2,1,0:T(8,128)S(1)} copy-done((f32[2,22,80,128]{3,2,1,0:T(8,128)S(1)}, f32[2,22,80,128]{3,2,1,0:T(8,128)}, u32[]{:S(2)}) %copy-start.11) | copy-done | bytes 1802264
  60.8 5.5 %shard_map.189 = f32[32,8,128]{2,1,0:T(8,128)S(1)} custom-call(f32[2,22,80,128]{3,2,1,0:T(8,128)S(1)} %copy-done.11, f32[2,16,64,128]{3,2,1,0:T(8,128)S(1)} %get-tuple-element.26.inner.dconv_ref, f32[8,512]{1,0:T(8,128)S(1)} %get-tuple-element.32.chan_ref), custom_call_target="tpu_custom_call" | custom-call | flops 4000000000 | bytes 4000000 | tf_op jit(solution)/shard_map/pallas_call | solution.py:445
  66.4 2.9 %collective-permute-start.15 = (f32[16,40,128]{2,1,0:T(8,128)S(1)}, f32[16,40,128]{2,1,0:T(8,128)S(1)}, u32[]{:S(2)}, u32[]{:S(2)}) collective-permute-start(f32[16,40,128]{2,1,0:T(8,128)S(1)} %pad_maximum_fusion), channel_id=1, source_target_pairs={{0,1},{1,0},{2,3},{3,2},{4,5},{5,4},{6,7},{7,6},{8,9},{9,8},{10,11... | collective-permute-start | bytes 983048 | tf_op jit(solution)/shard_map/ppermute | solution.py:354
  69.4 1.9 %collective-permute-start.13 = (f32[2,22,3,128]{3,2,1,0:T(4,128)S(1)}, f32[2,22,3,128]{3,2,1,0:T(4,128)S(1)}, u32[]{:S(2)}, u32[]{:S(2)}) collective-permute-start(f32[2,22,3,128]{3,2,1,0:T(4,128)S(1)} %pad_maximum_fusion.3), channel_id=1, source_target_pairs={{0,1},{1,2},{2,3},{3,4},{4,5},{5,6},{6,7},{8,9},{9,10},{10,11},{11... | collective-permute-start | bytes 202760 | tf_op jit(solution)/shard_map/ppermute | solution.py:350
  71.5 2.4 %collective-permute-start.16 = (f32[4,40,128]{2,1,0:T(8,128)S(1)}, f32[4,40,128]{2,1,0:T(8,128)S(1)}, u32[]{:S(2)}, u32[]{:S(2)}) collective-permute-start(f32[4,40,128]{2,1,0:T(8,128)S(1)} %get-tuple-element.48), channel_id=1, source_target_pairs={{0,8},{1,9},{2,10},{3,11},{4,12},{5,13},{6,14},{7,15},{8,0},{9,1},... | collective-permute-start | bytes 245768 | tf_op jit(solution)/shard_map/ppermute | solution.py:354
  73.9 2.3 %collective-permute-start.18 = (f32[4,40,128]{2,1,0:T(8,128)S(1)}, f32[4,40,128]{2,1,0:T(8,128)S(1)}, u32[]{:S(2)}, u32[]{:S(2)}) collective-permute-start(f32[4,40,128]{2,1,0:T(8,128)S(1)} %get-tuple-element.49), channel_id=1, source_target_pairs={{0,24},{1,25},{2,26},{3,27},{4,28},{5,29},{6,30},{7,31},{8,16},{9,... | collective-permute-start | bytes 245768 | tf_op jit(solution)/shard_map/ppermute | solution.py:354
  76.2 1.3 %collective-permute-start.14 = (f32[2,22,3,128]{3,2,1,0:T(4,128)S(1)}, f32[2,22,3,128]{3,2,1,0:T(4,128)S(1)}, u32[]{:S(2)}, u32[]{:S(2)}) collective-permute-start(f32[2,22,3,128]{3,2,1,0:T(4,128)S(1)} %pad_maximum_fusion.4), channel_id=1, source_target_pairs={{1,0},{2,1},{3,2},{4,3},{5,4},{6,5},{7,6},{9,8},{10,9},{11,10},{12... | collective-permute-start | bytes 202760 | tf_op jit(solution)/shard_map/ppermute | solution.py:350
  77.6 3.3 %collective-permute-done.18 = f32[4,40,128]{2,1,0:T(8,128)S(1)} collective-permute-done((f32[4,40,128]{2,1,0:T(8,128)S(1)}, f32[4,40,128]{2,1,0:T(8,128)S(1)}, u32[]{:S(2)}, u32[]{:S(2)}) %collective-permute-start.18) | collective-permute-done | bytes 81952 | tf_op jit(solution)/shard_map/ppermute | solution.py:354
  80.8 2.0 %collective-permute-done.17 = f32[4,40,128]{2,1,0:T(8,128)S(1)} collective-permute-done((f32[4,40,128]{2,1,0:T(8,128)S(1)}, f32[4,40,128]{2,1,0:T(8,128)S(1)}, u32[]{:S(2)}, u32[]{:S(2)}) %collective-permute-start.17) | collective-permute-done | bytes 81952 | tf_op jit(solution)/shard_map/ppermute | solution.py:354
  83.7 2.0 %collective-permute-start.20 = (f32[1,40,128]{2,1,0:T(8,128)S(1)}, f32[1,40,128]{2,1,0:T(8,128)S(1)}, u32[]{:S(2)}, u32[]{:S(2)}) collective-permute-start(f32[1,40,128]{2,1,0:T(8,128)S(1)} %get-tuple-element.60), channel_id=1, source_target_pairs={{0,4},{1,5},{2,6},{3,7},{4,0},{5,1},{6,2},{7,3},{8,12},{9,13},{10,... | collective-permute-start | bytes 61448 | tf_op jit(solution)/shard_map/ppermute | solution.py:354
  85.7 1.7 %collective-permute-start.19 = (f32[1,40,128]{2,1,0:T(8,128)S(1)}, f32[1,40,128]{2,1,0:T(8,128)S(1)}, u32[]{:S(2)}, u32[]{:S(2)}) collective-permute-start(f32[1,40,128]{2,1,0:T(8,128)S(1)} %get-tuple-element.61), channel_id=1, source_target_pairs={{0,2},{1,3},{2,0},{3,1},{4,6},{5,7},{6,4},{7,5},{8,10},{9,11},{10,... | collective-permute-start | bytes 61448 | tf_op jit(solution)/shard_map/ppermute | solution.py:354
  87.4 4.5 %shard_map.188 = f32[2,16,64,128]{3,2,1,0:T(8,128)} custom-call(f32[2,16,64,128]{3,2,1,0:T(8,128)S(1)} %get-tuple-element.26.inner.dconv_ref, f32[2,3,64,128]{3,2,1,0:T(8,128)S(1)} %collective-permute-done.11.top, f32[2,3,64,128]{3,2,1,0:T(8,128)S(1)} %collective-permute-done.12.bottom, f32[2,22,3,128]{3,2,1,0:T(4,128)S(1)} %collective-permute-done.13.left, ...), custom_call_target="tpu_custom_call" | custom-call | flops 4000000000 | bytes 4000000 | tf_op jit(solution)/shard_map/pallas_call | solution.py:465
  (74 shorter events, 10.4 us)
Async XLA Ops:
  0.6 35.2 %copy-start = (f32[2,16,64,128]{3,2,1,0:T(8,128)S(1)}, f32[2,16,64,128]{3,2,1,0:T(8,128)}, u32[]{:S(2)}) copy-start(f32[2,16,64,128]{3,2,1,0:T(8,128)} %feat.1) | copy-start | bytes 3145732
  6.8 29.0 %copy-start.10 = (f32[2,16,64,128]{3,2,1,0:T(8,128)S(1)}, f32[2,16,64,128]{3,2,1,0:T(8,128)}, u32[]{:S(2)}) copy-start(f32[2,16,64,128]{3,2,1,0:T(8,128)} %cot_ref.3) | copy-start | bytes 3145732
  6.9 13.7 %collective-permute-start.6 = (f32[1,40,128]{2,1,0:T(8,128)S(1)}, f32[1,40,128]{2,1,0:T(8,128)S(1)}, u32[]{:S(2)}, u32[]{:S(2)}) collective-permute-start(f32[1,40,128]{2,1,0:T(8,128)S(1)} %bitcast.24), channel_id=1, source_target_pairs={{0,6},{1,7},{2,4},{3,5},{4,2},{5,3},{6,0},{7,1},{8,14},{9,15},{10,... | collective-permute-start | bytes 61448 | tf_op jit(solution)/shard_map/ppermute | solution.py:354
  12.0 8.6 %collective-permute-start.5 = (f32[1,40,128]{2,1,0:T(8,128)S(1)}, f32[1,40,128]{2,1,0:T(8,128)S(1)}, u32[]{:S(2)}, u32[]{:S(2)}) collective-permute-start(f32[1,40,128]{2,1,0:T(8,128)S(1)} %bitcast.25), channel_id=1, source_target_pairs={{0,4},{1,5},{2,6},{3,7},{4,0},{5,1},{6,2},{7,3},{8,12},{9,13},{10,... | collective-permute-start | bytes 61448 | tf_op jit(solution)/shard_map/ppermute | solution.py:354
  12.0 8.6 %collective-permute-start.4 = (f32[1,40,128]{2,1,0:T(8,128)S(1)}, f32[1,40,128]{2,1,0:T(8,128)S(1)}, u32[]{:S(2)}, u32[]{:S(2)}) collective-permute-start(f32[1,40,128]{2,1,0:T(8,128)S(1)} %bitcast.26), channel_id=1, source_target_pairs={{0,2},{1,3},{2,0},{3,1},{4,6},{5,7},{6,4},{7,5},{8,10},{9,11},{10,... | collective-permute-start | bytes 61448 | tf_op jit(solution)/shard_map/ppermute | solution.py:354
  13.7 15.9 %collective-permute-start.1 = (f32[2,3,64,128]{3,2,1,0:T(8,128)S(1)}, f32[2,3,64,128]{3,2,1,0:T(8,128)S(1)}, u32[]{:S(2)}, u32[]{:S(2)}) collective-permute-start(f32[2,3,64,128]{3,2,1,0:T(8,128)S(1)} %get-tuple-element.46), channel_id=1, source_target_pairs={{8,0},{16,8},{24,16},{9,1},{17,9},{25,17},{10,2},{18,10},{26,18},{... | collective-permute-start | bytes 589832 | tf_op jit(solution)/shard_map/ppermute | solution.py:350
  15.0 14.6 %collective-permute-start = (f32[2,3,64,128]{3,2,1,0:T(8,128)S(1)}, f32[2,3,64,128]{3,2,1,0:T(8,128)S(1)}, u32[]{:S(2)}, u32[]{:S(2)}) collective-permute-start(f32[2,3,64,128]{3,2,1,0:T(8,128)S(1)} %get-tuple-element.47), channel_id=1, source_target_pairs={{0,8},{8,16},{16,24},{1,9},{9,17},{17,25},{2,10},{10,18},{18,26},{... | collective-permute-start | bytes 589832 | tf_op jit(solution)/shard_map/ppermute | solution.py:350
  20.6 8.8 %collective-permute-start.9 = (f32[4,40,128]{2,1,0:T(8,128)S(1)}, f32[4,40,128]{2,1,0:T(8,128)S(1)}, u32[]{:S(2)}, u32[]{:S(2)}) collective-permute-start(f32[4,40,128]{2,1,0:T(8,128)S(1)} %pad_maximum_fusion.5), channel_id=1, source_target_pairs={{0,24},{1,25},{2,26},{3,27},{4,28},{5,29},{6,30},{7,31},{8,16},{9,... | collective-permute-start | bytes 245768 | tf_op jit(solution)/shard_map/ppermute | solution.py:354
  21.2 8.2 %collective-permute-start.8 = (f32[4,40,128]{2,1,0:T(8,128)S(1)}, f32[4,40,128]{2,1,0:T(8,128)S(1)}, u32[]{:S(2)}, u32[]{:S(2)}) collective-permute-start(f32[4,40,128]{2,1,0:T(8,128)S(1)} %pad_maximum_fusion.5), channel_id=1, source_target_pairs={{0,16},{1,17},{2,18},{3,19},{4,20},{5,21},{6,22},{7,23},{8,24},{9,... | collective-permute-start | bytes 245768 | tf_op jit(solution)/shard_map/ppermute | solution.py:354
  24.7 4.7 %collective-permute-start.7 = (f32[4,40,128]{2,1,0:T(8,128)S(1)}, f32[4,40,128]{2,1,0:T(8,128)S(1)}, u32[]{:S(2)}, u32[]{:S(2)}) collective-permute-start(f32[4,40,128]{2,1,0:T(8,128)S(1)} %pad_maximum_fusion.5), channel_id=1, source_target_pairs={{0,8},{1,9},{2,10},{3,11},{4,12},{5,13},{6,14},{7,15},{8,0},{9,1},... | collective-permute-start | bytes 245768 | tf_op jit(solution)/shard_map/ppermute | solution.py:354
  29.5 3.9 %collective-permute-start.10 = (f32[16,40,128]{2,1,0:T(8,128)S(1)}, f32[16,40,128]{2,1,0:T(8,128)S(1)}, u32[]{:S(2)}, u32[]{:S(2)}) collective-permute-start(f32[16,40,128]{2,1,0:T(8,128)S(1)} %get-tuple-element.63), channel_id=1, source_target_pairs={{0,1},{1,0},{2,3},{3,2},{4,5},{5,4},{6,7},{7,6},{8,9},{9,8},{10,11... | collective-permute-start | bytes 983048 | tf_op jit(solution)/shard_map/ppermute | solution.py:354
  29.6 3.8 %collective-permute-start.2 = (f32[2,22,3,128]{3,2,1,0:T(4,128)S(1)}, f32[2,22,3,128]{3,2,1,0:T(4,128)S(1)}, u32[]{:S(2)}, u32[]{:S(2)}) collective-permute-start(f32[2,22,3,128]{3,2,1,0:T(4,128)S(1)} %pad_maximum_fusion.1), channel_id=1, source_target_pairs={{0,1},{1,2},{2,3},{3,4},{4,5},{5,6},{6,7},{8,9},{9,10},{10,11},{11... | collective-permute-start | bytes 202760 | tf_op jit(solution)/shard_map/ppermute | solution.py:350
  32.1 3.7 %collective-permute-start.3 = (f32[2,22,3,128]{3,2,1,0:T(4,128)S(1)}, f32[2,22,3,128]{3,2,1,0:T(4,128)S(1)}, u32[]{:S(2)}, u32[]{:S(2)}) collective-permute-start(f32[2,22,3,128]{3,2,1,0:T(4,128)S(1)} %pad_maximum_fusion.2), channel_id=1, source_target_pairs={{1,0},{2,1},{3,2},{4,3},{5,4},{6,5},{7,6},{9,8},{10,9},{11,10},{12... | collective-permute-start | bytes 202760 | tf_op jit(solution)/shard_map/ppermute | solution.py:350
  54.7 14.7 %collective-permute-start.11 = (f32[2,3,64,128]{3,2,1,0:T(8,128)S(1)}, f32[2,3,64,128]{3,2,1,0:T(8,128)S(1)}, u32[]{:S(2)}, u32[]{:S(2)}) collective-permute-start(f32[2,3,64,128]{3,2,1,0:T(8,128)S(1)} %get-tuple-element.27), channel_id=1, source_target_pairs={{0,8},{8,16},{16,24},{1,9},{9,17},{17,25},{2,10},{10,18},{18,26},{... | collective-permute-start | bytes 589832 | tf_op jit(solution)/shard_map/ppermute | solution.py:350
  58.0 11.3 %collective-permute-start.12 = (f32[2,3,64,128]{3,2,1,0:T(8,128)S(1)}, f32[2,3,64,128]{3,2,1,0:T(8,128)S(1)}, u32[]{:S(2)}, u32[]{:S(2)}) collective-permute-start(f32[2,3,64,128]{3,2,1,0:T(8,128)S(1)} %get-tuple-element.28), channel_id=1, source_target_pairs={{8,0},{16,8},{24,16},{9,1},{17,9},{25,17},{10,2},{18,10},{26,18},{... | collective-permute-start | bytes 589832 | tf_op jit(solution)/shard_map/ppermute | solution.py:350
  66.4 5.0 %collective-permute-start.15 = (f32[16,40,128]{2,1,0:T(8,128)S(1)}, f32[16,40,128]{2,1,0:T(8,128)S(1)}, u32[]{:S(2)}, u32[]{:S(2)}) collective-permute-start(f32[16,40,128]{2,1,0:T(8,128)S(1)} %pad_maximum_fusion), channel_id=1, source_target_pairs={{0,1},{1,0},{2,3},{3,2},{4,5},{5,4},{6,7},{7,6},{8,9},{9,8},{10,11... | collective-permute-start | bytes 983048 | tf_op jit(solution)/shard_map/ppermute | solution.py:354
  69.4 17.9 %collective-permute-start.13 = (f32[2,22,3,128]{3,2,1,0:T(4,128)S(1)}, f32[2,22,3,128]{3,2,1,0:T(4,128)S(1)}, u32[]{:S(2)}, u32[]{:S(2)}) collective-permute-start(f32[2,22,3,128]{3,2,1,0:T(4,128)S(1)} %pad_maximum_fusion.3), channel_id=1, source_target_pairs={{0,1},{1,2},{2,3},{3,4},{4,5},{5,6},{6,7},{8,9},{9,10},{10,11},{11... | collective-permute-start | bytes 202760 | tf_op jit(solution)/shard_map/ppermute | solution.py:350
  71.5 6.1 %collective-permute-start.16 = (f32[4,40,128]{2,1,0:T(8,128)S(1)}, f32[4,40,128]{2,1,0:T(8,128)S(1)}, u32[]{:S(2)}, u32[]{:S(2)}) collective-permute-start(f32[4,40,128]{2,1,0:T(8,128)S(1)} %get-tuple-element.48), channel_id=1, source_target_pairs={{0,8},{1,9},{2,10},{3,11},{4,12},{5,13},{6,14},{7,15},{8,0},{9,1},... | collective-permute-start | bytes 245768 | tf_op jit(solution)/shard_map/ppermute | solution.py:354
  73.9 7.0 %collective-permute-start.18 = (f32[4,40,128]{2,1,0:T(8,128)S(1)}, f32[4,40,128]{2,1,0:T(8,128)S(1)}, u32[]{:S(2)}, u32[]{:S(2)}) collective-permute-start(f32[4,40,128]{2,1,0:T(8,128)S(1)} %get-tuple-element.49), channel_id=1, source_target_pairs={{0,24},{1,25},{2,26},{3,27},{4,28},{5,29},{6,30},{7,31},{8,16},{9,... | collective-permute-start | bytes 245768 | tf_op jit(solution)/shard_map/ppermute | solution.py:354
  76.2 6.7 %collective-permute-start.17 = (f32[4,40,128]{2,1,0:T(8,128)S(1)}, f32[4,40,128]{2,1,0:T(8,128)S(1)}, u32[]{:S(2)}, u32[]{:S(2)}) collective-permute-start(f32[4,40,128]{2,1,0:T(8,128)S(1)} %get-tuple-element.50), channel_id=1, source_target_pairs={{0,16},{1,17},{2,18},{3,19},{4,20},{5,21},{6,22},{7,23},{8,24},{9,... | collective-permute-start | bytes 245768 | tf_op jit(solution)/shard_map/ppermute | solution.py:354
  76.2 11.1 %collective-permute-start.14 = (f32[2,22,3,128]{3,2,1,0:T(4,128)S(1)}, f32[2,22,3,128]{3,2,1,0:T(4,128)S(1)}, u32[]{:S(2)}, u32[]{:S(2)}) collective-permute-start(f32[2,22,3,128]{3,2,1,0:T(4,128)S(1)} %pad_maximum_fusion.4), channel_id=1, source_target_pairs={{1,0},{2,1},{3,2},{4,3},{5,4},{6,5},{7,6},{9,8},{10,9},{11,10},{12... | collective-permute-start | bytes 202760 | tf_op jit(solution)/shard_map/ppermute | solution.py:350
  82.9 9.0 %collective-permute-start.21 = (f32[1,40,128]{2,1,0:T(8,128)S(1)}, f32[1,40,128]{2,1,0:T(8,128)S(1)}, u32[]{:S(2)}, u32[]{:S(2)}) collective-permute-start(f32[1,40,128]{2,1,0:T(8,128)S(1)} %get-tuple-element.59), channel_id=1, source_target_pairs={{0,6},{1,7},{2,4},{3,5},{4,2},{5,3},{6,0},{7,1},{8,14},{9,15},{10,... | collective-permute-start | bytes 61448 | tf_op jit(solution)/shard_map/ppermute | solution.py:354
  83.7 8.2 %collective-permute-start.20 = (f32[1,40,128]{2,1,0:T(8,128)S(1)}, f32[1,40,128]{2,1,0:T(8,128)S(1)}, u32[]{:S(2)}, u32[]{:S(2)}) collective-permute-start(f32[1,40,128]{2,1,0:T(8,128)S(1)} %get-tuple-element.60), channel_id=1, source_target_pairs={{0,4},{1,5},{2,6},{3,7},{4,0},{5,1},{6,2},{7,3},{8,12},{9,13},{10,... | collective-permute-start | bytes 61448 | tf_op jit(solution)/shard_map/ppermute | solution.py:354
  85.7 6.2 %collective-permute-start.19 = (f32[1,40,128]{2,1,0:T(8,128)S(1)}, f32[1,40,128]{2,1,0:T(8,128)S(1)}, u32[]{:S(2)}, u32[]{:S(2)}) collective-permute-start(f32[1,40,128]{2,1,0:T(8,128)S(1)} %get-tuple-element.61), channel_id=1, source_target_pairs={{0,2},{1,3},{2,0},{3,1},{4,6},{5,7},{6,4},{7,5},{8,10},{9,11},{10,... | collective-permute-start | bytes 61448 | tf_op jit(solution)/shard_map/ppermute | solution.py:354
  (10 other events, 7.6 us)

commit v2 on v1

--- a/solution.py
+++ b/solution.py
@@ -26,19 +26,19 @@
 NN = (((1,), (0,)), ((), ()))
 NT = (((1,), (1,)), ((), ()))
 f32, bf16 = jnp.float32, jnp.bfloat16
-VMEM_LIMIT = 48 * 1024 * 1024
 
 
 def ceil8(n):
     return (n + 7) // 8 * 8
 
 
-def call(body, outs, scratch=(), flops=0, size=0):
+def call(body, outs, scratch=(), flops=0, size=0, limit=8, **more):
     return pl.pallas_call(
         body,
         out_shape=outs,
         scratch_shapes=list(scratch),
-        compiler_params=pltpu.CompilerParams(vmem_limit_bytes=VMEM_LIMIT),
+        compiler_params=pltpu.CompilerParams(vmem_limit_bytes=limit * 1024 * 1024),
+        **more,
         cost_estimate=pl.CostEstimate(flops=flops, bytes_accessed=size, transcendentals=0),
     )
 
@@ -75,20 +75,74 @@
     return x
 
 
-def pack_body(ms, kernel_ref, cb, ng, ns, ob, ls, win_ref, ib, wout_ref, out_ref):
-    taps_i, cs, taps_j = kernel_ref.shape
-    hs = win_ref.shape[0]
+def pairs(count, second):
+    if not second:
+        return [(i, i ^ 1) for i in range(count)]
+    return [(i, (i + 1 if i % 2 else i - 1) % count) for i in range(count)]
+
+
+def both_pairs(a, b, axis):
+    count = lax.axis_size(axis)
+    return lax.ppermute(a, axis, pairs(count, False)), lax.ppermute(b, axis, pairs(count, True))
+
+
+def side(ms, axis):
+    i = lax.axis_index(axis)
+    even = i % 2 == 0
+    return even, jnp.where(even, i > 0, i < ms[axis] - 1)
+
+
+def start_body(ms, feat, kernel_hbm, cb, ng, ns, ob, ls, win_hbm, ib, wout_hbm, out_ref, row_a, row_b, col_a, col_b,
+               kernel_scr, v0, v1, v2, v3, v4, ib_scr, win_scr, wout_scr, low, high, sems):
+    batch, rows, cols, C = feat.shape
+    taps_i, cs, taps_j = kernel_hbm.shape
+    hs = win_hbm.shape[0]
     taps = taps_i * taps_j
+    m = taps_i // 2
+    even_r, _ = side(ms, "row")
+    even_c, _ = side(ms, "col")
+    far = jnp.where(even_r, rows - m, 0)
+    near = jnp.where(even_r, 0, rows - m)
+    vectors = (v0, v1, v2, v3, v4)
+    moves = [(kernel_hbm, kernel_scr), (win_hbm, win_scr), (wout_hbm, wout_scr), (ib, ib_scr)]
+    moves += list(zip((cb, ng, ns, ob, ls), vectors))
+    moves += [(feat.at[:, pl.ds(far, m)], row_a), (feat.at[:, pl.ds(near, m)], row_b)]
+    moves += [(feat.at[:, :, 0:8], low), (feat.at[:, :, cols - 8 : cols], high)]
+    copies = [pltpu.make_async_copy(src, dst, sems.at[n]) for n, (src, dst) in enumerate(moves)]
+    for copy in copies:
+        copy.start()
     out_ref[...] = jnp.zeros_like(out_ref)
-    out_ref[0:hs, :] = win_ref[...]
-    out_ref[hs : 2 * hs, :] = wout_ref[...]
+    for copy in copies:
+        copy.wait()
+    out_ref[0:hs, :] = win_scr[...]
+    out_ref[hs : 2 * hs, :] = wout_scr[...]
     base = 2 * hs
     for i in range(taps_i):
-        out_ref[base : base + cs, i * taps_j : (i + 1) * taps_j] = kernel_ref[i]
-    for n, ref in enumerate((cb, ng, ns, ob, ls)):
+        out_ref[base : base + cs, i * taps_j : (i + 1) * taps_j] = kernel_scr[i]
+    for n, ref in enumerate(vectors):
         column = jnp.broadcast_to(ref[...], (8, cs)).T
         out_ref[base : base + cs, taps + n : taps + n + 1] = column[:, 0:1]
-    out_ref[base + cs : base + cs + 1, 0:hs] = ib[...]
+    out_ref[base + cs : base + cs + 1, 0:hs] = ib_scr[...]
+    first, last = low[:, :, 0:m], high[:, :, 8 - m : 8]
+    col_a[...] = jnp.where(even_c, last, first)
+    col_b[...] = jnp.where(even_c, first, last)
+
+
+def sides_body(ms, edge_a, edge_b, got_a, got_b, out_a, out_b):
+    batch, rows, m, C = edge_a.shape
+    cols = got_a.shape[2]
+    even_r, true_r = side(ms, "row")
+    even_c, _ = side(ms, "col")
+    out_a[:, m : m + rows] = edge_a[...]
+    out_b[:, m : m + rows] = edge_b[...]
+    for got, end, keep in ((got_a, even_r, None), (got_b, jnp.logical_not(even_r), true_r)):
+        at = jnp.where(end, rows + m, 0)
+        x = got[...]
+        if keep is not None:
+            x = jnp.where(keep, x, 0.0)
+        last, first = x[:, :, cols - m :], x[:, :, 0:m]
+        out_a[:, pl.ds(at, m)] = jnp.where(even_c, last, first)
+        out_b[:, pl.ds(at, m)] = jnp.where(even_c, first, last)
 
 
 def depthwise_block(read, weight, rows, taps_i, taps_j, start):
@@ -105,15 +159,20 @@
     return acc
 
 
-def fill(dst, inner, top, bottom, left, right):
+def fill(ms, dst, inner, row_a, row_b, col_a, col_b):
     batch, rows, cols, _ = inner.shape
-    m = top.shape[1]
+    m = row_a.shape[1]
+    even_r, true_r = side(ms, "row")
+    even_c, true_c = side(ms, "col")
+    at_a = jnp.where(even_r, rows + m, 0)
+    at_b = jnp.where(even_r, 0, rows + m)
     for b in range(batch):
         dst[b, m : m + rows, LEFT : LEFT + cols, :] = inner[b]
-        dst[b, 0:m, LEFT : LEFT + cols, :] = top[b]
-        dst[b, m + rows : m + rows + m, LEFT : LEFT + cols, :] = bottom[b]
-        dst[b, :, LEFT - m : LEFT, :] = left[b]
-        dst[b, :, LEFT + cols : LEFT + cols + m, :] = right[b]
+        dst[b, pl.ds(at_a, m), LEFT : LEFT + cols, :] = row_a[b]
+        dst[b, pl.ds(at_b, m), LEFT : LEFT + cols, :] = jnp.where(true_r, row_b[b], 0.0)
+        x, y = col_a[b], jnp.where(true_c, col_b[b], 0.0)
+        dst[b, :, LEFT - m : LEFT, :] = jnp.where(even_c, y, x)
+        dst[b, :, LEFT + cols : LEFT + cols + m, :] = jnp.where(even_c, x, y)
 
 
 def small_columns(slots_ref, hs, cs, count, me, order, scratch):
@@ -125,8 +184,8 @@
 
 def mix_body(
     ms, order, factor, taps_i, taps_j, tile,
-    feat, top, bottom, left, right, slots_ref, cot_ref,
-    src_ref, dconv_ref, edge_top, edge_bottom, grads_ref, chan_ref, small_ref,
+    feat, got_ra, got_rb, got_ca, got_cb, slots_ref, cot_ref,
+    src_ref, dconv_ref, row_a, row_b, col_a, col_b, grads_ref, chan_ref, small_ref,
     conv_scr, cols_scr, kb_scr, win_scr, wout_scr, w1_scr, w2_scr, w4_scr, bias_scr,
     gw1_scr, gw2_scr, gb_scr, gg_scr, gs_scr, gc_scr, cot_sum,
 ):
@@ -139,7 +198,7 @@
     hs = hid // count
     me = device_index(ms)
 
-    fill(src_ref, feat, top, bottom, left, right)
+    fill(ms, src_ref, feat, got_ra, got_rb, got_ca, got_cb)
     columns = small_columns(slots_ref, hs, cs, count, me, order, cols_scr)
     cols_scr[...] = columns
     rows_form = columns.T
@@ -246,8 +305,13 @@
 
     lax.fori_loop(0, batch * per_image, step, 0)
 
-    edge_top[...] = dconv_ref[:, 0:m]
-    edge_bottom[...] = dconv_ref[:, rows - m : rows]
+    even_r, _ = side(ms, "row")
+    even_c, _ = side(ms, "col")
+    row_a[...] = dconv_ref[:, pl.ds(jnp.where(even_r, rows - m, 0), m)]
+    row_b[...] = dconv_ref[:, pl.ds(jnp.where(even_r, 0, rows - m), m)]
+    first, last = dconv_ref[:, :, 0:m], dconv_ref[:, :, cols - m : cols]
+    col_a[...] = jnp.where(even_c, last, first)
+    col_b[...] = jnp.where(even_c, first, last)
 
     h = gw2_scr[:, 0:C] + gw2_scr[:, C : 2 * C]
     gw1 = (gw1_scr[:, 0:C] + gw1_scr[:, C : 2 * C]) * factor
@@ -304,11 +368,11 @@
         out_ref[s, cs : cs + 1, 0:hs] = chan_ref[5:6, s * hs : (s + 1) * hs]
 
 
-def features_grad_body(taps_i, taps_j, inner, top, bottom, left, right, small_ref, cot_ref, out_ref, ext_scr, kb_scr):
+def features_grad_body(ms, taps_i, taps_j, inner, got_ra, got_rb, got_ca, got_cb, small_ref, cot_ref, out_ref, ext_scr, kb_scr):
     batch, rows, cols, C = inner.shape
     m = taps_i // 2
     taps = taps_i * taps_j
-    fill(ext_scr, inner, top, bottom, left, right)
+    fill(ms, ext_scr, inner, got_ra, got_rb, got_ca, got_cb)
     for t in range(taps):
         kb_scr[t] = jnp.broadcast_to(small_ref[t : t + 1, :], (8, C))
 
@@ -344,12 +408,6 @@
     ib[...] = small[cs : cs + 1, 0:hs]
 
 
-def shifted(x, axis, step):
-    count = lax.axis_size(axis)
-    pairs = [(i, i + step) for i in range(count) if 0 <= i + step < count]
-    return lax.ppermute(x, axis, pairs)
-
-
 def flip(x, mask, count):
     return lax.ppermute(x, AXES, [(i, i ^ mask) for i in range(count)])
 
@@ -385,13 +443,38 @@
     slot = 2 * hs + 8
     wide = ceil8(LEFT + cols + m)
 
-    block = call(functools.partial(pack_body, ms), shape(slot, LANES), size=100000)(
-        conv_kernel.transpose(0, 2, 1),
-        *(v.reshape(1, cs) for v in (conv_bias, norm_gain, norm_shift, out_bias, layer_scale)),
-        w_in.T, in_bias.reshape(1, hs), w_out,
-    )
-    top = shifted(features[:, rows - m :], "row", 1)
-    bottom = shifted(features[:, :m], "row", -1)
+    vm = pltpu.VMEM
+    vectors = [v.reshape(1, cs) for v in (conv_bias, norm_gain, norm_shift, out_bias, layer_scale)]
+    block, row_a, row_b, col_a, col_b = call(
+        functools.partial(start_body, ms),
+        (
+            shape(slot, LANES),
+            *(shape(batch, m, cols, C) for _ in range(2)),
+            *(shape(batch, rows, m, C) for _ in range(2)),
+        ),
+        scratch=(
+            vm((taps_i, cs, taps_j), f32),
+            *(vm((1, cs), f32) for _ in range(5)),
+            vm((1, hs), f32),
+            vm((hs, C), f32),
+            vm((hs, C), f32),
+            vm((batch, rows, 8, C), f32),
+            vm((batch, rows, 8, C), f32),
+            pltpu.SemaphoreType.DMA((13,)),
+        ),
+        size=10**6,
+        in_specs=[pl.BlockSpec(memory_space=pltpu.HBM)] * 10,
+    )(features, conv_kernel.transpose(0, 2, 1), *vectors, w_in.T, in_bias.reshape(1, hs), w_out)
+
+    def sides(edge_a, edge_b, got_a, got_b):
+        out = call(
+            functools.partial(sides_body, ms),
+            tuple(shape(batch, rows + 2 * m, m, C) for _ in range(2)),
+            size=10**6,
+        )(edge_a, edge_b, got_a, got_b)
+        return both_pairs(*out, "col")
+
+    got_ra, got_rb = both_pairs(row_a, row_b, "row")
     slots = block[None]
     groups = groups_of(ms)
     order = [0]
@@ -399,21 +482,15 @@
         order = [mask ^ x for mask in masks(group) for x in order]
         slots = jnp.concatenate([slots] + [flip(slots, mask, count) for mask in masks(group)[1:]])
 
-    def sides(top, inner, bottom):
-        low = jnp.concatenate([x[:, :, cols - m :] for x in (top, inner, bottom)], axis=1)
-        high = jnp.concatenate([x[:, :, :m] for x in (top, inner, bottom)], axis=1)
-        return shifted(low, "col", 1), shifted(high, "col", -1)
-
-    left, right = sides(top, features, bottom)
+    got_ca, got_cb = sides(col_a, col_b, got_ra, got_rb)
     tile = 4 * cols
-    vm = pltpu.VMEM
-    src, dconv, edge_top, edge_bottom, grads, chan, small = call(
+    src, dconv, d_row_a, d_row_b, d_col_a, d_col_b, grads, chan, small = call(
         functools.partial(mix_body, ms, order, factor, taps_i, taps_j, tile),
         (
             shape(batch, rows + 2 * m, wide, C),
             shape(batch, rows, cols, C),
-            shape(batch, m, cols, C),
-            shape(batch, m, cols, C),
+            *(shape(batch, m, cols, C) for _ in range(2)),
+            *(shape(batch, rows, m, C) for _ in range(2)),
             shape(count, 2 * hs, C),
             shape(8, hid),
             shape(LANES, C),
@@ -438,10 +515,10 @@
         ),
         flops=12 * 10**9,
         size=8 * 10**6,
-    )(features, top, bottom, left, right, slots, cotangent)
-
-    d_top = shifted(edge_bottom, "row", 1)
-    d_bottom = shifted(edge_top, "row", -1)
+        limit=24,
+    )(features, got_ra, got_rb, got_ca, got_cb, slots, cotangent)
+
+    d_got_ra, d_got_rb = both_pairs(d_row_a, d_row_b, "row")
     smalls = call(
         functools.partial(kernel_grad_body, ms, order, factor, taps_i, taps_j, count),
         shape(count, 8, LANES),
@@ -450,7 +527,7 @@
         size=4 * 10**6,
     )(src, dconv, chan)
 
-    d_left, d_right = sides(d_top, dconv, d_bottom)
+    d_got_ca, d_got_cb = sides(d_col_a, d_col_b, d_got_ra, d_got_rb)
 
     parts = [jnp.concatenate([grads, smalls], axis=1)]
     for group in groups[::-1]:
@@ -463,12 +540,12 @@
         parts += [flip(whole[k * step : (k + 1) * step], mask, count) for k, mask in enumerate(order) if k]
 
     features_grad = call(
-        functools.partial(features_grad_body, taps_i, taps_j),
+        functools.partial(features_grad_body, ms, taps_i, taps_j),
         shape(batch, rows, cols, C),
         scratch=(vm((batch, rows + 2 * m, wide, C), f32), vm((taps, 8, C), f32)),
         flops=4 * 10**9,
         size=4 * 10**6,
-    )(dconv, d_top, d_bottom, d_left, d_right, small, cotangent)
+    )(dconv, d_got_ra, d_got_rb, d_got_ca, d_got_cb, small, cotangent)
 
     outs = call(
         functools.partial(finish_body, taps_i, taps_j, cs, hs),

time: 93.2 us -> 92.4 us (level)
  waiting for transfers between devices: 12.4 us -> 30.3 us
  starting transfers between devices: 39.4 us -> 25.5 us
  local copies, waits for them, and re-layouts: 9.81 us -> 7.36 us
  Pallas kernels: 29.8 us -> 27.9 us
    ppermute x8, waiting for transfers between devices: 2.38 us -> 20.7 us  [the longest x4 13.8 us: both_pairs(): lax.ppermute(b, axis, pairs(count, True))]
    ppermute x8, starting transfers between devices: 17.4 us -> 8.06 us  [the longest x4 6.71 us: both_pairs(): lax.ppermute(b, axis, pairs(count, True))]
    ppermute x14, starting transfers between devices: 22 us -> 17.5 us  [flip(): return lax.ppermute(x, AXES, [(i, i ^ mask) for i in range(count)])]
    pallas_call x1, Pallas kernels: 18.9 us -> 16.4 us  [per_device(): call(functools.partial(mix_body, ms, order, factor, taps_i, taps_j, tile)...]
    slice x7 -> x0, local copies, waits for them, and re-layouts: 2.1 us -> none  [the longest x6 1.05 us: sides(): high = jnp.concatenate([x[:, :, :m] for x in (top, inner, bottom)], axis=1)]
    pallas_call x2 -> x4, Pallas kernels: 4.67 us -> 5.24 us  [the longest x1 4.55 us: per_device(): call(functools.partial(features_grad_body, ms, taps_i, taps_j), shape(bat...]
  transfers between devices with their start and end apart: 22 -> 22, of which waited for: 4 -> 10; matrix products, arithmetic and copies ran while one was open for 3% -> 0% of each run, Pallas kernels for 11% -> 5%
where the time goes in v2:
time: 92.4 us; the launch traced here: 91.9 us
  waiting for transfers between devices  30.3 us (33%)
  Pallas kernels  27.9 us (30%)
  starting transfers between devices  25.5 us (28%)
  local copies, waits for them, and re-layouts  7.36 us (8%)
    ppermute x14, starting transfers between devices, flip(): return lax.ppermute(x, AXES, [(i, i ^ mask) for i in range(count)])  17.5 us
    pallas_call x1, Pallas kernels, per_device(): call(functools.partial(mix_body, ms, order, factor, taps_i, taps_j, tile)...  16.4 us
    ppermute x4, waiting for transfers between devices, both_pairs(): lax.ppermute(b, axis, pairs(count, True))  13.8 us
    ppermute x14, waiting for transfers between devices, flip(): return lax.ppermute(x, AXES, [(i, i ^ mask) for i in range(count)])  9.6 us
    unnamed x30, local copies, waits for them, and re-layouts  7.3 us
    ppermute x4, waiting for transfers between devices, both_pairs(): lax.ppermute(a, axis, pairs(count, False))  6.83 us
    ppermute x4, starting transfers between devices, both_pairs(): lax.ppermute(b, axis, pairs(count, True))  6.71 us
    pallas_call x1, Pallas kernels, per_device(): call(functools.partial(kernel_grad_body, ms, order, factor, taps_i, taps_...  5.52 us
  transfers between devices with their start and end apart: 22, of which 10 were waited for; matrix products, arithmetic and copies ran while one was open for 0% of the time, Pallas kernels for 5%

profile of v2, /device:TPU:0, one launch (start us, length us, event | category | flops | bytes accessed | tf_op | source)
XLA Modules:
  0.0 91.9 jit_solution(7376024856920053152)
XLA Ops:
  0.7 1.2 %copy-done = f32[2,16,64,128]{3,2,1,0:T(8,128)S(1)} copy-done((f32[2,16,64,128]{3,2,1,0:T(8,128)S(1)}, f32[2,16,64,128]{3,2,1,0:T(8,128)}, u32[]{:S(2)}) %copy-start) | copy-done | bytes 1048600
  1.9 0.7 copy-done.2
  8.5 5.1 %collective-permute-start.6 = (f32[1,40,128]{2,1,0:T(8,128)S(1)}, f32[1,40,128]{2,1,0:T(8,128)S(1)}, u32[]{:S(2)}, u32[]{:S(2)}) collective-permute-start(f32[1,40,128]{2,1,0:T(8,128)S(1)} %bitcast.24), channel_id=1, source_target_pairs={{0,6},{1,7},{2,4},{3,5},{4,2},{5,3},{6,0},{7,1},{8,14},{9,15},{10,... | collective-permute-start | bytes 61448 | tf_op jit(solution)/shard_map/ppermute | solution.py:412
  14.3 1.1 %collective-permute-done.6 = f32[1,40,128]{2,1,0:T(8,128)S(1)} collective-permute-done((f32[1,40,128]{2,1,0:T(8,128)S(1)}, f32[1,40,128]{2,1,0:T(8,128)S(1)}, u32[]{:S(2)}, u32[]{:S(2)}) %collective-permute-start.6) | collective-permute-done | bytes 20512 | tf_op jit(solution)/shard_map/ppermute | solution.py:412
  15.4 2.9 %collective-permute-done.5 = f32[1,40,128]{2,1,0:T(8,128)S(1)} collective-permute-done((f32[1,40,128]{2,1,0:T(8,128)S(1)}, f32[1,40,128]{2,1,0:T(8,128)S(1)}, u32[]{:S(2)}, u32[]{:S(2)}) %collective-permute-start.5) | collective-permute-done | bytes 20512 | tf_op jit(solution)/shard_map/ppermute | solution.py:412
  18.4 2.5 %collective-permute-start.9 = (f32[4,40,128]{2,1,0:T(8,128)S(1)}, f32[4,40,128]{2,1,0:T(8,128)S(1)}, u32[]{:S(2)}, u32[]{:S(2)}) collective-permute-start(f32[4,40,128]{2,1,0:T(8,128)S(1)} %pad_maximum_fusion.1), channel_id=1, source_target_pairs={{0,24},{1,25},{2,26},{3,27},{4,28},{5,29},{6,30},{7,31},{8,16},{9,... | collective-permute-start | bytes 245768 | tf_op jit(solution)/shard_map/ppermute | solution.py:412
  21.9 3.9 %collective-permute-done.7 = f32[4,40,128]{2,1,0:T(8,128)S(1)} collective-permute-done((f32[4,40,128]{2,1,0:T(8,128)S(1)}, f32[4,40,128]{2,1,0:T(8,128)S(1)}, u32[]{:S(2)}, u32[]{:S(2)}) %collective-permute-start.7) | collective-permute-done | bytes 81952 | tf_op jit(solution)/shard_map/ppermute | solution.py:412
  26.6 2.4 %collective-permute-start.1 = (f32[2,3,64,128]{3,2,1,0:T(8,128)S(1)}, f32[2,3,64,128]{3,2,1,0:T(8,128)S(1)}, u32[]{:S(2)}, u32[]{:S(2)}) collective-permute-start(f32[2,3,64,128]{3,2,1,0:T(8,128)S(1)} %get-tuple-element.38), channel_id=1, source_target_pairs={{0,24},{8,16},{16,8},{24,0},{1,25},{9,17},{17,9},{25,1},{2,26},{10... | collective-permute-start | bytes 589832 | tf_op jit(solution)/shard_map/ppermute | solution.py:86
  29.0 4.7 %collective-permute-done.got_a.got_ra = f32[2,3,64,128]{3,2,1,0:T(8,128)S(1)} collective-permute-done((f32[2,3,64,128]{3,2,1,0:T(8,128)S(1)}, f32[2,3,64,128]{3,2,1,0:T(8,128)S(1)}, u32[]{:S(2)}, u32[]{:S(2)}) %collective-permute-start) | collective-permute-done | bytes 196640 | tf_op jit(solution)/shard_map/ppermute | solution.py:86
  33.7 4.7 %collective-permute-done.1.got_b.got_rb = f32[2,3,64,128]{3,2,1,0:T(8,128)S(1)} collective-permute-done((f32[2,3,64,128]{3,2,1,0:T(8,128)S(1)}, f32[2,3,64,128]{3,2,1,0:T(8,128)S(1)}, u32[]{:S(2)}, u32[]{:S(2)}) %collective-permute-start.1) | collective-permute-done | bytes 196640 | tf_op jit(solution)/shard_map/ppermute | solution.py:86
  38.6 1.6 %collective-permute-start.3 = (f32[2,22,3,128]{3,2,1,0:T(4,128)S(1)}, f32[2,22,3,128]{3,2,1,0:T(4,128)S(1)}, u32[]{:S(2)}, u32[]{:S(2)}) collective-permute-start(f32[2,22,3,128]{3,2,1,0:T(4,128)S(1)} %get-tuple-element.42), channel_id=1, source_target_pairs={{0,7},{1,2},{2,1},{3,4},{4,3},{5,6},{6,5},{7,0},{8,15},{9,10},{10,... | collective-permute-start | bytes 202760 | tf_op jit(solution)/shard_map/ppermute | solution.py:86
  40.2 4.9 %collective-permute-done.3.got_cb = f32[2,22,3,128]{3,2,1,0:T(4,128)S(1)} collective-permute-done((f32[2,22,3,128]{3,2,1,0:T(4,128)S(1)}, f32[2,22,3,128]{3,2,1,0:T(4,128)S(1)}, u32[]{:S(2)}, u32[]{:S(2)}) %collective-permute-start.3) | collective-permute-done | bytes 67616 | tf_op jit(solution)/shard_map/ppermute | solution.py:86
  45.1 16.4 %shard_map.188 = (f32[2,22,80,128]{3,2,1,0:T(8,128)S(1)}, f32[2,16,64,128]{3,2,1,0:T(8,128)S(1)}, f32[2,3,64,128]{3,2,1,0:T(8,128)S(1)}, f32[2,3,64,128]{3,2,1,0...) custom-call(f32[2,16,64,128]{3,2,1,0:T(8,128)S(1)} %copy-done.1, ...), custom_call_target="tpu_custom_call" | custom-call | flops 12000000000 | bytes 8000000 | tf_op jit(solution)/shard_map/pallas_call | solution.py:487
  61.5 5.5 %shard_map.191 = f32[32,8,128]{2,1,0:T(8,128)S(1)} custom-call(f32[2,22,80,128]{3,2,1,0:T(8,128)S(1)} %get-tuple-element.53.src_ref, f32[2,16,64,128]{3,2,1,0:T(8,128)S(1)} %get-tuple-element.44.inner.dconv_ref, f32[8,512]{1,0:T(8,128)S(1)} %get-tuple-element.54.chan_ref), custom_call_target="tpu_custom_call" | custom-call | flops 4000000000 | bytes 4000000 | tf_op jit(solution)/shard_map/pallas_call | solution.py:522
  67.7 1.4 %collective-permute-start.12 = (f32[2,3,64,128]{3,2,1,0:T(8,128)S(1)}, f32[2,3,64,128]{3,2,1,0:T(8,128)S(1)}, u32[]{:S(2)}, u32[]{:S(2)}) collective-permute-start(f32[2,3,64,128]{3,2,1,0:T(8,128)S(1)} %get-tuple-element.46), channel_id=1, source_target_pairs={{0,24},{8,16},{16,8},{24,0},{1,25},{9,17},{17,9},{25,1},{2,26},{10... | collective-permute-start | bytes 589832 | tf_op jit(solution)/shard_map/ppermute | solution.py:86
  69.8 2.4 %collective-permute-start.18 = (f32[4,40,128]{2,1,0:T(8,128)S(1)}, f32[4,40,128]{2,1,0:T(8,128)S(1)}, u32[]{:S(2)}, u32[]{:S(2)}) collective-permute-start(f32[4,40,128]{2,1,0:T(8,128)S(1)} %get-tuple-element.65), channel_id=1, source_target_pairs={{0,24},{1,25},{2,26},{3,27},{4,28},{5,29},{6,30},{7,31},{8,16},{9,... | collective-permute-start | bytes 245768 | tf_op jit(solution)/shard_map/ppermute | solution.py:412
  72.8 2.1 %collective-permute-done.11.got_a.got_ra = f32[2,3,64,128]{3,2,1,0:T(8,128)S(1)} collective-permute-done((f32[2,3,64,128]{3,2,1,0:T(8,128)S(1)}, f32[2,3,64,128]{3,2,1,0:T(8,128)S(1)}, u32[]{:S(2)}, u32[]{:S(2)}) %collective-permute-start.11) | collective-permute-done | bytes 196640 | tf_op jit(solution)/shard_map/ppermute | solution.py:86
  74.9 4.2 %collective-permute-done.12.got_b.got_rb = f32[2,3,64,128]{3,2,1,0:T(8,128)S(1)} collective-permute-done((f32[2,3,64,128]{3,2,1,0:T(8,128)S(1)}, f32[2,3,64,128]{3,2,1,0:T(8,128)S(1)}, u32[]{:S(2)}, u32[]{:S(2)}) %collective-permute-start.12) | collective-permute-done | bytes 196640 | tf_op jit(solution)/shard_map/ppermute | solution.py:86
  79.2 1.3 %collective-permute-start.14 = (f32[2,22,3,128]{3,2,1,0:T(4,128)S(1)}, f32[2,22,3,128]{3,2,1,0:T(4,128)S(1)}, u32[]{:S(2)}, u32[]{:S(2)}) collective-permute-start(f32[2,22,3,128]{3,2,1,0:T(4,128)S(1)} %get-tuple-element.50), channel_id=1, source_target_pairs={{0,7},{1,2},{2,1},{3,4},{4,3},{5,6},{6,5},{7,0},{8,15},{9,10},{10,... | collective-permute-start | bytes 202760 | tf_op jit(solution)/shard_map/ppermute | solution.py:86
  80.9 1.3 %collective-permute-done.18 = f32[4,40,128]{2,1,0:T(8,128)S(1)} collective-permute-done((f32[4,40,128]{2,1,0:T(8,128)S(1)}, f32[4,40,128]{2,1,0:T(8,128)S(1)}, u32[]{:S(2)}, u32[]{:S(2)}) %collective-permute-start.18) | collective-permute-done | bytes 81952 | tf_op jit(solution)/shard_map/ppermute | solution.py:412
  82.2 0.8 collective-permute-start.21
  83.0 3.6 %collective-permute-start.19 = (f32[1,40,128]{2,1,0:T(8,128)S(1)}, f32[1,40,128]{2,1,0:T(8,128)S(1)}, u32[]{:S(2)}, u32[]{:S(2)}) collective-permute-start(f32[1,40,128]{2,1,0:T(8,128)S(1)} %get-tuple-element.69), channel_id=1, source_target_pairs={{0,2},{1,3},{2,0},{3,1},{4,6},{5,7},{6,4},{7,5},{8,10},{9,11},{10,... | collective-permute-start | bytes 61448 | tf_op jit(solution)/shard_map/ppermute | solution.py:412
  86.7 4.5 %shard_map.190 = f32[2,16,64,128]{3,2,1,0:T(8,128)} custom-call(f32[2,16,64,128]{3,2,1,0:T(8,128)S(1)} %get-tuple-element.44.inner.dconv_ref, f32[2,3,64,128]{3,2,1,0:T(8,128)S(1)} %collective-permute-done.11.got_a.got_ra, f32[2,3,64,128]{3,2,1,0:T(8,128)S(1)} %collective-permute-done.12.got_b.got_rb, f32[2,22,3,128]{3,2,1,0:T(4,128)S(1)} %collective-permute-done.13.got_ca, ...), custom_call_target="tpu_custom_call" | custom-call | flops 4000000000 | bytes 4000000 | tf_op jit(solution)/shard_map/pallas_call | solution.py:542
  91.2 0.7 shard_map.192
  (65 shorter events, 10.9 us)
Async XLA Ops:
  7.9 37.2 %copy-start.1 = (f32[2,16,64,128]{3,2,1,0:T(8,128)S(1)}, f32[2,16,64,128]{3,2,1,0:T(8,128)}, u32[]{:S(2)}) copy-start(f32[2,16,64,128]{3,2,1,0:T(8,128)} %feat.3) | copy-start | bytes 3145732
  7.9 37.2 %copy-start.11 = (f32[2,16,64,128]{3,2,1,0:T(8,128)S(1)}, f32[2,16,64,128]{3,2,1,0:T(8,128)}, u32[]{:S(2)}) copy-start(f32[2,16,64,128]{3,2,1,0:T(8,128)} %cot_ref.3) | copy-start | bytes 3145732
  8.5 6.9 %collective-permute-start.6 = (f32[1,40,128]{2,1,0:T(8,128)S(1)}, f32[1,40,128]{2,1,0:T(8,128)S(1)}, u32[]{:S(2)}, u32[]{:S(2)}) collective-permute-start(f32[1,40,128]{2,1,0:T(8,128)S(1)} %bitcast.24), channel_id=1, source_target_pairs={{0,6},{1,7},{2,4},{3,5},{4,2},{5,3},{6,0},{7,1},{8,14},{9,15},{10,... | collective-permute-start | bytes 61448 | tf_op jit(solution)/shard_map/ppermute | solution.py:412
  13.7 4.7 %collective-permute-start.5 = (f32[1,40,128]{2,1,0:T(8,128)S(1)}, f32[1,40,128]{2,1,0:T(8,128)S(1)}, u32[]{:S(2)}, u32[]{:S(2)}) collective-permute-start(f32[1,40,128]{2,1,0:T(8,128)S(1)} %bitcast.25), channel_id=1, source_target_pairs={{0,4},{1,5},{2,6},{3,7},{4,0},{5,1},{6,2},{7,3},{8,12},{9,13},{10,... | collective-permute-start | bytes 61448 | tf_op jit(solution)/shard_map/ppermute | solution.py:412
  13.7 4.7 %collective-permute-start.4 = (f32[1,40,128]{2,1,0:T(8,128)S(1)}, f32[1,40,128]{2,1,0:T(8,128)S(1)}, u32[]{:S(2)}, u32[]{:S(2)}) collective-permute-start(f32[1,40,128]{2,1,0:T(8,128)S(1)} %bitcast.26), channel_id=1, source_target_pairs={{0,2},{1,3},{2,0},{3,1},{4,6},{5,7},{6,4},{7,5},{8,10},{9,11},{10,... | collective-permute-start | bytes 61448 | tf_op jit(solution)/shard_map/ppermute | solution.py:412
  18.4 7.5 %collective-permute-start.9 = (f32[4,40,128]{2,1,0:T(8,128)S(1)}, f32[4,40,128]{2,1,0:T(8,128)S(1)}, u32[]{:S(2)}, u32[]{:S(2)}) collective-permute-start(f32[4,40,128]{2,1,0:T(8,128)S(1)} %pad_maximum_fusion.1), channel_id=1, source_target_pairs={{0,24},{1,25},{2,26},{3,27},{4,28},{5,29},{6,30},{7,31},{8,16},{9,... | collective-permute-start | bytes 245768 | tf_op jit(solution)/shard_map/ppermute | solution.py:412
  20.9 5.0 %collective-permute-start.8 = (f32[4,40,128]{2,1,0:T(8,128)S(1)}, f32[4,40,128]{2,1,0:T(8,128)S(1)}, u32[]{:S(2)}, u32[]{:S(2)}) collective-permute-start(f32[4,40,128]{2,1,0:T(8,128)S(1)} %pad_maximum_fusion.1), channel_id=1, source_target_pairs={{0,16},{1,17},{2,18},{3,19},{4,20},{5,21},{6,22},{7,23},{8,24},{9,... | collective-permute-start | bytes 245768 | tf_op jit(solution)/shard_map/ppermute | solution.py:412
  21.4 4.4 %collective-permute-start.7 = (f32[4,40,128]{2,1,0:T(8,128)S(1)}, f32[4,40,128]{2,1,0:T(8,128)S(1)}, u32[]{:S(2)}, u32[]{:S(2)}) collective-permute-start(f32[4,40,128]{2,1,0:T(8,128)S(1)} %pad_maximum_fusion.1), channel_id=1, source_target_pairs={{0,8},{1,9},{2,10},{3,11},{4,12},{5,13},{6,14},{7,15},{8,0},{9,1},... | collective-permute-start | bytes 245768 | tf_op jit(solution)/shard_map/ppermute | solution.py:412
  25.9 14.2 %collective-permute-start.10 = (f32[16,40,128]{2,1,0:T(8,128)S(1)}, f32[16,40,128]{2,1,0:T(8,128)S(1)}, u32[]{:S(2)}, u32[]{:S(2)}) collective-permute-start(f32[16,40,128]{2,1,0:T(8,128)S(1)} %get-tuple-element.71), channel_id=1, source_target_pairs={{0,1},{1,0},{2,3},{3,2},{4,5},{5,4},{6,7},{7,6},{8,9},{9,8},{10,11... | collective-permute-start | bytes 983048 | tf_op jit(solution)/shard_map/ppermute | solution.py:412
  26.0 7.8 %collective-permute-start = (f32[2,3,64,128]{3,2,1,0:T(8,128)S(1)}, f32[2,3,64,128]{3,2,1,0:T(8,128)S(1)}, u32[]{:S(2)}, u32[]{:S(2)}) collective-permute-start(f32[2,3,64,128]{3,2,1,0:T(8,128)S(1)} %get-tuple-element.37), channel_id=1, source_target_pairs={{0,8},{8,0},{16,24},{24,16},{1,9},{9,1},{17,25},{25,17},{2,10},{10... | collective-permute-start | bytes 589832 | tf_op jit(solution)/shard_map/ppermute | solution.py:86
  26.6 11.9 %collective-permute-start.1 = (f32[2,3,64,128]{3,2,1,0:T(8,128)S(1)}, f32[2,3,64,128]{3,2,1,0:T(8,128)S(1)}, u32[]{:S(2)}, u32[]{:S(2)}) collective-permute-start(f32[2,3,64,128]{3,2,1,0:T(8,128)S(1)} %get-tuple-element.38), channel_id=1, source_target_pairs={{0,24},{8,16},{16,8},{24,0},{1,25},{9,17},{17,9},{25,1},{2,26},{10... | collective-permute-start | bytes 589832 | tf_op jit(solution)/shard_map/ppermute | solution.py:86
  38.5 1.7 %collective-permute-start.2 = (f32[2,22,3,128]{3,2,1,0:T(4,128)S(1)}, f32[2,22,3,128]{3,2,1,0:T(4,128)S(1)}, u32[]{:S(2)}, u32[]{:S(2)}) collective-permute-start(f32[2,22,3,128]{3,2,1,0:T(4,128)S(1)} %get-tuple-element.41), channel_id=1, source_target_pairs={{0,1},{1,0},{2,3},{3,2},{4,5},{5,4},{6,7},{7,6},{8,9},{9,8},{10,11... | collective-permute-start | bytes 202760 | tf_op jit(solution)/shard_map/ppermute | solution.py:86
  38.6 6.5 %collective-permute-start.3 = (f32[2,22,3,128]{3,2,1,0:T(4,128)S(1)}, f32[2,22,3,128]{3,2,1,0:T(4,128)S(1)}, u32[]{:S(2)}, u32[]{:S(2)}) collective-permute-start(f32[2,22,3,128]{3,2,1,0:T(4,128)S(1)} %get-tuple-element.42), channel_id=1, source_target_pairs={{0,7},{1,2},{2,1},{3,4},{4,3},{5,6},{6,5},{7,0},{8,15},{9,10},{10,... | collective-permute-start | bytes 202760 | tf_op jit(solution)/shard_map/ppermute | solution.py:86
  67.0 2.1 %collective-permute-start.15 = (f32[16,40,128]{2,1,0:T(8,128)S(1)}, f32[16,40,128]{2,1,0:T(8,128)S(1)}, u32[]{:S(2)}, u32[]{:S(2)}) collective-permute-start(f32[16,40,128]{2,1,0:T(8,128)S(1)} %pad_maximum_fusion), channel_id=1, source_target_pairs={{0,1},{1,0},{2,3},{3,2},{4,5},{5,4},{6,7},{7,6},{8,9},{9,8},{10,11... | collective-permute-start | bytes 983048 | tf_op jit(solution)/shard_map/ppermute | solution.py:412
  67.1 7.8 %collective-permute-start.11 = (f32[2,3,64,128]{3,2,1,0:T(8,128)S(1)}, f32[2,3,64,128]{3,2,1,0:T(8,128)S(1)}, u32[]{:S(2)}, u32[]{:S(2)}) collective-permute-start(f32[2,3,64,128]{3,2,1,0:T(8,128)S(1)} %get-tuple-element.45), channel_id=1, source_target_pairs={{0,8},{8,0},{16,24},{24,16},{1,9},{9,1},{17,25},{25,17},{2,10},{10... | collective-permute-start | bytes 589832 | tf_op jit(solution)/shard_map/ppermute | solution.py:86
  67.7 11.4 %collective-permute-start.12 = (f32[2,3,64,128]{3,2,1,0:T(8,128)S(1)}, f32[2,3,64,128]{3,2,1,0:T(8,128)S(1)}, u32[]{:S(2)}, u32[]{:S(2)}) collective-permute-start(f32[2,3,64,128]{3,2,1,0:T(8,128)S(1)} %get-tuple-element.46), channel_id=1, source_target_pairs={{0,24},{8,16},{16,8},{24,0},{1,25},{9,17},{17,9},{25,1},{2,26},{10... | collective-permute-start | bytes 589832 | tf_op jit(solution)/shard_map/ppermute | solution.py:86
  69.2 11.7 %collective-permute-start.16 = (f32[4,40,128]{2,1,0:T(8,128)S(1)}, f32[4,40,128]{2,1,0:T(8,128)S(1)}, u32[]{:S(2)}, u32[]{:S(2)}) collective-permute-start(f32[4,40,128]{2,1,0:T(8,128)S(1)} %get-tuple-element.64), channel_id=1, source_target_pairs={{0,8},{1,9},{2,10},{3,11},{4,12},{5,13},{6,14},{7,15},{8,0},{9,1},... | collective-permute-start | bytes 245768 | tf_op jit(solution)/shard_map/ppermute | solution.py:412
  69.8 12.3 %collective-permute-start.18 = (f32[4,40,128]{2,1,0:T(8,128)S(1)}, f32[4,40,128]{2,1,0:T(8,128)S(1)}, u32[]{:S(2)}, u32[]{:S(2)}) collective-permute-start(f32[4,40,128]{2,1,0:T(8,128)S(1)} %get-tuple-element.65), channel_id=1, source_target_pairs={{0,24},{1,25},{2,26},{3,27},{4,28},{5,29},{6,30},{7,31},{8,16},{9,... | collective-permute-start | bytes 245768 | tf_op jit(solution)/shard_map/ppermute | solution.py:412
  72.3 9.9 %collective-permute-start.17 = (f32[4,40,128]{2,1,0:T(8,128)S(1)}, f32[4,40,128]{2,1,0:T(8,128)S(1)}, u32[]{:S(2)}, u32[]{:S(2)}) collective-permute-start(f32[4,40,128]{2,1,0:T(8,128)S(1)} %get-tuple-element.66), channel_id=1, source_target_pairs={{0,16},{1,17},{2,18},{3,19},{4,20},{5,21},{6,22},{7,23},{8,24},{9,... | collective-permute-start | bytes 245768 | tf_op jit(solution)/shard_map/ppermute | solution.py:412
  79.1 7.5 %collective-permute-start.13 = (f32[2,22,3,128]{3,2,1,0:T(4,128)S(1)}, f32[2,22,3,128]{3,2,1,0:T(4,128)S(1)}, u32[]{:S(2)}, u32[]{:S(2)}) collective-permute-start(f32[2,22,3,128]{3,2,1,0:T(4,128)S(1)} %get-tuple-element.49), channel_id=1, source_target_pairs={{0,1},{1,0},{2,3},{3,2},{4,5},{5,4},{6,7},{7,6},{8,9},{9,8},{10,11... | collective-permute-start | bytes 202760 | tf_op jit(solution)/shard_map/ppermute | solution.py:86
  79.2 7.4 %collective-permute-start.14 = (f32[2,22,3,128]{3,2,1,0:T(4,128)S(1)}, f32[2,22,3,128]{3,2,1,0:T(4,128)S(1)}, u32[]{:S(2)}, u32[]{:S(2)}) collective-permute-start(f32[2,22,3,128]{3,2,1,0:T(4,128)S(1)} %get-tuple-element.50), channel_id=1, source_target_pairs={{0,7},{1,2},{2,1},{3,4},{4,3},{5,6},{6,5},{7,0},{8,15},{9,10},{10,... | collective-permute-start | bytes 202760 | tf_op jit(solution)/shard_map/ppermute | solution.py:86
  82.2 9.0 %collective-permute-start.21 = (f32[1,40,128]{2,1,0:T(8,128)S(1)}, f32[1,40,128]{2,1,0:T(8,128)S(1)}, u32[]{:S(2)}, u32[]{:S(2)}) collective-permute-start(f32[1,40,128]{2,1,0:T(8,128)S(1)} %get-tuple-element.67), channel_id=1, source_target_pairs={{0,6},{1,7},{2,4},{3,5},{4,2},{5,3},{6,0},{7,1},{8,14},{9,15},{10,... | collective-permute-start | bytes 61448 | tf_op jit(solution)/shard_map/ppermute | solution.py:412
  83.0 8.2 %collective-permute-start.20 = (f32[1,40,128]{2,1,0:T(8,128)S(1)}, f32[1,40,128]{2,1,0:T(8,128)S(1)}, u32[]{:S(2)}, u32[]{:S(2)}) collective-permute-start(f32[1,40,128]{2,1,0:T(8,128)S(1)} %get-tuple-element.68), channel_id=1, source_target_pairs={{0,4},{1,5},{2,6},{3,7},{4,0},{5,1},{6,2},{7,3},{8,12},{9,13},{10,... | collective-permute-start | bytes 61448 | tf_op jit(solution)/shard_map/ppermute | solution.py:412
  83.0 8.2 %collective-permute-start.19 = (f32[1,40,128]{2,1,0:T(8,128)S(1)}, f32[1,40,128]{2,1,0:T(8,128)S(1)}, u32[]{:S(2)}, u32[]{:S(2)}) collective-permute-start(f32[1,40,128]{2,1,0:T(8,128)S(1)} %get-tuple-element.69), channel_id=1, source_target_pairs={{0,2},{1,3},{2,0},{3,1},{4,6},{5,7},{6,4},{7,5},{8,10},{9,11},{10,... | collective-permute-start | bytes 61448 | tf_op jit(solution)/shard_map/ppermute | solution.py:412
  (10 other events, 7.3 us)

commit v3 on v2

--- a/solution.py
+++ b/solution.py
@@ -37,7 +37,7 @@
         body,
         out_shape=outs,
         scratch_shapes=list(scratch),
-        compiler_params=pltpu.CompilerParams(vmem_limit_bytes=limit * 1024 * 1024),
+        compiler_params=pltpu.CompilerParams(vmem_limit_bytes=limit and limit * 1024 * 1024),
         **more,
         cost_estimate=pl.CostEstimate(flops=flops, bytes_accessed=size, transcendentals=0),
     )
@@ -128,7 +128,7 @@
     col_b[...] = jnp.where(even_c, first, last)
 
 
-def sides_body(ms, edge_a, edge_b, got_a, got_b, out_a, out_b):
+def with_corners(ms, edge_a, edge_b, got_a, got_b, out_a, out_b):
     batch, rows, m, C = edge_a.shape
     cols = got_a.shape[2]
     even_r, true_r = side(ms, "row")
@@ -143,6 +143,35 @@
         last, first = x[:, :, cols - m :], x[:, :, 0:m]
         out_a[:, pl.ds(at, m)] = jnp.where(even_c, last, first)
         out_b[:, pl.ds(at, m)] = jnp.where(even_c, first, last)
+
+
+def lay_out(parts, out):
+    n = 0
+    for part in parts:
+        out[n : n + part.shape[0]] = part[...]
+        n += part.shape[0]
+
+
+def first_join_body(ms, edge_a, edge_b, got_a, got_b, *refs):
+    parts, (slots, out_a, out_b) = refs[:-3], refs[-3:]
+    lay_out(parts, slots)
+    with_corners(ms, edge_a, edge_b, got_a, got_b, out_a, out_b)
+
+
+def join_body(waits, *refs):
+    lay_out(refs[waits:-1], refs[-1])
+
+
+def back_join_body(ms, edge_a, edge_b, got_a, got_b, large, large_got, small, small_got, *refs):
+    out_a, out_b = refs[-2:]
+    rows = large.shape[1]
+    n = 0
+    for out in refs[:-2]:
+        count = out.shape[0]
+        out[:, 0:rows] = large[n : n + count] + large_got[n : n + count]
+        out[:, rows:] = small[n : n + count] + small_got[n : n + count]
+        n += count
+    with_corners(ms, edge_a, edge_b, got_a, got_b, out_a, out_b)
 
 
 def depthwise_block(read, weight, rows, taps_i, taps_j, start):
@@ -463,26 +492,31 @@
             pltpu.SemaphoreType.DMA((13,)),
         ),
         size=10**6,
-        in_specs=[pl.BlockSpec(memory_space=pltpu.HBM)] * 10,
+        limit=None,
+        in_specs=[pl.BlockSpec(memory_space=pl.ANY)] * 10,
     )(features, conv_kernel.transpose(0, 2, 1), *vectors, w_in.T, in_bias.reshape(1, hs), w_out)
 
-    def sides(edge_a, edge_b, got_a, got_b):
-        out = call(
-            functools.partial(sides_body, ms),
-            tuple(shape(batch, rows + 2 * m, m, C) for _ in range(2)),
-            size=10**6,
-        )(edge_a, edge_b, got_a, got_b)
-        return both_pairs(*out, "col")
-
+    edges = tuple(shape(batch, rows + 2 * m, m, C) for _ in range(2))
+    anywhere, in_vmem = pl.BlockSpec(memory_space=pl.ANY), pl.BlockSpec(memory_space=pltpu.VMEM)
+    groups = groups_of(ms)
+    order = [0]
     got_ra, got_rb = both_pairs(row_a, row_b, "row")
     slots = block[None]
-    groups = groups_of(ms)
-    order = [0]
-    for group in groups:
+    for n, group in enumerate(groups):
+        parts = [slots] + [flip(slots, mask, count) for mask in masks(group)[1:]]
         order = [mask ^ x for mask in masks(group) for x in order]
-        slots = jnp.concatenate([slots] + [flip(slots, mask, count) for mask in masks(group)[1:]])
-
-    got_ca, got_cb = sides(col_a, col_b, got_ra, got_rb)
+        slots = shape(len(order), slot, LANES)
+        if n == 0:
+            slots, edge_a, edge_b = call(functools.partial(first_join_body, ms), (slots, *edges))(
+                col_a, col_b, got_ra, got_rb, *parts
+            )
+            got_ca, got_cb = both_pairs(edge_a, edge_b, "col")
+        else:
+            waits = (got_ca, got_cb) if n == 1 else ()
+            slots = call(
+                functools.partial(join_body, len(waits)), slots,
+                in_specs=[anywhere] * len(waits) + [in_vmem] * len(parts),
+            )(*waits, *parts)
     tile = 4 * cols
     src, dconv, d_row_a, d_row_b, d_col_a, d_col_b, grads, chan, small = call(
         functools.partial(mix_body, ms, order, factor, taps_i, taps_j, tile),
@@ -519,6 +553,9 @@
     )(features, got_ra, got_rb, got_ca, got_cb, slots, cotangent)
 
     d_got_ra, d_got_rb = both_pairs(d_row_a, d_row_b, "row")
+    last = groups[-1][0]
+    half = count // 2
+    large_got = flip(grads[half:], last, count)
     smalls = call(
         functools.partial(kernel_grad_body, ms, order, factor, taps_i, taps_j, count),
         shape(count, 8, LANES),
@@ -526,18 +563,22 @@
         flops=4 * 10**9,
         size=4 * 10**6,
     )(src, dconv, chan)
-
-    d_got_ca, d_got_cb = sides(d_col_a, d_col_b, d_got_ra, d_got_rb)
-
-    parts = [jnp.concatenate([grads, smalls], axis=1)]
-    for group in groups[::-1]:
-        whole = parts[0]
-        for part in parts[1:]:
-            whole = whole + part
-        order = masks(group)
-        step = whole.shape[0] // len(order)
-        parts = [whole[:step]]
-        parts += [flip(whole[k * step : (k + 1) * step], mask, count) for k, mask in enumerate(order) if k]
+    small_got = flip(smalls[half:], last, count)
+    ways = len(masks(groups[-2]))
+    *parts, edge_a, edge_b = call(
+        functools.partial(back_join_body, ms),
+        (*(shape(half // ways, slot, LANES) for _ in range(ways)), *edges),
+    )(d_col_a, d_col_b, d_got_ra, d_got_rb, grads, large_got, smalls, small_got)
+    d_got_ca, d_got_cb = both_pairs(edge_a, edge_b, "col")
+    for n, group in reversed(list(enumerate(groups[:-1]))):
+        parts = [parts[0]] + [flip(part, mask, count) for part, mask in zip(parts[1:], masks(group)[1:])]
+        if n:
+            whole = parts[0]
+            for part in parts[1:]:
+                whole = whole + part
+            ways = len(masks(groups[n - 1]))
+            step = whole.shape[0] // ways
+            parts = [whole[k * step : (k + 1) * step] for k in range(ways)]
 
     features_grad = call(
         functools.partial(features_grad_body, ms, taps_i, taps_j),

time: 92.4 us -> 76.6 us (0.83)
  waiting for transfers between devices: 30.3 us -> 12.9 us
  starting transfers between devices: 25.5 us -> 30.6 us
  local copies, waits for them, and re-layouts: 7.36 us -> 2.45 us
  Pallas kernels: 27.9 us -> 29.6 us
    ppermute x4, waiting for transfers between devices: 13.8 us -> 5.02 us  [both_pairs(): lax.ppermute(b, axis, pairs(count, True))]
    ppermute x4, waiting for transfers between devices: 6.83 us -> 0.01 us  [both_pairs(): lax.ppermute(a, axis, pairs(count, False))]
    unnamed x30 -> x10, local copies, waits for them, and re-layouts: 7.3 us -> 2.41 us
    ppermute x4, starting transfers between devices: 1.35 us -> 4.57 us  [both_pairs(): lax.ppermute(a, axis, pairs(count, False))]
    ppermute x4, starting transfers between devices: 6.71 us -> 9.33 us  [both_pairs(): lax.ppermute(b, axis, pairs(count, True))]
    ppermute x14 -> x15, waiting for transfers between devices: 9.6 us -> 7.85 us  [flip(): return lax.ppermute(x, AXES, [(i, i ^ mask) for i in range(count)])]
    pallas_call x1, Pallas kernels: 0.62 us -> 2.25 us  [per_device(): call(functools.partial(start_body, ms), (shape(slot, LANES), *(shape(batc...]
    ppermute x14 -> x15, starting transfers between devices: 17.5 us -> 16.7 us  [flip(): return lax.ppermute(x, AXES, [(i, i ^ mask) for i in range(count)])]
  transfers between devices with their start and end apart: 22 -> 23, of which waited for: 10 -> 8; matrix products, arithmetic and copies ran while one was open for 0% -> 0% of each run, Pallas kernels for 5% -> 13%
where the time goes in v3:
time: 76.6 us; the launch traced here: 76.3 us
  starting transfers between devices  30.6 us (40%)
  Pallas kernels  29.6 us (39%)
  waiting for transfers between devices  12.9 us (17%)
  local copies, waits for them, and re-layouts  2.45 us (3%)
  between operations  0.77 us (1%)
    ppermute x15, starting transfers between devices, flip(): return lax.ppermute(x, AXES, [(i, i ^ mask) for i in range(count)])  16.7 us
    pallas_call x1, Pallas kernels, per_device(): call(functools.partial(mix_body, ms, order, factor, taps_i, taps_j, tile)...  16.4 us
    ppermute x4, starting transfers between devices, both_pairs(): lax.ppermute(b, axis, pairs(count, True))  9.33 us
    ppermute x15, waiting for transfers between devices, flip(): return lax.ppermute(x, AXES, [(i, i ^ mask) for i in range(count)])  7.85 us
    pallas_call x1, Pallas kernels, per_device(): call(functools.partial(kernel_grad_body, ms, order, factor, taps_i, taps_...  5.53 us
    ppermute x4, waiting for transfers between devices, both_pairs(): lax.ppermute(b, axis, pairs(count, True))  5.02 us
    ppermute x4, starting transfers between devices, both_pairs(): lax.ppermute(a, axis, pairs(count, False))  4.57 us
    pallas_call x1, Pallas kernels, per_device(): call(functools.partial(features_grad_body, ms, taps_i, taps_j), shape(bat...  4.55 us
  transfers between devices with their start and end apart: 23, of which 8 were waited for; matrix products, arithmetic and copies ran while one was open for 0% of the time, Pallas kernels for 13%

profile of v3, /device:TPU:0, one launch (start us, length us, event | category | flops | bytes accessed | tf_op | source)
XLA Modules:
  0.0 76.3 jit_solution(14756733750967912845)
XLA Ops:
  0.7 2.3 %shard_map.186 = (f32[40,128]{1,0:T(8,128)}, f32[2,3,64,128]{3,2,1,0:T(8,128)}, f32[2,3,64,128]{3,2,1,0:T(8,128)}, f32[2,16,3,128]{3,2,1,0:T(4,128)}, f32[2,16,3,128]{3,2,1,0:T(4,128)}) custom-call(f32[2,16,64,128]{3,2,1,0:T(8,128)} %feat.3, f32[7,4,7]{2,1,0:T(4,128)} %bitcast.29, f32[1,4]{1,0:T(1,128)} %bitcast.31, f32[1,4]{1,0:T(1,128)} %bitcast.32, ...), custom_call_target="tpu_custom_call" | custom-call | bytes 1000000 | tf_op jit(solution)/shard_map/pallas_call | solution.py:477
  2.9 3.0 %collective-permute-start = (f32[2,3,64,128]{3,2,1,0:T(8,128)}, f32[2,3,64,128]{3,2,1,0:T(8,128)S(1)}, u32[]{:S(2)}, u32[]{:S(2)}) collective-permute-start(f32[2,3,64,128]{3,2,1,0:T(8,128)} %get-tuple-element.42), channel_id=1, source_target_pairs={{0,8},{8,0},{16,24},{24,16},{1,9},{9,1},{17,25},{25,17},{2,10},{10... | collective-permute-start | bytes 589832 | tf_op jit(solution)/shard_map/ppermute | solution.py:86
  5.9 1.5 %collective-permute-start.1 = (f32[2,3,64,128]{3,2,1,0:T(8,128)}, f32[2,3,64,128]{3,2,1,0:T(8,128)S(1)}, u32[]{:S(2)}, u32[]{:S(2)}) collective-permute-start(f32[2,3,64,128]{3,2,1,0:T(8,128)} %get-tuple-element.43), channel_id=1, source_target_pairs={{0,24},{8,16},{16,8},{24,0},{1,25},{9,17},{17,9},{25,1},{2,26},{10... | collective-permute-start | bytes 589832 | tf_op jit(solution)/shard_map/ppermute | solution.py:86
  7.4 3.6 %collective-permute-start.4 = (f32[1,40,128]{2,1,0:T(8,128)}, f32[1,40,128]{2,1,0:T(8,128)S(1)}, u32[]{:S(2)}, u32[]{:S(2)}) collective-permute-start(f32[1,40,128]{2,1,0:T(8,128)} %bitcast.22), channel_id=1, source_target_pairs={{0,6},{1,7},{2,4},{3,5},{4,2},{5,3},{6,0},{7,1},{8,14},{9,15},{10,... | collective-permute-start | bytes 61448 | tf_op jit(solution)/shard_map/ppermute | solution.py:441
  11.8 1.5 %collective-permute-done.4.refs_3_ = f32[1,40,128]{2,1,0:T(8,128)S(1)} collective-permute-done((f32[1,40,128]{2,1,0:T(8,128)}, f32[1,40,128]{2,1,0:T(8,128)S(1)}, u32[]{:S(2)}, u32[]{:S(2)}) %collective-permute-start.4) | collective-permute-done | bytes 20512 | tf_op jit(solution)/shard_map/ppermute | solution.py:441
  13.3 2.7 %collective-permute-done.3.refs_2_ = f32[1,40,128]{2,1,0:T(8,128)S(1)} collective-permute-done((f32[1,40,128]{2,1,0:T(8,128)}, f32[1,40,128]{2,1,0:T(8,128)S(1)}, u32[]{:S(2)}, u32[]{:S(2)}) %collective-permute-start.3) | collective-permute-done | bytes 20512 | tf_op jit(solution)/shard_map/ppermute | solution.py:441
  16.5 0.8 %copy-done.1 = f32[2,16,3,128]{3,2,1,0:T(4,128)S(1)} copy-done((f32[2,16,3,128]{3,2,1,0:T(4,128)S(1)}, f32[2,16,3,128]{3,2,1,0:T(4,128)}, u32[]{:S(2)}) %copy-start.1) | copy-done | bytes 49176
  18.9 1.5 %collective-permute-start.9 = (f32[4,40,128]{2,1,0:T(8,128)S(1)}, f32[4,40,128]{2,1,0:T(8,128)S(1)}, u32[]{:S(2)}, u32[]{:S(2)}) collective-permute-start(f32[4,40,128]{2,1,0:T(8,128)S(1)} %get-tuple-element.49.refs_2_), channel_id=1, source_target_pairs={{0,24},{1,25},{2,26},{3,27},{4,28},{5,29},{6,30},{7,31},{8,16},{9,... | collective-permute-start | bytes 245768 | tf_op jit(solution)/shard_map/ppermute | solution.py:441
  20.4 1.5 %collective-permute-start.8 = (f32[4,40,128]{2,1,0:T(8,128)S(1)}, f32[4,40,128]{2,1,0:T(8,128)S(1)}, u32[]{:S(2)}, u32[]{:S(2)}) collective-permute-start(f32[4,40,128]{2,1,0:T(8,128)S(1)} %get-tuple-element.49.refs_2_), channel_id=1, source_target_pairs={{0,16},{1,17},{2,18},{3,19},{4,20},{5,21},{6,22},{7,23},{8,24},{9,... | collective-permute-start | bytes 245768 | tf_op jit(solution)/shard_map/ppermute | solution.py:441
  22.5 3.7 %collective-permute-start.6 = (f32[2,22,3,128]{3,2,1,0:T(4,128)S(1)}, f32[2,22,3,128]{3,2,1,0:T(4,128)S(1)}, u32[]{:S(2)}, u32[]{:S(2)}) collective-permute-start(f32[2,22,3,128]{3,2,1,0:T(4,128)S(1)} %get-tuple-element.48), channel_id=1, source_target_pairs={{0,7},{1,2},{2,1},{3,4},{4,3},{5,6},{6,5},{7,0},{8,15},{9,10},{10,... | collective-permute-start | bytes 202760 | tf_op jit(solution)/shard_map/ppermute | solution.py:86
  26.2 2.5 %collective-permute-done.6.refs_1_.got_cb = f32[2,22,3,128]{3,2,1,0:T(4,128)S(1)} collective-permute-done((f32[2,22,3,128]{3,2,1,0:T(4,128)S(1)}, f32[2,22,3,128]{3,2,1,0:T(4,128)S(1)}, u32[]{:S(2)}, u32[]{:S(2)}) %collective-permute-start.6) | collective-permute-done | bytes 67616 | tf_op jit(solution)/shard_map/ppermute | solution.py:86
  28.8 1.6 %collective-permute-done.10.refs_1_ = f32[16,40,128]{2,1,0:T(8,128)S(1)} collective-permute-done((f32[16,40,128]{2,1,0:T(8,128)S(1)}, f32[16,40,128]{2,1,0:T(8,128)S(1)}, u32[]{:S(2)}, u32[]{:S(2)}) %collective-permute-start.10) | collective-permute-done | bytes 327712 | tf_op jit(solution)/shard_map/ppermute | solution.py:441
  30.5 16.4 %shard_map.190 = (f32[2,22,80,128]{3,2,1,0:T(8,128)S(1)}, f32[2,16,64,128]{3,2,1,0:T(8,128)S(1)}, f32[2,3,64,128]{3,2,1,0:T(8,128)S(1)}, f32[2,3,64,128]{3,2,1,0...) custom-call(f32[2,16,64,128]{3,2,1,0:T(8,128)S(1)} %copy-done, ...), custom_call_target="tpu_custom_call" | custom-call | flops 12000000000 | bytes 8000000 | tf_op jit(solution)/shard_map/pallas_call | solution.py:521
  46.9 1.6 %collective-permute-start.11 = (f32[2,3,64,128]{3,2,1,0:T(8,128)S(1)}, f32[2,3,64,128]{3,2,1,0:T(8,128)S(1)}, u32[]{:S(2)}, u32[]{:S(2)}) collective-permute-start(f32[2,3,64,128]{3,2,1,0:T(8,128)S(1)} %get-tuple-element.51), channel_id=1, source_target_pairs={{0,8},{8,0},{16,24},{24,16},{1,9},{9,1},{17,25},{25,17},{2,10},{10... | collective-permute-start | bytes 589832 | tf_op jit(solution)/shard_map/ppermute | solution.py:86
  49.0 5.5 %shard_map.191.small = f32[32,8,128]{2,1,0:T(8,128)S(1)} custom-call(f32[2,22,80,128]{3,2,1,0:T(8,128)S(1)} %get-tuple-element.56.src_ref, f32[2,16,64,128]{3,2,1,0:T(8,128)S(1)} %get-tuple-element.50.dconv_ref.inner, f32[8,512]{1,0:T(8,128)S(1)} %get-tuple-element.57.chan_ref), custom_call_target="tpu_custom_call" | custom-call | flops 4000000000 | bytes 4000000 | tf_op jit(solution)/shard_map/pallas_call | solution.py:559
  55.1 0.9 %collective-permute-done.14.small_got = f32[16,8,128]{2,1,0:T(8,128)S(1)} collective-permute-done((f32[16,8,128]{2,1,0:T(8,128)S(1)}, f32[16,8,128]{2,1,0:T(8,128)S(1)}, u32[]{:S(2)}, u32[]{:S(2)}) %collective-permute-start.14) | collective-permute-done | bytes 65568 | tf_op jit(solution)/shard_map/ppermute | solution.py:441
  56.0 2.0 %collective-permute-done.12.got_b.got_rb = f32[2,3,64,128]{3,2,1,0:T(8,128)S(1)} collective-permute-done((f32[2,3,64,128]{3,2,1,0:T(8,128)S(1)}, f32[2,3,64,128]{3,2,1,0:T(8,128)S(1)}, u32[]{:S(2)}, u32[]{:S(2)}) %collective-permute-start.12) | collective-permute-done | bytes 196640 | tf_op jit(solution)/shard_map/ppermute | solution.py:86
  58.1 1.6 %collective-permute-start.17 = (f32[4,40,128]{2,1,0:T(8,128)S(1)}, f32[4,40,128]{2,1,0:T(8,128)S(1)}, u32[]{:S(2)}, u32[]{:S(2)}) collective-permute-start(f32[4,40,128]{2,1,0:T(8,128)S(1)} %get-tuple-element.62), channel_id=1, source_target_pairs={{0,8},{1,9},{2,10},{3,11},{4,12},{5,13},{6,14},{7,15},{8,0},{9,1},... | collective-permute-start | bytes 245768 | tf_op jit(solution)/shard_map/ppermute | solution.py:441
  59.6 1.5 %collective-permute-start.18 = (f32[4,40,128]{2,1,0:T(8,128)S(1)}, f32[4,40,128]{2,1,0:T(8,128)S(1)}, u32[]{:S(2)}, u32[]{:S(2)}) collective-permute-start(f32[4,40,128]{2,1,0:T(8,128)S(1)} %get-tuple-element.63), channel_id=1, source_target_pairs={{0,16},{1,17},{2,18},{3,19},{4,20},{5,21},{6,22},{7,23},{8,24},{9,... | collective-permute-start | bytes 245768 | tf_op jit(solution)/shard_map/ppermute | solution.py:441
  61.6 3.6 %collective-permute-start.16 = (f32[2,22,3,128]{3,2,1,0:T(4,128)S(1)}, f32[2,22,3,128]{3,2,1,0:T(4,128)S(1)}, u32[]{:S(2)}, u32[]{:S(2)}) collective-permute-start(f32[2,22,3,128]{3,2,1,0:T(4,128)S(1)} %get-tuple-element.59), channel_id=1, source_target_pairs={{0,7},{1,2},{2,1},{3,4},{4,3},{5,6},{6,5},{7,0},{8,15},{9,10},{10,... | collective-permute-start | bytes 202760 | tf_op jit(solution)/shard_map/ppermute | solution.py:86
  65.3 1.2 %collective-permute-done.19 = f32[4,40,128]{2,1,0:T(8,128)S(1)} collective-permute-done((f32[4,40,128]{2,1,0:T(8,128)S(1)}, f32[4,40,128]{2,1,0:T(8,128)S(1)}, u32[]{:S(2)}, u32[]{:S(2)}) %collective-permute-start.19) | collective-permute-done | bytes 81952 | tf_op jit(solution)/shard_map/ppermute | solution.py:441
  66.5 3.6 %collective-permute-start.22 = (f32[1,40,128]{2,1,0:T(8,128)S(1)}, f32[1,40,128]{2,1,0:T(8,128)S(1)}, u32[]{:S(2)}, u32[]{:S(2)}) collective-permute-start(f32[1,40,128]{2,1,0:T(8,128)S(1)} %get-tuple-element.74), channel_id=1, source_target_pairs={{0,6},{1,7},{2,4},{3,5},{4,2},{5,3},{6,0},{7,1},{8,14},{9,15},{10,... | collective-permute-start | bytes 61448 | tf_op jit(solution)/shard_map/ppermute | solution.py:441
  70.2 0.8 %collective-permute-start.20 = (f32[1,40,128]{2,1,0:T(8,128)S(1)}, f32[1,40,128]{2,1,0:T(8,128)S(1)}, u32[]{:S(2)}, u32[]{:S(2)}) collective-permute-start(f32[1,40,128]{2,1,0:T(8,128)S(1)} %get-tuple-element.76), channel_id=1, source_target_pairs={{0,2},{1,3},{2,0},{3,1},{4,6},{5,7},{6,4},{7,5},{8,10},{9,11},{10,... | collective-permute-start | bytes 61448 | tf_op jit(solution)/shard_map/ppermute | solution.py:441
  71.0 4.5 %shard_map.193 = f32[2,16,64,128]{3,2,1,0:T(8,128)} custom-call(f32[2,16,64,128]{3,2,1,0:T(8,128)S(1)} %get-tuple-element.50.dconv_ref.inner, f32[2,3,64,128]{3,2,1,0:T(8,128)S(1)} %collective-permute-done.11.got_a.got_ra, f32[2,3,64,128]{3,2,1,0:T(8,128)S(1)} %collective-permute-done.12.got_b.got_rb, f32[2,22,3,128]{3,2,1,0:T(4,128)S(1)} %collective-permute-done.15.got_ca, ...), custom_call_target="tpu_custom_call" | custom-call | flops 4000000000 | bytes 4000000 | tf_op jit(solution)/shard_map/pallas_call | solution.py:583
  (45 shorter events, 6.1 us)
Async XLA Ops:
  0.6 29.8 %copy-start = (f32[2,16,64,128]{3,2,1,0:T(8,128)S(1)}, f32[2,16,64,128]{3,2,1,0:T(8,128)}, u32[]{:S(2)}) copy-start(f32[2,16,64,128]{3,2,1,0:T(8,128)} %feat.3) | copy-start | bytes 3145732
  2.9 13.0 %collective-permute-start = (f32[2,3,64,128]{3,2,1,0:T(8,128)}, f32[2,3,64,128]{3,2,1,0:T(8,128)S(1)}, u32[]{:S(2)}, u32[]{:S(2)}) collective-permute-start(f32[2,3,64,128]{3,2,1,0:T(8,128)} %get-tuple-element.42), channel_id=1, source_target_pairs={{0,8},{8,0},{16,24},{24,16},{1,9},{9,1},{17,25},{25,17},{2,10},{10... | collective-permute-start | bytes 589832 | tf_op jit(solution)/shard_map/ppermute | solution.py:86
  5.9 10.5 %collective-permute-start.1 = (f32[2,3,64,128]{3,2,1,0:T(8,128)}, f32[2,3,64,128]{3,2,1,0:T(8,128)S(1)}, u32[]{:S(2)}, u32[]{:S(2)}) collective-permute-start(f32[2,3,64,128]{3,2,1,0:T(8,128)} %get-tuple-element.43), channel_id=1, source_target_pairs={{0,24},{8,16},{16,8},{24,0},{1,25},{9,17},{17,9},{25,1},{2,26},{10... | collective-permute-start | bytes 589832 | tf_op jit(solution)/shard_map/ppermute | solution.py:86
  7.4 5.8 %collective-permute-start.4 = (f32[1,40,128]{2,1,0:T(8,128)}, f32[1,40,128]{2,1,0:T(8,128)S(1)}, u32[]{:S(2)}, u32[]{:S(2)}) collective-permute-start(f32[1,40,128]{2,1,0:T(8,128)} %bitcast.22), channel_id=1, source_target_pairs={{0,6},{1,7},{2,4},{3,5},{4,2},{5,3},{6,0},{7,1},{8,14},{9,15},{10,... | collective-permute-start | bytes 61448 | tf_op jit(solution)/shard_map/ppermute | solution.py:441
  11.0 4.9 %collective-permute-start.3 = (f32[1,40,128]{2,1,0:T(8,128)}, f32[1,40,128]{2,1,0:T(8,128)S(1)}, u32[]{:S(2)}, u32[]{:S(2)}) collective-permute-start(f32[1,40,128]{2,1,0:T(8,128)} %bitcast.23), channel_id=1, source_target_pairs={{0,4},{1,5},{2,6},{3,7},{4,0},{5,1},{6,2},{7,3},{8,12},{9,13},{10,... | collective-permute-start | bytes 61448 | tf_op jit(solution)/shard_map/ppermute | solution.py:441
  11.0 4.9 %collective-permute-start.2 = (f32[1,40,128]{2,1,0:T(8,128)}, f32[1,40,128]{2,1,0:T(8,128)S(1)}, u32[]{:S(2)}, u32[]{:S(2)}) collective-permute-start(f32[1,40,128]{2,1,0:T(8,128)} %bitcast.24), channel_id=1, source_target_pairs={{0,2},{1,3},{2,0},{3,1},{4,6},{5,7},{6,4},{7,5},{8,10},{9,11},{10,... | collective-permute-start | bytes 61448 | tf_op jit(solution)/shard_map/ppermute | solution.py:441
  18.9 9.7 %collective-permute-start.9 = (f32[4,40,128]{2,1,0:T(8,128)S(1)}, f32[4,40,128]{2,1,0:T(8,128)S(1)}, u32[]{:S(2)}, u32[]{:S(2)}) collective-permute-start(f32[4,40,128]{2,1,0:T(8,128)S(1)} %get-tuple-element.49.refs_2_), channel_id=1, source_target_pairs={{0,24},{1,25},{2,26},{3,27},{4,28},{5,29},{6,30},{7,31},{8,16},{9,... | collective-permute-start | bytes 245768 | tf_op jit(solution)/shard_map/ppermute | solution.py:441
  20.4 8.3 %collective-permute-start.8 = (f32[4,40,128]{2,1,0:T(8,128)S(1)}, f32[4,40,128]{2,1,0:T(8,128)S(1)}, u32[]{:S(2)}, u32[]{:S(2)}) collective-permute-start(f32[4,40,128]{2,1,0:T(8,128)S(1)} %get-tuple-element.49.refs_2_), channel_id=1, source_target_pairs={{0,16},{1,17},{2,18},{3,19},{4,20},{5,21},{6,22},{7,23},{8,24},{9,... | collective-permute-start | bytes 245768 | tf_op jit(solution)/shard_map/ppermute | solution.py:441
  21.9 6.7 %collective-permute-start.7 = (f32[4,40,128]{2,1,0:T(8,128)S(1)}, f32[4,40,128]{2,1,0:T(8,128)S(1)}, u32[]{:S(2)}, u32[]{:S(2)}) collective-permute-start(f32[4,40,128]{2,1,0:T(8,128)S(1)} %get-tuple-element.49.refs_2_), channel_id=1, source_target_pairs={{0,8},{1,9},{2,10},{3,11},{4,12},{5,13},{6,14},{7,15},{8,0},{9,1},... | collective-permute-start | bytes 245768 | tf_op jit(solution)/shard_map/ppermute | solution.py:441
  22.5 3.7 %collective-permute-start.5 = (f32[2,22,3,128]{3,2,1,0:T(4,128)S(1)}, f32[2,22,3,128]{3,2,1,0:T(4,128)S(1)}, u32[]{:S(2)}, u32[]{:S(2)}) collective-permute-start(f32[2,22,3,128]{3,2,1,0:T(4,128)S(1)} %get-tuple-element.47), channel_id=1, source_target_pairs={{0,1},{1,0},{2,3},{3,2},{4,5},{5,4},{6,7},{7,6},{8,9},{9,8},{10,11... | collective-permute-start | bytes 202760 | tf_op jit(solution)/shard_map/ppermute | solution.py:86
  22.5 6.2 %collective-permute-start.6 = (f32[2,22,3,128]{3,2,1,0:T(4,128)S(1)}, f32[2,22,3,128]{3,2,1,0:T(4,128)S(1)}, u32[]{:S(2)}, u32[]{:S(2)}) collective-permute-start(f32[2,22,3,128]{3,2,1,0:T(4,128)S(1)} %get-tuple-element.48), channel_id=1, source_target_pairs={{0,7},{1,2},{2,1},{3,4},{4,3},{5,6},{6,5},{7,0},{8,15},{9,10},{10,... | collective-permute-start | bytes 202760 | tf_op jit(solution)/shard_map/ppermute | solution.py:86
  28.7 1.7 %collective-permute-start.10 = (f32[16,40,128]{2,1,0:T(8,128)S(1)}, f32[16,40,128]{2,1,0:T(8,128)S(1)}, u32[]{:S(2)}, u32[]{:S(2)}) collective-permute-start(f32[16,40,128]{2,1,0:T(8,128)S(1)} %shard_map.188.refs_0_), channel_id=1, source_target_pairs={{0,1},{1,0},{2,3},{3,2},{4,5},{5,4},{6,7},{7,6},{8,9},{9,8},{10,11... | collective-permute-start | bytes 983048 | tf_op jit(solution)/shard_map/ppermute | solution.py:441
  46.9 9.2 %collective-permute-start.11 = (f32[2,3,64,128]{3,2,1,0:T(8,128)S(1)}, f32[2,3,64,128]{3,2,1,0:T(8,128)S(1)}, u32[]{:S(2)}, u32[]{:S(2)}) collective-permute-start(f32[2,3,64,128]{3,2,1,0:T(8,128)S(1)} %get-tuple-element.51), channel_id=1, source_target_pairs={{0,8},{8,0},{16,24},{24,16},{1,9},{9,1},{17,25},{25,17},{2,10},{10... | collective-permute-start | bytes 589832 | tf_op jit(solution)/shard_map/ppermute | solution.py:86
  48.4 9.6 %collective-permute-start.12 = (f32[2,3,64,128]{3,2,1,0:T(8,128)S(1)}, f32[2,3,64,128]{3,2,1,0:T(8,128)S(1)}, u32[]{:S(2)}, u32[]{:S(2)}) collective-permute-start(f32[2,3,64,128]{3,2,1,0:T(8,128)S(1)} %get-tuple-element.52), channel_id=1, source_target_pairs={{0,24},{8,16},{16,8},{24,0},{1,25},{9,17},{17,9},{25,1},{2,26},{10... | collective-permute-start | bytes 589832 | tf_op jit(solution)/shard_map/ppermute | solution.py:86
  48.9 9.1 %collective-permute-start.13 = (f32[16,32,128]{2,1,0:T(8,128)S(1)}, f32[16,32,128]{2,1,0:T(8,128)S(1)}, u32[]{:S(2)}, u32[]{:S(2)}) collective-permute-start(f32[16,32,128]{2,1,0:T(8,128)S(1)} %slice.18), channel_id=1, source_target_pairs={{0,1},{1,0},{2,3},{3,2},{4,5},{5,4},{6,7},{7,6},{8,9},{9,8},{10,11... | collective-permute-start | bytes 786440 | tf_op jit(solution)/shard_map/ppermute | solution.py:441
  54.5 1.5 %collective-permute-start.14 = (f32[16,8,128]{2,1,0:T(8,128)S(1)}, f32[16,8,128]{2,1,0:T(8,128)S(1)}, u32[]{:S(2)}, u32[]{:S(2)}) collective-permute-start(f32[16,8,128]{2,1,0:T(8,128)S(1)} %slice.24), channel_id=1, source_target_pairs={{0,1},{1,0},{2,3},{3,2},{4,5},{5,4},{6,7},{7,6},{8,9},{9,8},{10,11... | collective-permute-start | bytes 196616 | tf_op jit(solution)/shard_map/ppermute | solution.py:441
  58.1 7.2 %collective-permute-start.17 = (f32[4,40,128]{2,1,0:T(8,128)S(1)}, f32[4,40,128]{2,1,0:T(8,128)S(1)}, u32[]{:S(2)}, u32[]{:S(2)}) collective-permute-start(f32[4,40,128]{2,1,0:T(8,128)S(1)} %get-tuple-element.62), channel_id=1, source_target_pairs={{0,8},{1,9},{2,10},{3,11},{4,12},{5,13},{6,14},{7,15},{8,0},{9,1},... | collective-permute-start | bytes 245768 | tf_op jit(solution)/shard_map/ppermute | solution.py:441
  59.6 5.7 %collective-permute-start.18 = (f32[4,40,128]{2,1,0:T(8,128)S(1)}, f32[4,40,128]{2,1,0:T(8,128)S(1)}, u32[]{:S(2)}, u32[]{:S(2)}) collective-permute-start(f32[4,40,128]{2,1,0:T(8,128)S(1)} %get-tuple-element.63), channel_id=1, source_target_pairs={{0,16},{1,17},{2,18},{3,19},{4,20},{5,21},{6,22},{7,23},{8,24},{9,... | collective-permute-start | bytes 245768 | tf_op jit(solution)/shard_map/ppermute | solution.py:441
  61.2 5.3 %collective-permute-start.19 = (f32[4,40,128]{2,1,0:T(8,128)S(1)}, f32[4,40,128]{2,1,0:T(8,128)S(1)}, u32[]{:S(2)}, u32[]{:S(2)}) collective-permute-start(f32[4,40,128]{2,1,0:T(8,128)S(1)} %get-tuple-element.64), channel_id=1, source_target_pairs={{0,24},{1,25},{2,26},{3,27},{4,28},{5,29},{6,30},{7,31},{8,16},{9,... | collective-permute-start | bytes 245768 | tf_op jit(solution)/shard_map/ppermute | solution.py:441
  61.6 9.4 %collective-permute-start.15 = (f32[2,22,3,128]{3,2,1,0:T(4,128)S(1)}, f32[2,22,3,128]{3,2,1,0:T(4,128)S(1)}, u32[]{:S(2)}, u32[]{:S(2)}) collective-permute-start(f32[2,22,3,128]{3,2,1,0:T(4,128)S(1)} %get-tuple-element.58), channel_id=1, source_target_pairs={{0,1},{1,0},{2,3},{3,2},{4,5},{5,4},{6,7},{7,6},{8,9},{9,8},{10,11... | collective-permute-start | bytes 202760 | tf_op jit(solution)/shard_map/ppermute | solution.py:86
  61.6 9.4 %collective-permute-start.16 = (f32[2,22,3,128]{3,2,1,0:T(4,128)S(1)}, f32[2,22,3,128]{3,2,1,0:T(4,128)S(1)}, u32[]{:S(2)}, u32[]{:S(2)}) collective-permute-start(f32[2,22,3,128]{3,2,1,0:T(4,128)S(1)} %get-tuple-element.59), channel_id=1, source_target_pairs={{0,7},{1,2},{2,1},{3,4},{4,3},{5,6},{6,5},{7,0},{8,15},{9,10},{10,... | collective-permute-start | bytes 202760 | tf_op jit(solution)/shard_map/ppermute | solution.py:86
  66.5 9.0 %collective-permute-start.22 = (f32[1,40,128]{2,1,0:T(8,128)S(1)}, f32[1,40,128]{2,1,0:T(8,128)S(1)}, u32[]{:S(2)}, u32[]{:S(2)}) collective-permute-start(f32[1,40,128]{2,1,0:T(8,128)S(1)} %get-tuple-element.74), channel_id=1, source_target_pairs={{0,6},{1,7},{2,4},{3,5},{4,2},{5,3},{6,0},{7,1},{8,14},{9,15},{10,... | collective-permute-start | bytes 61448 | tf_op jit(solution)/shard_map/ppermute | solution.py:441
  70.2 5.4 %collective-permute-start.21 = (f32[1,40,128]{2,1,0:T(8,128)S(1)}, f32[1,40,128]{2,1,0:T(8,128)S(1)}, u32[]{:S(2)}, u32[]{:S(2)}) collective-permute-start(f32[1,40,128]{2,1,0:T(8,128)S(1)} %get-tuple-element.75), channel_id=1, source_target_pairs={{0,4},{1,5},{2,6},{3,7},{4,0},{5,1},{6,2},{7,3},{8,12},{9,13},{10,... | collective-permute-start | bytes 61448 | tf_op jit(solution)/shard_map/ppermute | solution.py:441
  70.2 5.4 %collective-permute-start.20 = (f32[1,40,128]{2,1,0:T(8,128)S(1)}, f32[1,40,128]{2,1,0:T(8,128)S(1)}, u32[]{:S(2)}, u32[]{:S(2)}) collective-permute-start(f32[1,40,128]{2,1,0:T(8,128)S(1)} %get-tuple-element.76), channel_id=1, source_target_pairs={{0,2},{1,3},{2,0},{3,1},{4,6},{5,7},{6,4},{7,5},{8,10},{9,11},{10,... | collective-permute-start | bytes 61448 | tf_op jit(solution)/shard_map/ppermute | solution.py:441
  (4 other events, 14.0 us)

commit v4 on v3

--- a/solution.py
+++ b/solution.py
@@ -92,22 +92,20 @@
     return even, jnp.where(even, i > 0, i < ms[axis] - 1)
 
 
-def start_body(ms, feat, kernel_hbm, cb, ng, ns, ob, ls, win_hbm, ib, wout_hbm, out_ref, row_a, row_b, col_a, col_b,
-               kernel_scr, v0, v1, v2, v3, v4, ib_scr, win_scr, wout_scr, low, high, sems):
+def start_body(ms, feat, kernel_hbm, cb, ng, ns, ob, ls, win_hbm, ib, wout_hbm, out_ref, row_a, row_b,
+               kernel_scr, v0, v1, v2, v3, v4, ib_scr, win_scr, wout_scr, sems):
     batch, rows, cols, C = feat.shape
     taps_i, cs, taps_j = kernel_hbm.shape
     hs = win_hbm.shape[0]
     taps = taps_i * taps_j
     m = taps_i // 2
     even_r, _ = side(ms, "row")
-    even_c, _ = side(ms, "col")
     far = jnp.where(even_r, rows - m, 0)
     near = jnp.where(even_r, 0, rows - m)
     vectors = (v0, v1, v2, v3, v4)
     moves = [(kernel_hbm, kernel_scr), (win_hbm, win_scr), (wout_hbm, wout_scr), (ib, ib_scr)]
     moves += list(zip((cb, ng, ns, ob, ls), vectors))
     moves += [(feat.at[:, pl.ds(far, m)], row_a), (feat.at[:, pl.ds(near, m)], row_b)]
-    moves += [(feat.at[:, :, 0:8], low), (feat.at[:, :, cols - 8 : cols], high)]
     copies = [pltpu.make_async_copy(src, dst, sems.at[n]) for n, (src, dst) in enumerate(moves)]
     for copy in copies:
         copy.start()
@@ -123,9 +121,6 @@
         column = jnp.broadcast_to(ref[...], (8, cs)).T
         out_ref[base : base + cs, taps + n : taps + n + 1] = column[:, 0:1]
     out_ref[base + cs : base + cs + 1, 0:hs] = ib_scr[...]
-    first, last = low[:, :, 0:m], high[:, :, 8 - m : 8]
-    col_a[...] = jnp.where(even_c, last, first)
-    col_b[...] = jnp.where(even_c, first, last)
 
 
 def with_corners(ms, edge_a, edge_b, got_a, got_b, out_a, out_b):
@@ -145,21 +140,14 @@
         out_b[:, pl.ds(at, m)] = jnp.where(even_c, first, last)
 
 
-def lay_out(parts, out):
-    n = 0
-    for part in parts:
-        out[n : n + part.shape[0]] = part[...]
-        n += part.shape[0]
-
-
-def first_join_body(ms, edge_a, edge_b, got_a, got_b, *refs):
-    parts, (slots, out_a, out_b) = refs[:-3], refs[-3:]
-    lay_out(parts, slots)
+def first_join_body(ms, inner, got_a, got_b, slots, out_slots, out_a, out_b, edge_a, edge_b):
+    cols, m = inner.shape[2], got_a.shape[1]
+    even_c, _ = side(ms, "col")
+    first, last = inner[:, :, 0:m], inner[:, :, cols - m :]
+    edge_a[...] = jnp.where(even_c, last, first)
+    edge_b[...] = jnp.where(even_c, first, last)
     with_corners(ms, edge_a, edge_b, got_a, got_b, out_a, out_b)
-
-
-def join_body(waits, *refs):
-    lay_out(refs[waits:-1], refs[-1])
+    out_slots[...] = slots[...]
 
 
 def back_join_body(ms, edge_a, edge_b, got_a, got_b, large, large_got, small, small_got, *refs):
@@ -186,6 +174,15 @@
                     term = w[i] * s
                     acc[p] = term if acc[p] is None else acc[p] + term
     return acc
+
+
+def slot_for(distance, order):
+    at = jnp.int32(0)
+    bit = 1
+    while bit < len(order):
+        at = at + jnp.where((distance & bit) != 0, order.index(bit), 0)
+        bit *= 2
+    return at
 
 
 def fill(ms, dst, inner, row_a, row_b, col_a, col_b):
@@ -204,15 +201,8 @@
         dst[b, :, LEFT + cols : LEFT + cols + m, :] = jnp.where(even_c, x, y)
 
 
-def small_columns(slots_ref, hs, cs, count, me, order, scratch):
-    base = 2 * hs
-    for s in range(count):
-        scratch[order[s] * cs : (order[s] + 1) * cs, :] = slots_ref[s, base : base + cs, :]
-    return exchange_order(scratch[...], cs, count, me)
-
-
 def mix_body(
-    ms, order, factor, taps_i, taps_j, tile,
+    ms, order, holders, factor, taps_i, taps_j, tile,
     feat, got_ra, got_rb, got_ca, got_cb, slots_ref, cot_ref,
     src_ref, dconv_ref, row_a, row_b, col_a, col_b, grads_ref, chan_ref, small_ref,
     conv_scr, cols_scr, kb_scr, win_scr, wout_scr, w1_scr, w2_scr, w4_scr, bias_scr,
@@ -228,20 +218,18 @@
     me = device_index(ms)
 
     fill(ms, src_ref, feat, got_ra, got_rb, got_ca, got_cb)
-    columns = small_columns(slots_ref, hs, cs, count, me, order, cols_scr)
-    cols_scr[...] = columns
-    rows_form = columns.T
+    base = 2 * hs
+    for s, dev in enumerate(holders):
+        cols_scr[dev * cs : (dev + 1) * cs, :] = slots_ref[s, base : base + cs, :]
+        win_scr[dev * hs : (dev + 1) * hs, :] = slots_ref[s, 0:hs, :]
+        wout_scr[dev * hs : (dev + 1) * hs, :] = slots_ref[s, hs : 2 * hs, :]
+        spread = jnp.broadcast_to(slots_ref[s, base + cs : base + cs + 1, :], (LANES, LANES)).T
+        bias_scr[dev * hs : (dev + 1) * hs, :] = spread[0:hs, :]
+    rows_form = cols_scr[...].T
     small_ref[...] = rows_form
     for t in range(taps):
         kb_scr[t] = jnp.broadcast_to(rows_form[t : t + 1, :], (8, C))
     conv_bias = jnp.broadcast_to(rows_form[taps : taps + 1, :], (8, C))
-
-    for s in range(count):
-        win_scr[s * hs : (s + 1) * hs, :] = slots_ref[s, 0:hs, :]
-        wout_scr[s * hs : (s + 1) * hs, :] = slots_ref[s, hs : 2 * hs, :]
-    for s in range(count):
-        cols_bias = jnp.broadcast_to(slots_ref[s, 2 * hs + cs : 2 * hs + cs + 1, :], (LANES, LANES)).T
-        bias_scr[s * hs : (s + 1) * hs, :] = cols_bias[0:hs, :]
 
     scale_row = rows_form[taps + 4 : taps + 5, :]
     wh, wl = split(win_scr[...])
@@ -343,12 +331,13 @@
     col_b[...] = jnp.where(even_c, first, last)
 
     h = gw2_scr[:, 0:C] + gw2_scr[:, C : 2 * C]
-    gw1 = (gw1_scr[:, 0:C] + gw1_scr[:, C : 2 * C]) * factor
-    gw2 = h * (scale_row * factor)
+    gw1_scr[:, 0:C] = (gw1_scr[:, 0:C] + gw1_scr[:, C : 2 * C]) * factor
+    gw2_scr[:, 0:C] = h * (scale_row * factor)
     gb = (jnp.sum(gb_scr[...].T, axis=0, keepdims=True)) * factor
-    for s in range(count):
-        grads_ref[s, 0:hs, :] = gw1[s * hs : (s + 1) * hs, :]
-        grads_ref[s, hs : 2 * hs, :] = gw2[s * hs : (s + 1) * hs, :]
+    for dev in range(count):
+        at = slot_for(me ^ dev, order)
+        grads_ref[at, 0:hs, :] = gw1_scr[dev * hs : (dev + 1) * hs, 0:C]
+        grads_ref[at, hs : 2 * hs, :] = gw2_scr[dev * hs : (dev + 1) * hs, 0:C]
     total = jnp.sum(cot_sum[...], axis=0, keepdims=True)
     outb = rows_form[taps + 3 : taps + 4, :]
     scale_grad = jnp.sum(h * wout_scr[...], axis=0, keepdims=True) + outb * total
@@ -394,7 +383,8 @@
     hs = chan_ref.shape[1] // count
     for s in range(count):
         out_ref[s, 0:cs, :] = columns[order[s] * cs : (order[s] + 1) * cs, :]
-        out_ref[s, cs : cs + 1, 0:hs] = chan_ref[5:6, s * hs : (s + 1) * hs]
+    for dev in range(count):
+        out_ref[slot_for(me ^ dev, order), cs : cs + 1, 0:hs] = chan_ref[5:6, dev * hs : (dev + 1) * hs]
 
 
 def features_grad_body(ms, taps_i, taps_j, inner, got_ra, got_rb, got_ca, got_cb, small_ref, cot_ref, out_ref, ext_scr, kb_scr):
@@ -474,12 +464,11 @@
 
     vm = pltpu.VMEM
     vectors = [v.reshape(1, cs) for v in (conv_bias, norm_gain, norm_shift, out_bias, layer_scale)]
-    block, row_a, row_b, col_a, col_b = call(
+    block, row_a, row_b = call(
         functools.partial(start_body, ms),
         (
             shape(slot, LANES),
             *(shape(batch, m, cols, C) for _ in range(2)),
-            *(shape(batch, rows, m, C) for _ in range(2)),
         ),
         scratch=(
             vm((taps_i, cs, taps_j), f32),
@@ -487,9 +476,7 @@
             vm((1, hs), f32),
             vm((hs, C), f32),
             vm((hs, C), f32),
-            vm((batch, rows, 8, C), f32),
-            vm((batch, rows, 8, C), f32),
-            pltpu.SemaphoreType.DMA((13,)),
+            pltpu.SemaphoreType.DMA((11,)),
         ),
         size=10**6,
         limit=None,
@@ -497,29 +484,23 @@
     )(features, conv_kernel.transpose(0, 2, 1), *vectors, w_in.T, in_bias.reshape(1, hs), w_out)
 
     edges = tuple(shape(batch, rows + 2 * m, m, C) for _ in range(2))
-    anywhere, in_vmem = pl.BlockSpec(memory_space=pl.ANY), pl.BlockSpec(memory_space=pltpu.VMEM)
     groups = groups_of(ms)
     order = [0]
+    for group in groups:
+        order = [mask ^ x for mask in masks(group) for x in order]
     got_ra, got_rb = both_pairs(row_a, row_b, "row")
-    slots = block[None]
-    for n, group in enumerate(groups):
-        parts = [slots] + [flip(slots, mask, count) for mask in masks(group)[1:]]
-        order = [mask ^ x for mask in masks(group) for x in order]
-        slots = shape(len(order), slot, LANES)
-        if n == 0:
-            slots, edge_a, edge_b = call(functools.partial(first_join_body, ms), (slots, *edges))(
-                col_a, col_b, got_ra, got_rb, *parts
-            )
-            got_ca, got_cb = both_pairs(edge_a, edge_b, "col")
-        else:
-            waits = (got_ca, got_cb) if n == 1 else ()
-            slots = call(
-                functools.partial(join_body, len(waits)), slots,
-                in_specs=[anywhere] * len(waits) + [in_vmem] * len(parts),
-            )(*waits, *parts)
+    slots = lax.all_gather(block, "row")
+    slots, edge_a, edge_b = call(
+        functools.partial(first_join_body, ms),
+        (shape(*slots.shape), *edges),
+        scratch=[vm((batch, rows, m, C), f32) for _ in range(2)],
+    )(features, got_ra, got_rb, slots)
+    got_ca, got_cb = both_pairs(edge_a, edge_b, "col")
+    holders = [r * ms["col"] + c for c in range(ms["col"]) for r in range(ms["row"])]
+    slots = lax.all_gather(slots, "col").reshape(count, slot, LANES)
     tile = 4 * cols
     src, dconv, d_row_a, d_row_b, d_col_a, d_col_b, grads, chan, small = call(
-        functools.partial(mix_body, ms, order, factor, taps_i, taps_j, tile),
+        functools.partial(mix_body, ms, order, holders, factor, taps_i, taps_j, tile),
         (
             shape(batch, rows + 2 * m, wide, C),
             shape(batch, rows, cols, C),

time: 76.6 us -> 84.4 us (1.10)
  blocking collectives: 0 us -> 26.8 us
  starting transfers between devices: 30.6 us -> 21.4 us
  waiting for transfers between devices: 12.9 us -> 5.4 us
  local copies, waits for them, and re-layouts: 2.45 us -> 0.04 us
    all_gather x0 -> x2, blocking collectives: none -> 26.8 us  [the longest x1 15.2 us: per_device(): slots = lax.all_gather(slots, 'col').reshape(count, slot, LANES)]
    ppermute x15 -> x8, starting transfers between devices: 16.7 us -> 8.64 us  [flip(): return lax.ppermute(x, AXES, [(i, i ^ mask) for i in range(count)])]
    ppermute x15 -> x8, waiting for transfers between devices: 7.85 us -> 3.29 us  [flip(): return lax.ppermute(x, AXES, [(i, i ^ mask) for i in range(count)])]
    ppermute x4, waiting for transfers between devices: 5.02 us -> 2.09 us  [both_pairs(): lax.ppermute(b, axis, pairs(count, True))]
    unnamed x10 -> x4, local copies, waits for them, and re-layouts: 2.41 us -> 0.01 us
    ppermute x4, starting transfers between devices: 9.33 us -> 8.15 us  [both_pairs(): lax.ppermute(b, axis, pairs(count, True))]
    pallas_call x4 -> x2, Pallas kernels: 16.5 us -> 16.6 us  [the longest x1 16.5 us: per_device(): call(functools.partial(mix_body, ms, order, holders, factor, taps_i, taps...]
  transfers between devices with their start and end apart: 23 -> 16, of which waited for: 8 -> 5; matrix products, arithmetic and copies ran while one was open for 0% -> 0% of each run, Pallas kernels for 13% -> 12%
where the time goes in v4:
time: 84.4 us; the launch traced here: 84.1 us
  Pallas kernels  29.7 us (35%)
  blocking collectives  26.8 us (32%)
  starting transfers between devices  21.4 us (25%)
  waiting for transfers between devices  5.4 us (6%)
    pallas_call x1, Pallas kernels, per_device(): call(functools.partial(mix_body, ms, order, holders, factor, taps_i, taps...  16.5 us
    all_gather x1, blocking collectives, per_device(): slots = lax.all_gather(slots, 'col').reshape(count, slot, LANES)  15.2 us
    all_gather x1, blocking collectives, per_device(): slots = lax.all_gather(block, 'row')  11.6 us
    ppermute x8, starting transfers between devices, flip(): return lax.ppermute(x, AXES, [(i, i ^ mask) for i in range(count)])  8.64 us
    ppermute x4, starting transfers between devices, both_pairs(): lax.ppermute(b, axis, pairs(count, True))  8.15 us
    pallas_call x1, Pallas kernels, per_device(): call(functools.partial(kernel_grad_body, ms, order, factor, taps_i, taps_...  5.66 us
    ppermute x4, starting transfers between devices, both_pairs(): lax.ppermute(a, axis, pairs(count, False))  4.58 us
    pallas_call x1, Pallas kernels, per_device(): call(functools.partial(features_grad_body, ms, taps_i, taps_j), shape(bat...  4.55 us
  transfers between devices with their start and end apart: 16, of which 5 were waited for; matrix products, arithmetic and copies ran while one was open for 0% of the time, Pallas kernels for 12%

profile of v4, /device:TPU:0, one launch (start us, length us, event | category | flops | bytes accessed | tf_op | source)
XLA Modules:
  0.0 84.1 jit_solution(5859579038195087615)
XLA Ops:
  0.7 2.1 %shard_map.186 = (f32[40,128]{1,0:T(8,128)}, f32[2,3,64,128]{3,2,1,0:T(8,128)}, f32[2,3,64,128]{3,2,1,0:T(8,128)}) custom-call(f32[2,16,64,128]{3,2,1,0:T(8,128)} %feat.3, f32[7,4,7]{2,1,0:T(4,128)} %bitcast.26, f32[1,4]{1,0:T(1,128)} %bitcast.28, f32[1,4]{1,0:T(1,128)} %bitcast.29, f32[1,4]{1,0:T(1,128)} %bitcast.30, f32[1,4]{1,0:T(1,128)} %bitcast.31, ...), custom_call_target="tpu_custom_call" | custom-call | bytes 1000000 | tf_op jit(solution)/shard_map/pallas_call | solution.py:467
  2.8 3.0 %collective-permute-start = (f32[2,3,64,128]{3,2,1,0:T(8,128)}, f32[2,3,64,128]{3,2,1,0:T(8,128)S(1)}, u32[]{:S(2)}, u32[]{:S(2)}) collective-permute-start(f32[2,3,64,128]{3,2,1,0:T(8,128)} %get-tuple-element.40), channel_id=1, source_target_pairs={{0,8},{8,0},{16,24},{24,16},{1,9},{9,1},{17,25},{25,17},{2,10},{10... | collective-permute-start | bytes 589832 | tf_op jit(solution)/shard_map/ppermute | solution.py:86
  5.8 1.5 %collective-permute-start.1 = (f32[2,3,64,128]{3,2,1,0:T(8,128)}, f32[2,3,64,128]{3,2,1,0:T(8,128)S(1)}, u32[]{:S(2)}, u32[]{:S(2)}) collective-permute-start(f32[2,3,64,128]{3,2,1,0:T(8,128)} %get-tuple-element.41), channel_id=1, source_target_pairs={{0,24},{8,16},{16,8},{24,0},{1,25},{9,17},{17,9},{25,1},{2,26},{10... | collective-permute-start | bytes 589832 | tf_op jit(solution)/shard_map/ppermute | solution.py:86
  7.3 11.6 %all-gather = f32[160,128]{1,0:T(8,128)S(1)} all-gather(f32[40,128]{1,0:T(8,128)} %get-tuple-element.42), channel_id=2, replica_groups=mesh['row'=4,'col'=8] {'row'}, dimensions={0}, use_global_device_ids=true | all-gather | bytes 102400 | tf_op jit(solution)/shard_map/all_gather | solution.py:492
  19.1 3.7 %collective-permute-start.3 = (f32[2,22,3,128]{3,2,1,0:T(4,128)S(1)}, f32[2,22,3,128]{3,2,1,0:T(4,128)S(1)}, u32[]{:S(2)}, u32[]{:S(2)}) collective-permute-start(f32[2,22,3,128]{3,2,1,0:T(4,128)S(1)} %get-tuple-element.44), channel_id=1, source_target_pairs={{0,7},{1,2},{2,1},{3,4},{4,3},{5,6},{6,5},{7,0},{8,15},{9,10},{10,... | collective-permute-start | bytes 202760 | tf_op jit(solution)/shard_map/ppermute | solution.py:86
  22.8 15.2 %all-gather.1.slots_ref = f32[32,40,128]{2,1,0:T(8,128)S(1)} all-gather(f32[4,40,128]{2,1,0:T(8,128)S(1)} %get-tuple-element.45), channel_id=3, replica_groups=mesh['row'=4,'col'=8] {'col'}, dimensions={0}, use_global_device_ids=true | all-gather | bytes 737280 | tf_op jit(solution)/shard_map/all_gather | solution.py:500
  38.0 16.5 %shard_map.188 = (f32[2,22,80,128]{3,2,1,0:T(8,128)S(1)}, f32[2,16,64,128]{3,2,1,0:T(8,128)S(1)}, f32[2,3,64,128]{3,2,1,0:T(8,128)S(1)}, f32[2,3,64,128]{3,2,1,0...) custom-call(f32[2,16,64,128]{3,2,1,0:T(8,128)S(1)} %copy-done, ...), custom_call_target="tpu_custom_call" | custom-call | flops 12000000000 | bytes 8000000 | tf_op jit(solution)/shard_map/pallas_call | solution.py:502
  54.5 1.5 %collective-permute-start.4 = (f32[2,3,64,128]{3,2,1,0:T(8,128)S(1)}, f32[2,3,64,128]{3,2,1,0:T(8,128)S(1)}, u32[]{:S(2)}, u32[]{:S(2)}) collective-permute-start(f32[2,3,64,128]{3,2,1,0:T(8,128)S(1)} %get-tuple-element.47), channel_id=1, source_target_pairs={{0,8},{8,0},{16,24},{24,16},{1,9},{9,1},{17,25},{25,17},{2,10},{10... | collective-permute-start | bytes 589832 | tf_op jit(solution)/shard_map/ppermute | solution.py:86
  56.0 1.5 %collective-permute-start.5 = (f32[2,3,64,128]{3,2,1,0:T(8,128)S(1)}, f32[2,3,64,128]{3,2,1,0:T(8,128)S(1)}, u32[]{:S(2)}, u32[]{:S(2)}) collective-permute-start(f32[2,3,64,128]{3,2,1,0:T(8,128)S(1)} %get-tuple-element.48), channel_id=1, source_target_pairs={{0,24},{8,16},{16,8},{24,0},{1,25},{9,17},{17,9},{25,1},{2,26},{10... | collective-permute-start | bytes 589832 | tf_op jit(solution)/shard_map/ppermute | solution.py:86
  57.7 5.7 %shard_map.189.small = f32[32,8,128]{2,1,0:T(8,128)S(1)} custom-call(f32[2,22,80,128]{3,2,1,0:T(8,128)S(1)} %get-tuple-element.52.src_ref, f32[2,16,64,128]{3,2,1,0:T(8,128)S(1)} %get-tuple-element.46.dconv_ref.inner, f32[8,512]{1,0:T(8,128)S(1)} %get-tuple-element.53.chan_ref), custom_call_target="tpu_custom_call" | custom-call | flops 4000000000 | bytes 4000000 | tf_op jit(solution)/shard_map/pallas_call | solution.py:540
  63.4 0.6 collective-permute-start.7
  63.9 0.9 %collective-permute-done.7.small_got = f32[16,8,128]{2,1,0:T(8,128)S(1)} collective-permute-done((f32[16,8,128]{2,1,0:T(8,128)S(1)}, f32[16,8,128]{2,1,0:T(8,128)S(1)}, u32[]{:S(2)}, u32[]{:S(2)}) %collective-permute-start.7) | collective-permute-done | bytes 65568 | tf_op jit(solution)/shard_map/ppermute | solution.py:431
  64.8 2.1 %collective-permute-done.5.got_b.got_rb = f32[2,3,64,128]{3,2,1,0:T(8,128)S(1)} collective-permute-done((f32[2,3,64,128]{3,2,1,0:T(8,128)S(1)}, f32[2,3,64,128]{3,2,1,0:T(8,128)S(1)}, u32[]{:S(2)}, u32[]{:S(2)}) %collective-permute-start.5) | collective-permute-done | bytes 196640 | tf_op jit(solution)/shard_map/ppermute | solution.py:86
  67.0 0.6 collective-permute-start.10
  67.6 1.4 %collective-permute-start.11 = (f32[4,40,128]{2,1,0:T(8,128)S(1)}, f32[4,40,128]{2,1,0:T(8,128)S(1)}, u32[]{:S(2)}, u32[]{:S(2)}) collective-permute-start(f32[4,40,128]{2,1,0:T(8,128)S(1)} %get-tuple-element.59), channel_id=1, source_target_pairs={{0,16},{1,17},{2,18},{3,19},{4,20},{5,21},{6,22},{7,23},{8,24},{9,... | collective-permute-start | bytes 245768 | tf_op jit(solution)/shard_map/ppermute | solution.py:431
  69.0 1.5 %collective-permute-start.12 = (f32[4,40,128]{2,1,0:T(8,128)S(1)}, f32[4,40,128]{2,1,0:T(8,128)S(1)}, u32[]{:S(2)}, u32[]{:S(2)}) collective-permute-start(f32[4,40,128]{2,1,0:T(8,128)S(1)} %get-tuple-element.60), channel_id=1, source_target_pairs={{0,24},{1,25},{2,26},{3,27},{4,28},{5,29},{6,30},{7,31},{8,16},{9,... | collective-permute-start | bytes 245768 | tf_op jit(solution)/shard_map/ppermute | solution.py:431
  70.5 1.4 %collective-permute-start.9 = (f32[2,22,3,128]{3,2,1,0:T(4,128)S(1)}, f32[2,22,3,128]{3,2,1,0:T(4,128)S(1)}, u32[]{:S(2)}, u32[]{:S(2)}) collective-permute-start(f32[2,22,3,128]{3,2,1,0:T(4,128)S(1)} %get-tuple-element.55), channel_id=1, source_target_pairs={{0,7},{1,2},{2,1},{3,4},{4,3},{5,6},{6,5},{7,0},{8,15},{9,10},{10,... | collective-permute-start | bytes 202760 | tf_op jit(solution)/shard_map/ppermute | solution.py:86
  72.0 0.4 collective-permute-done.10
  72.4 0.6 collective-permute-done.11
  72.9 1.4 %collective-permute-done.12 = f32[4,40,128]{2,1,0:T(8,128)S(1)} collective-permute-done((f32[4,40,128]{2,1,0:T(8,128)S(1)}, f32[4,40,128]{2,1,0:T(8,128)S(1)}, u32[]{:S(2)}, u32[]{:S(2)}) %collective-permute-start.12) | collective-permute-done | bytes 81952 | tf_op jit(solution)/shard_map/ppermute | solution.py:431
  74.4 1.4 %collective-permute-start.15 = (f32[1,40,128]{2,1,0:T(8,128)S(1)}, f32[1,40,128]{2,1,0:T(8,128)S(1)}, u32[]{:S(2)}, u32[]{:S(2)}) collective-permute-start(f32[1,40,128]{2,1,0:T(8,128)S(1)} %get-tuple-element.70), channel_id=1, source_target_pairs={{0,6},{1,7},{2,4},{3,5},{4,2},{5,3},{6,0},{7,1},{8,14},{9,15},{10,... | collective-permute-start | bytes 61448 | tf_op jit(solution)/shard_map/ppermute | solution.py:431
  75.8 3.1 %collective-permute-start.13 = (f32[1,40,128]{2,1,0:T(8,128)S(1)}, f32[1,40,128]{2,1,0:T(8,128)S(1)}, u32[]{:S(2)}, u32[]{:S(2)}) collective-permute-start(f32[1,40,128]{2,1,0:T(8,128)S(1)} %get-tuple-element.72), channel_id=1, source_target_pairs={{0,2},{1,3},{2,0},{3,1},{4,6},{5,7},{6,4},{7,5},{8,10},{9,11},{10,... | collective-permute-start | bytes 61448 | tf_op jit(solution)/shard_map/ppermute | solution.py:431
  78.8 4.5 %shard_map.191 = f32[2,16,64,128]{3,2,1,0:T(8,128)} custom-call(f32[2,16,64,128]{3,2,1,0:T(8,128)S(1)} %get-tuple-element.46.dconv_ref.inner, f32[2,3,64,128]{3,2,1,0:T(8,128)S(1)} %collective-permute-done.4.got_a.got_ra, f32[2,3,64,128]{3,2,1,0:T(8,128)S(1)} %collective-permute-done.5.got_b.got_rb, f32[2,22,3,128]{3,2,1,0:T(4,128)S(1)} %collective-permute-done.8.got_ca, ...), custom_call_target="tpu_custom_call" | custom-call | flops 4000000000 | bytes 4000000 | tf_op jit(solution)/shard_map/pallas_call | solution.py:564
  83.4 0.7 shard_map.192
  (25 shorter events, 0.4 us)
Async XLA Ops:
  0.6 18.2 %copy-start = (f32[2,16,64,128]{3,2,1,0:T(8,128)S(1)}, f32[2,16,64,128]{3,2,1,0:T(8,128)}, u32[]{:S(2)}) copy-start(f32[2,16,64,128]{3,2,1,0:T(8,128)} %feat.3) | copy-start | bytes 3145732
  0.7 37.3 %copy-start.1 = (f32[2,16,64,128]{3,2,1,0:T(8,128)S(1)}, f32[2,16,64,128]{3,2,1,0:T(8,128)}, u32[]{:S(2)}) copy-start(f32[2,16,64,128]{3,2,1,0:T(8,128)} %cot_ref.3) | copy-start | bytes 3145732
  2.8 16.1 %collective-permute-start = (f32[2,3,64,128]{3,2,1,0:T(8,128)}, f32[2,3,64,128]{3,2,1,0:T(8,128)S(1)}, u32[]{:S(2)}, u32[]{:S(2)}) collective-permute-start(f32[2,3,64,128]{3,2,1,0:T(8,128)} %get-tuple-element.40), channel_id=1, source_target_pairs={{0,8},{8,0},{16,24},{24,16},{1,9},{9,1},{17,25},{25,17},{2,10},{10... | collective-permute-start | bytes 589832 | tf_op jit(solution)/shard_map/ppermute | solution.py:86
  5.8 13.1 %collective-permute-start.1 = (f32[2,3,64,128]{3,2,1,0:T(8,128)}, f32[2,3,64,128]{3,2,1,0:T(8,128)S(1)}, u32[]{:S(2)}, u32[]{:S(2)}) collective-permute-start(f32[2,3,64,128]{3,2,1,0:T(8,128)} %get-tuple-element.41), channel_id=1, source_target_pairs={{0,24},{8,16},{16,8},{24,0},{1,25},{9,17},{17,9},{25,1},{2,26},{10... | collective-permute-start | bytes 589832 | tf_op jit(solution)/shard_map/ppermute | solution.py:86
  19.0 19.0 %collective-permute-start.2 = (f32[2,22,3,128]{3,2,1,0:T(4,128)S(1)}, f32[2,22,3,128]{3,2,1,0:T(4,128)S(1)}, u32[]{:S(2)}, u32[]{:S(2)}) collective-permute-start(f32[2,22,3,128]{3,2,1,0:T(4,128)S(1)} %get-tuple-element.43), channel_id=1, source_target_pairs={{0,1},{1,0},{2,3},{3,2},{4,5},{5,4},{6,7},{7,6},{8,9},{9,8},{10,11... | collective-permute-start | bytes 202760 | tf_op jit(solution)/shard_map/ppermute | solution.py:86
  19.1 18.9 %collective-permute-start.3 = (f32[2,22,3,128]{3,2,1,0:T(4,128)S(1)}, f32[2,22,3,128]{3,2,1,0:T(4,128)S(1)}, u32[]{:S(2)}, u32[]{:S(2)}) collective-permute-start(f32[2,22,3,128]{3,2,1,0:T(4,128)S(1)} %get-tuple-element.44), channel_id=1, source_target_pairs={{0,7},{1,2},{2,1},{3,4},{4,3},{5,6},{6,5},{7,0},{8,15},{9,10},{10,... | collective-permute-start | bytes 202760 | tf_op jit(solution)/shard_map/ppermute | solution.py:86
  54.5 10.3 %collective-permute-start.4 = (f32[2,3,64,128]{3,2,1,0:T(8,128)S(1)}, f32[2,3,64,128]{3,2,1,0:T(8,128)S(1)}, u32[]{:S(2)}, u32[]{:S(2)}) collective-permute-start(f32[2,3,64,128]{3,2,1,0:T(8,128)S(1)} %get-tuple-element.47), channel_id=1, source_target_pairs={{0,8},{8,0},{16,24},{24,16},{1,9},{9,1},{17,25},{25,17},{2,10},{10... | collective-permute-start | bytes 589832 | tf_op jit(solution)/shard_map/ppermute | solution.py:86
  56.0 10.9 %collective-permute-start.5 = (f32[2,3,64,128]{3,2,1,0:T(8,128)S(1)}, f32[2,3,64,128]{3,2,1,0:T(8,128)S(1)}, u32[]{:S(2)}, u32[]{:S(2)}) collective-permute-start(f32[2,3,64,128]{3,2,1,0:T(8,128)S(1)} %get-tuple-element.48), channel_id=1, source_target_pairs={{0,24},{8,16},{16,8},{24,0},{1,25},{9,17},{17,9},{25,1},{2,26},{10... | collective-permute-start | bytes 589832 | tf_op jit(solution)/shard_map/ppermute | solution.py:86
  57.6 9.3 %collective-permute-start.6 = (f32[16,32,128]{2,1,0:T(8,128)S(1)}, f32[16,32,128]{2,1,0:T(8,128)S(1)}, u32[]{:S(2)}, u32[]{:S(2)}) collective-permute-start(f32[16,32,128]{2,1,0:T(8,128)S(1)} %slice.18), channel_id=1, source_target_pairs={{0,1},{1,0},{2,3},{3,2},{4,5},{5,4},{6,7},{7,6},{8,9},{9,8},{10,11... | collective-permute-start | bytes 786440 | tf_op jit(solution)/shard_map/ppermute | solution.py:431
  63.4 1.5 %collective-permute-start.7 = (f32[16,8,128]{2,1,0:T(8,128)S(1)}, f32[16,8,128]{2,1,0:T(8,128)S(1)}, u32[]{:S(2)}, u32[]{:S(2)}) collective-permute-start(f32[16,8,128]{2,1,0:T(8,128)S(1)} %slice.24), channel_id=1, source_target_pairs={{0,1},{1,0},{2,3},{3,2},{4,5},{5,4},{6,7},{7,6},{8,9},{9,8},{10,11... | collective-permute-start | bytes 196616 | tf_op jit(solution)/shard_map/ppermute | solution.py:431
  67.0 5.4 %collective-permute-start.10 = (f32[4,40,128]{2,1,0:T(8,128)S(1)}, f32[4,40,128]{2,1,0:T(8,128)S(1)}, u32[]{:S(2)}, u32[]{:S(2)}) collective-permute-start(f32[4,40,128]{2,1,0:T(8,128)S(1)} %get-tuple-element.58), channel_id=1, source_target_pairs={{0,8},{1,9},{2,10},{3,11},{4,12},{5,13},{6,14},{7,15},{8,0},{9,1},... | collective-permute-start | bytes 245768 | tf_op jit(solution)/shard_map/ppermute | solution.py:431
  67.6 5.3 %collective-permute-start.11 = (f32[4,40,128]{2,1,0:T(8,128)S(1)}, f32[4,40,128]{2,1,0:T(8,128)S(1)}, u32[]{:S(2)}, u32[]{:S(2)}) collective-permute-start(f32[4,40,128]{2,1,0:T(8,128)S(1)} %get-tuple-element.59), channel_id=1, source_target_pairs={{0,16},{1,17},{2,18},{3,19},{4,20},{5,21},{6,22},{7,23},{8,24},{9,... | collective-permute-start | bytes 245768 | tf_op jit(solution)/shard_map/ppermute | solution.py:431
  69.0 5.3 %collective-permute-start.12 = (f32[4,40,128]{2,1,0:T(8,128)S(1)}, f32[4,40,128]{2,1,0:T(8,128)S(1)}, u32[]{:S(2)}, u32[]{:S(2)}) collective-permute-start(f32[4,40,128]{2,1,0:T(8,128)S(1)} %get-tuple-element.60), channel_id=1, source_target_pairs={{0,24},{1,25},{2,26},{3,27},{4,28},{5,29},{6,30},{7,31},{8,16},{9,... | collective-permute-start | bytes 245768 | tf_op jit(solution)/shard_map/ppermute | solution.py:431
  70.5 8.3 %collective-permute-start.8 = (f32[2,22,3,128]{3,2,1,0:T(4,128)S(1)}, f32[2,22,3,128]{3,2,1,0:T(4,128)S(1)}, u32[]{:S(2)}, u32[]{:S(2)}) collective-permute-start(f32[2,22,3,128]{3,2,1,0:T(4,128)S(1)} %get-tuple-element.54), channel_id=1, source_target_pairs={{0,1},{1,0},{2,3},{3,2},{4,5},{5,4},{6,7},{7,6},{8,9},{9,8},{10,11... | collective-permute-start | bytes 202760 | tf_op jit(solution)/shard_map/ppermute | solution.py:86
  70.5 8.3 %collective-permute-start.9 = (f32[2,22,3,128]{3,2,1,0:T(4,128)S(1)}, f32[2,22,3,128]{3,2,1,0:T(4,128)S(1)}, u32[]{:S(2)}, u32[]{:S(2)}) collective-permute-start(f32[2,22,3,128]{3,2,1,0:T(4,128)S(1)} %get-tuple-element.55), channel_id=1, source_target_pairs={{0,7},{1,2},{2,1},{3,4},{4,3},{5,6},{6,5},{7,0},{8,15},{9,10},{10,... | collective-permute-start | bytes 202760 | tf_op jit(solution)/shard_map/ppermute | solution.py:86
  74.4 9.0 %collective-permute-start.15 = (f32[1,40,128]{2,1,0:T(8,128)S(1)}, f32[1,40,128]{2,1,0:T(8,128)S(1)}, u32[]{:S(2)}, u32[]{:S(2)}) collective-permute-start(f32[1,40,128]{2,1,0:T(8,128)S(1)} %get-tuple-element.70), channel_id=1, source_target_pairs={{0,6},{1,7},{2,4},{3,5},{4,2},{5,3},{6,0},{7,1},{8,14},{9,15},{10,... | collective-permute-start | bytes 61448 | tf_op jit(solution)/shard_map/ppermute | solution.py:431
  75.7 7.6 %collective-permute-start.14 = (f32[1,40,128]{2,1,0:T(8,128)S(1)}, f32[1,40,128]{2,1,0:T(8,128)S(1)}, u32[]{:S(2)}, u32[]{:S(2)}) collective-permute-start(f32[1,40,128]{2,1,0:T(8,128)S(1)} %get-tuple-element.71), channel_id=1, source_target_pairs={{0,4},{1,5},{2,6},{3,7},{4,0},{5,1},{6,2},{7,3},{8,12},{9,13},{10,... | collective-permute-start | bytes 61448 | tf_op jit(solution)/shard_map/ppermute | solution.py:431
  75.8 7.6 %collective-permute-start.13 = (f32[1,40,128]{2,1,0:T(8,128)S(1)}, f32[1,40,128]{2,1,0:T(8,128)S(1)}, u32[]{:S(2)}, u32[]{:S(2)}) collective-permute-start(f32[1,40,128]{2,1,0:T(8,128)S(1)} %get-tuple-element.72), channel_id=1, source_target_pairs={{0,2},{1,3},{2,0},{3,1},{4,6},{5,7},{6,4},{7,5},{8,10},{9,11},{10,... | collective-permute-start | bytes 61448 | tf_op jit(solution)/shard_map/ppermute | solution.py:431

commit v5 on v3

--- a/solution.py
+++ b/solution.py
@@ -92,22 +92,20 @@
     return even, jnp.where(even, i > 0, i < ms[axis] - 1)
 
 
-def start_body(ms, feat, kernel_hbm, cb, ng, ns, ob, ls, win_hbm, ib, wout_hbm, out_ref, row_a, row_b, col_a, col_b,
-               kernel_scr, v0, v1, v2, v3, v4, ib_scr, win_scr, wout_scr, low, high, sems):
+def start_body(ms, feat, kernel_hbm, cb, ng, ns, ob, ls, win_hbm, ib, wout_hbm, out_ref, row_a, row_b,
+               kernel_scr, v0, v1, v2, v3, v4, ib_scr, win_scr, wout_scr, sems):
     batch, rows, cols, C = feat.shape
     taps_i, cs, taps_j = kernel_hbm.shape
     hs = win_hbm.shape[0]
     taps = taps_i * taps_j
     m = taps_i // 2
     even_r, _ = side(ms, "row")
-    even_c, _ = side(ms, "col")
     far = jnp.where(even_r, rows - m, 0)
     near = jnp.where(even_r, 0, rows - m)
     vectors = (v0, v1, v2, v3, v4)
     moves = [(kernel_hbm, kernel_scr), (win_hbm, win_scr), (wout_hbm, wout_scr), (ib, ib_scr)]
     moves += list(zip((cb, ng, ns, ob, ls), vectors))
     moves += [(feat.at[:, pl.ds(far, m)], row_a), (feat.at[:, pl.ds(near, m)], row_b)]
-    moves += [(feat.at[:, :, 0:8], low), (feat.at[:, :, cols - 8 : cols], high)]
     copies = [pltpu.make_async_copy(src, dst, sems.at[n]) for n, (src, dst) in enumerate(moves)]
     for copy in copies:
         copy.start()
@@ -123,9 +121,6 @@
         column = jnp.broadcast_to(ref[...], (8, cs)).T
         out_ref[base : base + cs, taps + n : taps + n + 1] = column[:, 0:1]
     out_ref[base + cs : base + cs + 1, 0:hs] = ib_scr[...]
-    first, last = low[:, :, 0:m], high[:, :, 8 - m : 8]
-    col_a[...] = jnp.where(even_c, last, first)
-    col_b[...] = jnp.where(even_c, first, last)
 
 
 def with_corners(ms, edge_a, edge_b, got_a, got_b, out_a, out_b):
@@ -145,17 +140,24 @@
         out_b[:, pl.ds(at, m)] = jnp.where(even_c, first, last)
 
 
-def lay_out(parts, out):
-    n = 0
+def lay_out(parts, out, n=0):
     for part in parts:
         out[n : n + part.shape[0]] = part[...]
         n += part.shape[0]
 
 
-def first_join_body(ms, edge_a, edge_b, got_a, got_b, *refs):
-    parts, (slots, out_a, out_b) = refs[:-3], refs[-3:]
-    lay_out(parts, slots)
+def first_join_body(ms, own_hbm, inner, got_a, got_b, *refs):
+    parts, (slots, out_a, out_b, edge_a, edge_b, sem) = refs[:-6], refs[-6:]
+    copy = pltpu.make_async_copy(own_hbm, slots.at[0:1], sem)
+    copy.start()
+    cols, m = inner.shape[2], got_a.shape[1]
+    even_c, _ = side(ms, "col")
+    first, last = inner[:, :, 0:m], inner[:, :, cols - m :]
+    edge_a[...] = jnp.where(even_c, last, first)
+    edge_b[...] = jnp.where(even_c, first, last)
     with_corners(ms, edge_a, edge_b, got_a, got_b, out_a, out_b)
+    lay_out(parts, slots, 1)
+    copy.wait()
 
 
 def join_body(waits, *refs):
@@ -474,12 +476,11 @@
 
     vm = pltpu.VMEM
     vectors = [v.reshape(1, cs) for v in (conv_bias, norm_gain, norm_shift, out_bias, layer_scale)]
-    block, row_a, row_b, col_a, col_b = call(
+    block, row_a, row_b = call(
         functools.partial(start_body, ms),
         (
             shape(slot, LANES),
             *(shape(batch, m, cols, C) for _ in range(2)),
-            *(shape(batch, rows, m, C) for _ in range(2)),
         ),
         scratch=(
             vm((taps_i, cs, taps_j), f32),
@@ -487,9 +488,7 @@
             vm((1, hs), f32),
             vm((hs, C), f32),
             vm((hs, C), f32),
-            vm((batch, rows, 8, C), f32),
-            vm((batch, rows, 8, C), f32),
-            pltpu.SemaphoreType.DMA((13,)),
+            pltpu.SemaphoreType.DMA((11,)),
         ),
         size=10**6,
         limit=None,
@@ -507,9 +506,12 @@
         order = [mask ^ x for mask in masks(group) for x in order]
         slots = shape(len(order), slot, LANES)
         if n == 0:
-            slots, edge_a, edge_b = call(functools.partial(first_join_body, ms), (slots, *edges))(
-                col_a, col_b, got_ra, got_rb, *parts
-            )
+            slots, edge_a, edge_b = call(
+                functools.partial(first_join_body, ms),
+                (slots, *edges),
+                scratch=(*(vm((batch, rows, m, C), f32) for _ in range(2)), pltpu.SemaphoreType.DMA),
+                in_specs=[anywhere] + [in_vmem] * (len(parts) + 2),
+            )(parts[0], features, got_ra, got_rb, *parts[1:])
             got_ca, got_cb = both_pairs(edge_a, edge_b, "col")
         else:
             waits = (got_ca, got_cb) if n == 1 else ()
@@ -517,7 +519,7 @@
                 functools.partial(join_body, len(waits)), slots,
                 in_specs=[anywhere] * len(waits) + [in_vmem] * len(parts),
             )(*waits, *parts)
-    tile = 4 * cols
+    tile = 8 * cols
     src, dconv, d_row_a, d_row_b, d_col_a, d_col_b, grads, chan, small = call(
         functools.partial(mix_body, ms, order, factor, taps_i, taps_j, tile),
         (

time: 76.6 us -> 73.6 us (0.961)
  local copies, waits for them, and re-layouts: 2.45 us -> 0.77 us
  Pallas kernels: 29.6 us -> 28.4 us
    unnamed x10 -> x6, local copies, waits for them, and re-layouts: 2.41 us -> 0.74 us
    pallas_call x1, Pallas kernels: 16.4 us -> 15.3 us  [per_device(): call(functools.partial(mix_body, ms, order, factor, taps_i, taps_j, tile)...]
  transfers between devices with their start and end apart: 23 -> 23, of which waited for: 8 -> 8; matrix products, arithmetic and copies ran while one was open for 0% -> 0% of each run, Pallas kernels for 13% -> 14%
where the time goes in v5:
time: 73.6 us; the launch traced here: 73.4 us
  starting transfers between devices  30.6 us (42%)
  Pallas kernels  28.4 us (39%)
  waiting for transfers between devices  12.9 us (18%)
  local copies, waits for them, and re-layouts  0.77 us (1%)
  between operations  0.77 us (1%)
    ppermute x15, starting transfers between devices, flip(): return lax.ppermute(x, AXES, [(i, i ^ mask) for i in range(count)])  16.7 us
    pallas_call x1, Pallas kernels, per_device(): call(functools.partial(mix_body, ms, order, factor, taps_i, taps_j, tile)...  15.3 us
    ppermute x4, starting transfers between devices, both_pairs(): lax.ppermute(b, axis, pairs(count, True))  9.33 us
    ppermute x15, waiting for transfers between devices, flip(): return lax.ppermute(x, AXES, [(i, i ^ mask) for i in range(count)])  7.85 us
    pallas_call x1, Pallas kernels, per_device(): call(functools.partial(kernel_grad_body, ms, order, factor, taps_i, taps_...  5.52 us
    ppermute x4, waiting for transfers between devices, both_pairs(): lax.ppermute(b, axis, pairs(count, True))  5.01 us
    ppermute x4, starting transfers between devices, both_pairs(): lax.ppermute(a, axis, pairs(count, False))  4.56 us
    pallas_call x1, Pallas kernels, per_device(): call(functools.partial(features_grad_body, ms, taps_i, taps_j), shape(bat...  4.55 us
  transfers between devices with their start and end apart: 23, of which 8 were waited for; matrix products, arithmetic and copies ran while one was open for 0% of the time, Pallas kernels for 14%

profile of v5, /device:TPU:0, one launch (start us, length us, event | category | flops | bytes accessed | tf_op | source)
XLA Modules:
  0.0 73.4 jit_solution(9400033103963477358)
XLA Ops:
  0.7 2.1 %shard_map.186 = (f32[40,128]{1,0:T(8,128)}, f32[2,3,64,128]{3,2,1,0:T(8,128)}, f32[2,3,64,128]{3,2,1,0:T(8,128)}) custom-call(f32[2,16,64,128]{3,2,1,0:T(8,128)} %feat.3, f32[7,4,7]{2,1,0:T(4,128)} %bitcast.29, f32[1,4]{1,0:T(1,128)} %bitcast.31, f32[1,4]{1,0:T(1,128)} %bitcast.32, f32[1,4]{1,0:T(1,128)} %bitcast.33, f32[1,4]{1,0:T(1,128)} %bitcast.34, ...), custom_call_target="tpu_custom_call" | custom-call | bytes 1000000 | tf_op jit(solution)/shard_map/pallas_call | solution.py:479
  2.7 3.0 %collective-permute-start = (f32[2,3,64,128]{3,2,1,0:T(8,128)}, f32[2,3,64,128]{3,2,1,0:T(8,128)S(1)}, u32[]{:S(2)}, u32[]{:S(2)}) collective-permute-start(f32[2,3,64,128]{3,2,1,0:T(8,128)} %get-tuple-element.40), channel_id=1, source_target_pairs={{0,8},{8,0},{16,24},{24,16},{1,9},{9,1},{17,25},{25,17},{2,10},{10... | collective-permute-start | bytes 589832 | tf_op jit(solution)/shard_map/ppermute | solution.py:86
  5.7 1.5 %collective-permute-start.1 = (f32[2,3,64,128]{3,2,1,0:T(8,128)}, f32[2,3,64,128]{3,2,1,0:T(8,128)S(1)}, u32[]{:S(2)}, u32[]{:S(2)}) collective-permute-start(f32[2,3,64,128]{3,2,1,0:T(8,128)} %get-tuple-element.41), channel_id=1, source_target_pairs={{0,24},{8,16},{16,8},{24,0},{1,25},{9,17},{17,9},{25,1},{2,26},{10... | collective-permute-start | bytes 589832 | tf_op jit(solution)/shard_map/ppermute | solution.py:86
  7.2 3.6 %collective-permute-start.4 = (f32[1,40,128]{2,1,0:T(8,128)}, f32[1,40,128]{2,1,0:T(8,128)S(1)}, u32[]{:S(2)}, u32[]{:S(2)}) collective-permute-start(f32[1,40,128]{2,1,0:T(8,128)} %bitcast.25), channel_id=1, source_target_pairs={{0,6},{1,7},{2,4},{3,5},{4,2},{5,3},{6,0},{7,1},{8,14},{9,15},{10,... | collective-permute-start | bytes 61448 | tf_op jit(solution)/shard_map/ppermute | solution.py:443
  10.8 0.8 %collective-permute-start.2 = (f32[1,40,128]{2,1,0:T(8,128)}, f32[1,40,128]{2,1,0:T(8,128)S(1)}, u32[]{:S(2)}, u32[]{:S(2)}) collective-permute-start(f32[1,40,128]{2,1,0:T(8,128)} %bitcast.27), channel_id=1, source_target_pairs={{0,2},{1,3},{2,0},{3,1},{4,6},{5,7},{6,4},{7,5},{8,10},{9,11},{10,... | collective-permute-start | bytes 61448 | tf_op jit(solution)/shard_map/ppermute | solution.py:443
  11.6 1.5 %collective-permute-done.4.refs_2_ = f32[1,40,128]{2,1,0:T(8,128)S(1)} collective-permute-done((f32[1,40,128]{2,1,0:T(8,128)}, f32[1,40,128]{2,1,0:T(8,128)S(1)}, u32[]{:S(2)}, u32[]{:S(2)}) %collective-permute-start.4) | collective-permute-done | bytes 20512 | tf_op jit(solution)/shard_map/ppermute | solution.py:443
  13.1 2.7 %collective-permute-done.3.refs_1_ = f32[1,40,128]{2,1,0:T(8,128)S(1)} collective-permute-done((f32[1,40,128]{2,1,0:T(8,128)}, f32[1,40,128]{2,1,0:T(8,128)S(1)}, u32[]{:S(2)}, u32[]{:S(2)}) %collective-permute-start.3) | collective-permute-done | bytes 20512 | tf_op jit(solution)/shard_map/ppermute | solution.py:443
  17.1 1.5 %collective-permute-start.9 = (f32[4,40,128]{2,1,0:T(8,128)S(1)}, f32[4,40,128]{2,1,0:T(8,128)S(1)}, u32[]{:S(2)}, u32[]{:S(2)}) collective-permute-start(f32[4,40,128]{2,1,0:T(8,128)S(1)} %get-tuple-element.45.refs_2_), channel_id=1, source_target_pairs={{0,24},{1,25},{2,26},{3,27},{4,28},{5,29},{6,30},{7,31},{8,16},{9,... | collective-permute-start | bytes 245768 | tf_op jit(solution)/shard_map/ppermute | solution.py:443
  18.6 1.5 %collective-permute-start.8 = (f32[4,40,128]{2,1,0:T(8,128)S(1)}, f32[4,40,128]{2,1,0:T(8,128)S(1)}, u32[]{:S(2)}, u32[]{:S(2)}) collective-permute-start(f32[4,40,128]{2,1,0:T(8,128)S(1)} %get-tuple-element.45.refs_2_), channel_id=1, source_target_pairs={{0,16},{1,17},{2,18},{3,19},{4,20},{5,21},{6,22},{7,23},{8,24},{9,... | collective-permute-start | bytes 245768 | tf_op jit(solution)/shard_map/ppermute | solution.py:443
  20.7 3.7 %collective-permute-start.6 = (f32[2,22,3,128]{3,2,1,0:T(4,128)S(1)}, f32[2,22,3,128]{3,2,1,0:T(4,128)S(1)}, u32[]{:S(2)}, u32[]{:S(2)}) collective-permute-start(f32[2,22,3,128]{3,2,1,0:T(4,128)S(1)} %get-tuple-element.44), channel_id=1, source_target_pairs={{0,7},{1,2},{2,1},{3,4},{4,3},{5,6},{6,5},{7,0},{8,15},{9,10},{10,... | collective-permute-start | bytes 202760 | tf_op jit(solution)/shard_map/ppermute | solution.py:86
  24.4 2.5 %collective-permute-done.6.refs_1_.got_cb = f32[2,22,3,128]{3,2,1,0:T(4,128)S(1)} collective-permute-done((f32[2,22,3,128]{3,2,1,0:T(4,128)S(1)}, f32[2,22,3,128]{3,2,1,0:T(4,128)S(1)}, u32[]{:S(2)}, u32[]{:S(2)}) %collective-permute-start.6) | collective-permute-done | bytes 67616 | tf_op jit(solution)/shard_map/ppermute | solution.py:86
  27.0 1.6 %collective-permute-done.10.refs_1_ = f32[16,40,128]{2,1,0:T(8,128)S(1)} collective-permute-done((f32[16,40,128]{2,1,0:T(8,128)S(1)}, f32[16,40,128]{2,1,0:T(8,128)S(1)}, u32[]{:S(2)}, u32[]{:S(2)}) %collective-permute-start.10) | collective-permute-done | bytes 327712 | tf_op jit(solution)/shard_map/ppermute | solution.py:443
  28.6 15.3 %shard_map.190 = (f32[2,22,80,128]{3,2,1,0:T(8,128)S(1)}, f32[2,16,64,128]{3,2,1,0:T(8,128)S(1)}, f32[2,3,64,128]{3,2,1,0:T(8,128)S(1)}, f32[2,3,64,128]{3,2,1,0...) custom-call(f32[2,16,64,128]{3,2,1,0:T(8,128)S(1)} %copy-done, ...), custom_call_target="tpu_custom_call" | custom-call | flops 12000000000 | bytes 8000000 | tf_op jit(solution)/shard_map/pallas_call | solution.py:523
  43.9 1.6 %collective-permute-start.11 = (f32[2,3,64,128]{3,2,1,0:T(8,128)S(1)}, f32[2,3,64,128]{3,2,1,0:T(8,128)S(1)}, u32[]{:S(2)}, u32[]{:S(2)}) collective-permute-start(f32[2,3,64,128]{3,2,1,0:T(8,128)S(1)} %get-tuple-element.47), channel_id=1, source_target_pairs={{0,8},{8,0},{16,24},{24,16},{1,9},{9,1},{17,25},{25,17},{2,10},{10... | collective-permute-start | bytes 589832 | tf_op jit(solution)/shard_map/ppermute | solution.py:86
  46.1 5.5 %shard_map.191.small = f32[32,8,128]{2,1,0:T(8,128)S(1)} custom-call(f32[2,22,80,128]{3,2,1,0:T(8,128)S(1)} %get-tuple-element.52.src_ref, f32[2,16,64,128]{3,2,1,0:T(8,128)S(1)} %get-tuple-element.46.dconv_ref.inner, f32[8,512]{1,0:T(8,128)S(1)} %get-tuple-element.53.chan_ref), custom_call_target="tpu_custom_call" | custom-call | flops 4000000000 | bytes 4000000 | tf_op jit(solution)/shard_map/pallas_call | solution.py:561
  52.2 0.9 %collective-permute-done.14.small_got = f32[16,8,128]{2,1,0:T(8,128)S(1)} collective-permute-done((f32[16,8,128]{2,1,0:T(8,128)S(1)}, f32[16,8,128]{2,1,0:T(8,128)S(1)}, u32[]{:S(2)}, u32[]{:S(2)}) %collective-permute-start.14) | collective-permute-done | bytes 65568 | tf_op jit(solution)/shard_map/ppermute | solution.py:443
  53.1 2.0 %collective-permute-done.12.got_b.got_rb = f32[2,3,64,128]{3,2,1,0:T(8,128)S(1)} collective-permute-done((f32[2,3,64,128]{3,2,1,0:T(8,128)S(1)}, f32[2,3,64,128]{3,2,1,0:T(8,128)S(1)}, u32[]{:S(2)}, u32[]{:S(2)}) %collective-permute-start.12) | collective-permute-done | bytes 196640 | tf_op jit(solution)/shard_map/ppermute | solution.py:86
  55.2 1.6 %collective-permute-start.17 = (f32[4,40,128]{2,1,0:T(8,128)S(1)}, f32[4,40,128]{2,1,0:T(8,128)S(1)}, u32[]{:S(2)}, u32[]{:S(2)}) collective-permute-start(f32[4,40,128]{2,1,0:T(8,128)S(1)} %get-tuple-element.58), channel_id=1, source_target_pairs={{0,8},{1,9},{2,10},{3,11},{4,12},{5,13},{6,14},{7,15},{8,0},{9,1},... | collective-permute-start | bytes 245768 | tf_op jit(solution)/shard_map/ppermute | solution.py:443
  56.7 1.5 %collective-permute-start.18 = (f32[4,40,128]{2,1,0:T(8,128)S(1)}, f32[4,40,128]{2,1,0:T(8,128)S(1)}, u32[]{:S(2)}, u32[]{:S(2)}) collective-permute-start(f32[4,40,128]{2,1,0:T(8,128)S(1)} %get-tuple-element.59), channel_id=1, source_target_pairs={{0,16},{1,17},{2,18},{3,19},{4,20},{5,21},{6,22},{7,23},{8,24},{9,... | collective-permute-start | bytes 245768 | tf_op jit(solution)/shard_map/ppermute | solution.py:443
  58.7 3.7 %collective-permute-start.16 = (f32[2,22,3,128]{3,2,1,0:T(4,128)S(1)}, f32[2,22,3,128]{3,2,1,0:T(4,128)S(1)}, u32[]{:S(2)}, u32[]{:S(2)}) collective-permute-start(f32[2,22,3,128]{3,2,1,0:T(4,128)S(1)} %get-tuple-element.55), channel_id=1, source_target_pairs={{0,7},{1,2},{2,1},{3,4},{4,3},{5,6},{6,5},{7,0},{8,15},{9,10},{10,... | collective-permute-start | bytes 202760 | tf_op jit(solution)/shard_map/ppermute | solution.py:86
  62.4 1.2 %collective-permute-done.19 = f32[4,40,128]{2,1,0:T(8,128)S(1)} collective-permute-done((f32[4,40,128]{2,1,0:T(8,128)S(1)}, f32[4,40,128]{2,1,0:T(8,128)S(1)}, u32[]{:S(2)}, u32[]{:S(2)}) %collective-permute-start.19) | collective-permute-done | bytes 81952 | tf_op jit(solution)/shard_map/ppermute | solution.py:443
  63.6 3.6 %collective-permute-start.22 = (f32[1,40,128]{2,1,0:T(8,128)S(1)}, f32[1,40,128]{2,1,0:T(8,128)S(1)}, u32[]{:S(2)}, u32[]{:S(2)}) collective-permute-start(f32[1,40,128]{2,1,0:T(8,128)S(1)} %get-tuple-element.70), channel_id=1, source_target_pairs={{0,6},{1,7},{2,4},{3,5},{4,2},{5,3},{6,0},{7,1},{8,14},{9,15},{10,... | collective-permute-start | bytes 61448 | tf_op jit(solution)/shard_map/ppermute | solution.py:443
  67.2 0.8 %collective-permute-start.20 = (f32[1,40,128]{2,1,0:T(8,128)S(1)}, f32[1,40,128]{2,1,0:T(8,128)S(1)}, u32[]{:S(2)}, u32[]{:S(2)}) collective-permute-start(f32[1,40,128]{2,1,0:T(8,128)S(1)} %get-tuple-element.72), channel_id=1, source_target_pairs={{0,2},{1,3},{2,0},{3,1},{4,6},{5,7},{6,4},{7,5},{8,10},{9,11},{10,... | collective-permute-start | bytes 61448 | tf_op jit(solution)/shard_map/ppermute | solution.py:443
  68.1 4.5 %shard_map.193 = f32[2,16,64,128]{3,2,1,0:T(8,128)} custom-call(f32[2,16,64,128]{3,2,1,0:T(8,128)S(1)} %get-tuple-element.46.dconv_ref.inner, f32[2,3,64,128]{3,2,1,0:T(8,128)S(1)} %collective-permute-done.11.got_a.got_ra, f32[2,3,64,128]{3,2,1,0:T(8,128)S(1)} %collective-permute-done.12.got_b.got_rb, f32[2,22,3,128]{3,2,1,0:T(4,128)S(1)} %collective-permute-done.15.got_ca, ...), custom_call_target="tpu_custom_call" | custom-call | flops 4000000000 | bytes 4000000 | tf_op jit(solution)/shard_map/pallas_call | solution.py:585
  (41 shorter events, 4.5 us)
Async XLA Ops:
  0.6 15.6 %copy-start = (f32[2,16,64,128]{3,2,1,0:T(8,128)S(1)}, f32[2,16,64,128]{3,2,1,0:T(8,128)}, u32[]{:S(2)}) copy-start(f32[2,16,64,128]{3,2,1,0:T(8,128)} %feat.3) | copy-start | bytes 3145732
  2.7 13.0 %collective-permute-start = (f32[2,3,64,128]{3,2,1,0:T(8,128)}, f32[2,3,64,128]{3,2,1,0:T(8,128)S(1)}, u32[]{:S(2)}, u32[]{:S(2)}) collective-permute-start(f32[2,3,64,128]{3,2,1,0:T(8,128)} %get-tuple-element.40), channel_id=1, source_target_pairs={{0,8},{8,0},{16,24},{24,16},{1,9},{9,1},{17,25},{25,17},{2,10},{10... | collective-permute-start | bytes 589832 | tf_op jit(solution)/shard_map/ppermute | solution.py:86
  5.7 10.5 %collective-permute-start.1 = (f32[2,3,64,128]{3,2,1,0:T(8,128)}, f32[2,3,64,128]{3,2,1,0:T(8,128)S(1)}, u32[]{:S(2)}, u32[]{:S(2)}) collective-permute-start(f32[2,3,64,128]{3,2,1,0:T(8,128)} %get-tuple-element.41), channel_id=1, source_target_pairs={{0,24},{8,16},{16,8},{24,0},{1,25},{9,17},{17,9},{25,1},{2,26},{10... | collective-permute-start | bytes 589832 | tf_op jit(solution)/shard_map/ppermute | solution.py:86
  7.2 5.8 %collective-permute-start.4 = (f32[1,40,128]{2,1,0:T(8,128)}, f32[1,40,128]{2,1,0:T(8,128)S(1)}, u32[]{:S(2)}, u32[]{:S(2)}) collective-permute-start(f32[1,40,128]{2,1,0:T(8,128)} %bitcast.25), channel_id=1, source_target_pairs={{0,6},{1,7},{2,4},{3,5},{4,2},{5,3},{6,0},{7,1},{8,14},{9,15},{10,... | collective-permute-start | bytes 61448 | tf_op jit(solution)/shard_map/ppermute | solution.py:443
  10.8 4.9 %collective-permute-start.3 = (f32[1,40,128]{2,1,0:T(8,128)}, f32[1,40,128]{2,1,0:T(8,128)S(1)}, u32[]{:S(2)}, u32[]{:S(2)}) collective-permute-start(f32[1,40,128]{2,1,0:T(8,128)} %bitcast.26), channel_id=1, source_target_pairs={{0,4},{1,5},{2,6},{3,7},{4,0},{5,1},{6,2},{7,3},{8,12},{9,13},{10,... | collective-permute-start | bytes 61448 | tf_op jit(solution)/shard_map/ppermute | solution.py:443
  10.8 4.9 %collective-permute-start.2 = (f32[1,40,128]{2,1,0:T(8,128)}, f32[1,40,128]{2,1,0:T(8,128)S(1)}, u32[]{:S(2)}, u32[]{:S(2)}) collective-permute-start(f32[1,40,128]{2,1,0:T(8,128)} %bitcast.27), channel_id=1, source_target_pairs={{0,2},{1,3},{2,0},{3,1},{4,6},{5,7},{6,4},{7,5},{8,10},{9,11},{10,... | collective-permute-start | bytes 61448 | tf_op jit(solution)/shard_map/ppermute | solution.py:443
  17.1 9.7 %collective-permute-start.9 = (f32[4,40,128]{2,1,0:T(8,128)S(1)}, f32[4,40,128]{2,1,0:T(8,128)S(1)}, u32[]{:S(2)}, u32[]{:S(2)}) collective-permute-start(f32[4,40,128]{2,1,0:T(8,128)S(1)} %get-tuple-element.45.refs_2_), channel_id=1, source_target_pairs={{0,24},{1,25},{2,26},{3,27},{4,28},{5,29},{6,30},{7,31},{8,16},{9,... | collective-permute-start | bytes 245768 | tf_op jit(solution)/shard_map/ppermute | solution.py:443
  18.6 8.3 %collective-permute-start.8 = (f32[4,40,128]{2,1,0:T(8,128)S(1)}, f32[4,40,128]{2,1,0:T(8,128)S(1)}, u32[]{:S(2)}, u32[]{:S(2)}) collective-permute-start(f32[4,40,128]{2,1,0:T(8,128)S(1)} %get-tuple-element.45.refs_2_), channel_id=1, source_target_pairs={{0,16},{1,17},{2,18},{3,19},{4,20},{5,21},{6,22},{7,23},{8,24},{9,... | collective-permute-start | bytes 245768 | tf_op jit(solution)/shard_map/ppermute | solution.py:443
  20.1 6.7 %collective-permute-start.7 = (f32[4,40,128]{2,1,0:T(8,128)S(1)}, f32[4,40,128]{2,1,0:T(8,128)S(1)}, u32[]{:S(2)}, u32[]{:S(2)}) collective-permute-start(f32[4,40,128]{2,1,0:T(8,128)S(1)} %get-tuple-element.45.refs_2_), channel_id=1, source_target_pairs={{0,8},{1,9},{2,10},{3,11},{4,12},{5,13},{6,14},{7,15},{8,0},{9,1},... | collective-permute-start | bytes 245768 | tf_op jit(solution)/shard_map/ppermute | solution.py:443
  20.7 3.7 %collective-permute-start.5 = (f32[2,22,3,128]{3,2,1,0:T(4,128)S(1)}, f32[2,22,3,128]{3,2,1,0:T(4,128)S(1)}, u32[]{:S(2)}, u32[]{:S(2)}) collective-permute-start(f32[2,22,3,128]{3,2,1,0:T(4,128)S(1)} %get-tuple-element.43), channel_id=1, source_target_pairs={{0,1},{1,0},{2,3},{3,2},{4,5},{5,4},{6,7},{7,6},{8,9},{9,8},{10,11... | collective-permute-start | bytes 202760 | tf_op jit(solution)/shard_map/ppermute | solution.py:86
  20.7 6.2 %collective-permute-start.6 = (f32[2,22,3,128]{3,2,1,0:T(4,128)S(1)}, f32[2,22,3,128]{3,2,1,0:T(4,128)S(1)}, u32[]{:S(2)}, u32[]{:S(2)}) collective-permute-start(f32[2,22,3,128]{3,2,1,0:T(4,128)S(1)} %get-tuple-element.44), channel_id=1, source_target_pairs={{0,7},{1,2},{2,1},{3,4},{4,3},{5,6},{6,5},{7,0},{8,15},{9,10},{10,... | collective-permute-start | bytes 202760 | tf_op jit(solution)/shard_map/ppermute | solution.py:86
  26.9 1.7 %collective-permute-start.10 = (f32[16,40,128]{2,1,0:T(8,128)S(1)}, f32[16,40,128]{2,1,0:T(8,128)S(1)}, u32[]{:S(2)}, u32[]{:S(2)}) collective-permute-start(f32[16,40,128]{2,1,0:T(8,128)S(1)} %shard_map.188.refs_0_), channel_id=1, source_target_pairs={{0,1},{1,0},{2,3},{3,2},{4,5},{5,4},{6,7},{7,6},{8,9},{9,8},{10,11... | collective-permute-start | bytes 983048 | tf_op jit(solution)/shard_map/ppermute | solution.py:443
  43.9 9.2 %collective-permute-start.11 = (f32[2,3,64,128]{3,2,1,0:T(8,128)S(1)}, f32[2,3,64,128]{3,2,1,0:T(8,128)S(1)}, u32[]{:S(2)}, u32[]{:S(2)}) collective-permute-start(f32[2,3,64,128]{3,2,1,0:T(8,128)S(1)} %get-tuple-element.47), channel_id=1, source_target_pairs={{0,8},{8,0},{16,24},{24,16},{1,9},{9,1},{17,25},{25,17},{2,10},{10... | collective-permute-start | bytes 589832 | tf_op jit(solution)/shard_map/ppermute | solution.py:86
  45.5 9.6 %collective-permute-start.12 = (f32[2,3,64,128]{3,2,1,0:T(8,128)S(1)}, f32[2,3,64,128]{3,2,1,0:T(8,128)S(1)}, u32[]{:S(2)}, u32[]{:S(2)}) collective-permute-start(f32[2,3,64,128]{3,2,1,0:T(8,128)S(1)} %get-tuple-element.48), channel_id=1, source_target_pairs={{0,24},{8,16},{16,8},{24,0},{1,25},{9,17},{17,9},{25,1},{2,26},{10... | collective-permute-start | bytes 589832 | tf_op jit(solution)/shard_map/ppermute | solution.py:86
  46.0 9.1 %collective-permute-start.13 = (f32[16,32,128]{2,1,0:T(8,128)S(1)}, f32[16,32,128]{2,1,0:T(8,128)S(1)}, u32[]{:S(2)}, u32[]{:S(2)}) collective-permute-start(f32[16,32,128]{2,1,0:T(8,128)S(1)} %slice.18), channel_id=1, source_target_pairs={{0,1},{1,0},{2,3},{3,2},{4,5},{5,4},{6,7},{7,6},{8,9},{9,8},{10,11... | collective-permute-start | bytes 786440 | tf_op jit(solution)/shard_map/ppermute | solution.py:443
  51.6 1.5 %collective-permute-start.14 = (f32[16,8,128]{2,1,0:T(8,128)S(1)}, f32[16,8,128]{2,1,0:T(8,128)S(1)}, u32[]{:S(2)}, u32[]{:S(2)}) collective-permute-start(f32[16,8,128]{2,1,0:T(8,128)S(1)} %slice.24), channel_id=1, source_target_pairs={{0,1},{1,0},{2,3},{3,2},{4,5},{5,4},{6,7},{7,6},{8,9},{9,8},{10,11... | collective-permute-start | bytes 196616 | tf_op jit(solution)/shard_map/ppermute | solution.py:443
  55.2 7.2 %collective-permute-start.17 = (f32[4,40,128]{2,1,0:T(8,128)S(1)}, f32[4,40,128]{2,1,0:T(8,128)S(1)}, u32[]{:S(2)}, u32[]{:S(2)}) collective-permute-start(f32[4,40,128]{2,1,0:T(8,128)S(1)} %get-tuple-element.58), channel_id=1, source_target_pairs={{0,8},{1,9},{2,10},{3,11},{4,12},{5,13},{6,14},{7,15},{8,0},{9,1},... | collective-permute-start | bytes 245768 | tf_op jit(solution)/shard_map/ppermute | solution.py:443
  56.7 5.7 %collective-permute-start.18 = (f32[4,40,128]{2,1,0:T(8,128)S(1)}, f32[4,40,128]{2,1,0:T(8,128)S(1)}, u32[]{:S(2)}, u32[]{:S(2)}) collective-permute-start(f32[4,40,128]{2,1,0:T(8,128)S(1)} %get-tuple-element.59), channel_id=1, source_target_pairs={{0,16},{1,17},{2,18},{3,19},{4,20},{5,21},{6,22},{7,23},{8,24},{9,... | collective-permute-start | bytes 245768 | tf_op jit(solution)/shard_map/ppermute | solution.py:443
  58.3 5.3 %collective-permute-start.19 = (f32[4,40,128]{2,1,0:T(8,128)S(1)}, f32[4,40,128]{2,1,0:T(8,128)S(1)}, u32[]{:S(2)}, u32[]{:S(2)}) collective-permute-start(f32[4,40,128]{2,1,0:T(8,128)S(1)} %get-tuple-element.60), channel_id=1, source_target_pairs={{0,24},{1,25},{2,26},{3,27},{4,28},{5,29},{6,30},{7,31},{8,16},{9,... | collective-permute-start | bytes 245768 | tf_op jit(solution)/shard_map/ppermute | solution.py:443
  58.7 9.4 %collective-permute-start.15 = (f32[2,22,3,128]{3,2,1,0:T(4,128)S(1)}, f32[2,22,3,128]{3,2,1,0:T(4,128)S(1)}, u32[]{:S(2)}, u32[]{:S(2)}) collective-permute-start(f32[2,22,3,128]{3,2,1,0:T(4,128)S(1)} %get-tuple-element.54), channel_id=1, source_target_pairs={{0,1},{1,0},{2,3},{3,2},{4,5},{5,4},{6,7},{7,6},{8,9},{9,8},{10,11... | collective-permute-start | bytes 202760 | tf_op jit(solution)/shard_map/ppermute | solution.py:86
  58.7 9.4 %collective-permute-start.16 = (f32[2,22,3,128]{3,2,1,0:T(4,128)S(1)}, f32[2,22,3,128]{3,2,1,0:T(4,128)S(1)}, u32[]{:S(2)}, u32[]{:S(2)}) collective-permute-start(f32[2,22,3,128]{3,2,1,0:T(4,128)S(1)} %get-tuple-element.55), channel_id=1, source_target_pairs={{0,7},{1,2},{2,1},{3,4},{4,3},{5,6},{6,5},{7,0},{8,15},{9,10},{10,... | collective-permute-start | bytes 202760 | tf_op jit(solution)/shard_map/ppermute | solution.py:86
  63.6 9.0 %collective-permute-start.22 = (f32[1,40,128]{2,1,0:T(8,128)S(1)}, f32[1,40,128]{2,1,0:T(8,128)S(1)}, u32[]{:S(2)}, u32[]{:S(2)}) collective-permute-start(f32[1,40,128]{2,1,0:T(8,128)S(1)} %get-tuple-element.70), channel_id=1, source_target_pairs={{0,6},{1,7},{2,4},{3,5},{4,2},{5,3},{6,0},{7,1},{8,14},{9,15},{10,... | collective-permute-start | bytes 61448 | tf_op jit(solution)/shard_map/ppermute | solution.py:443
  67.2 5.4 %collective-permute-start.21 = (f32[1,40,128]{2,1,0:T(8,128)S(1)}, f32[1,40,128]{2,1,0:T(8,128)S(1)}, u32[]{:S(2)}, u32[]{:S(2)}) collective-permute-start(f32[1,40,128]{2,1,0:T(8,128)S(1)} %get-tuple-element.71), channel_id=1, source_target_pairs={{0,4},{1,5},{2,6},{3,7},{4,0},{5,1},{6,2},{7,3},{8,12},{9,13},{10,... | collective-permute-start | bytes 61448 | tf_op jit(solution)/shard_map/ppermute | solution.py:443
  67.2 5.4 %collective-permute-start.20 = (f32[1,40,128]{2,1,0:T(8,128)S(1)}, f32[1,40,128]{2,1,0:T(8,128)S(1)}, u32[]{:S(2)}, u32[]{:S(2)}) collective-permute-start(f32[1,40,128]{2,1,0:T(8,128)S(1)} %get-tuple-element.72), channel_id=1, source_target_pairs={{0,2},{1,3},{2,0},{3,1},{4,6},{5,7},{6,4},{7,5},{8,10},{9,11},{10,... | collective-permute-start | bytes 61448 | tf_op jit(solution)/shard_map/ppermute | solution.py:443
  (2 other events, 12.4 us)
